TPU v7x, 32 devices: a whole 2x2x4 slice. The times are simulated.
32 devices in a mesh: section: 2 (over core), mp: 4 (over z), dp: 4 (over y, x).
Axes of the slice: x: 2, y: 2, z: 4, core: 2. Of those that a mesh axis runs over, the one named last changes fastest.
Arguments:
- char_ids: int32 [64, 20, 50], P('dp'), may hold values from 0 to 261
- row_lengths: int32 [64], P('dp'), may hold values from 1 to 20, as said below
- top_grad: bfloat16 [64, 20, 2, 512], P('dp'), may hold values from -6 to 6
- char_table: bfloat16 [262, 16], replicated, may hold values from -6 to 6
- conv_weight: bfloat16 [7, 16, 2048], P(None, None, 'mp'), may hold values from -0.5 to 0.5
- conv_bias: bfloat16 [2048], P('mp'), may hold values from -3 to 3
- highway_weight: bfloat16 [2, 2048, 2, 2048], P(None, None, None, 'mp'), may hold values from -0.125 to 0.125
- highway_bias: bfloat16 [2, 2, 2048], P(None, None, 'mp'), may hold values from -3 to 3
- proj_weight: bfloat16 [2048, 512], replicated, may hold values from -0.125 to 0.125
- proj_bias: bfloat16 [512], replicated, may hold values from -3 to 3
- lstm_input: bfloat16 [2, 2, 512, 4, 4096], P('section', None, None, None, 'mp'), may hold values from -0.25 to 0.25
- lstm_state: bfloat16 [2, 2, 512, 4, 4096], P('section', None, None, None, 'mp'), may hold values from -0.25 to 0.25
- lstm_bias: bfloat16 [2, 2, 4, 4096], P('section', None, None, 'mp'), may hold values from -3 to 3
- lstm_proj: bfloat16 [2, 2, 4096, 512], P('section', None, 'mp'), may hold values from -0.1875 to 0.1875
Outputs:
- char_table_grad: float32 [262, 16], replicated
- conv_weight_grad: float32 [7, 16, 2048], P(None, None, 'mp')
- conv_bias_grad: float32 [2048], P('mp')
- highway_weight_grad: float32 [2, 2048, 2, 2048], P(None, None, None, 'mp')
- highway_bias_grad: float32 [2, 2, 2048], P(None, None, 'mp')
- proj_weight_grad: float32 [2048, 512], replicated
- proj_bias_grad: float32 [512], replicated
- lstm_input_grad: float32 [2, 2, 512, 4, 4096], P('section', None, None, None, 'mp')
- lstm_state_grad: float32 [2, 2, 512, 4, 4096], P('section', None, None, None, 'mp')
- lstm_bias_grad: float32 [2, 2, 4, 4096], P('section', None, None, 'mp')
- lstm_proj_grad: float32 [2, 2, 4096, 512], P('section', None, 'mp')
Inputs may be any that keep to these rules, and one draw needn't show every extreme that they name: `row_lengths`: each row's live tokens; positions from it on are padding; some row has exactly 20.
All inputs are finite; a program needn't handle non-finite values.
Results may differ from a plain program's by a relative error of at most 0.019.
Values may be sent and summed in bfloat16 or wider, within the bound.
A program may use at most 384 MiB of HBM per device.

v0:
```python
import jax
import jax.numpy as jnp
from jax import lax
from jax.sharding import PartitionSpec as P

FILT = 2048
MICRO = 2
MB_ROWS = 8


def from_behind(block, axis, distance):
    devices = range(lax.axis_size(axis))
    route = [(i - distance, i) for i in devices if i - distance in devices]
    return lax.ppermute(block, axis, route)


def soft_clip(values):
    return 3.0 * jnp.tanh(values / 3.0)


def filter_widths(offset, amount):
    period = FILT // 32
    filter_index = offset + jnp.arange(amount, dtype=jnp.int32)
    in_period = filter_index % period
    widths = jnp.ones((amount,), jnp.int32)
    for exponent in range(6):
        widths = widths + (in_period * 64 >= period * 2**exponent).astype(jnp.int32)
    return widths


def spread(values):
    return lax.all_gather(values, "mp", axis=1, tiled=True)


def spread_back(weight_here, grad_mixed):
    return lax.psum_scatter(
        lax.dot_general(
            weight_here, grad_mixed, (((1,), (1,)), ((), ())), preferred_element_type=jnp.float32
        ),
        "mp",
        scatter_dimension=0,
        tiled=True,
    ).T


def cnn_forward(char_block, cnn_weights):
    char_table, conv_weight, conv_bias, highway_weight, highway_bias, proj_weight, proj_bias = (
        cnn_weights
    )
    row_count, seq_len, per_token = char_block.shape
    tok_count = row_count * seq_len
    flat_ids = char_block.reshape(-1)
    one_hot = (
        flat_ids[:, None] == jnp.arange(char_table.shape[0], dtype=jnp.int32)[None, :]
    ).astype(jnp.bfloat16)
    embedded = jnp.dot(one_hot, char_table, preferred_element_type=jnp.float32).astype(jnp.bfloat16)
    embedded = embedded.reshape(tok_count, per_token, -1)
    padded = jnp.pad(embedded, ((0, 0), (0, 6), (0, 0)))
    taps = jnp.concatenate(
        [padded[:, offset : offset + per_token, :] for offset in range(7)], axis=2
    )
    local_filters = conv_weight.shape[2]
    widths = filter_widths(lax.axis_index("mp") * local_filters, local_filters)
    tap_keep = jnp.arange(7, dtype=jnp.int32)[:, None] < widths[None, :]
    position_keep = jnp.arange(per_token, dtype=jnp.int32)[:, None] <= (per_token - widths)[None, :]
    masked = jnp.where(tap_keep[:, None, :], conv_weight, jnp.zeros_like(conv_weight)).reshape(
        -1, local_filters
    )
    scores = jnp.dot(
        taps.reshape(tok_count * per_token, -1), masked, preferred_element_type=jnp.float32
    )
    scores = scores.reshape(tok_count, per_token, local_filters) + conv_bias.astype(jnp.float32)
    guarded = jnp.where(position_keep[None], scores, -1e30)
    top_score = jnp.max(guarded, axis=1, keepdims=True)
    exp_terms = jnp.where(position_keep[None], jnp.exp(guarded - top_score), 0.0)
    exp_total = jnp.sum(exp_terms, axis=1)
    positions = (per_token - widths + 1).astype(jnp.float32)
    pooled = top_score[:, 0, :] + jnp.log(exp_total) - jnp.log(positions)
    pool_weights = exp_terms / exp_total[:, None, :]
    current = jax.nn.softplus(pooled)
    saved_layers = []
    for depth_index in range(highway_weight.shape[0]):
        gathered = spread(current.astype(jnp.bfloat16))
        weight_here = highway_weight[depth_index].reshape(gathered.shape[1], -1)
        mixed_out = jnp.dot(gathered, weight_here, preferred_element_type=jnp.float32)
        mixed_out = mixed_out + highway_bias[depth_index].reshape(-1).astype(jnp.float32)
        transform = mixed_out[:, :local_filters]
        gate_value = jax.nn.sigmoid(mixed_out[:, local_filters:])
        saved_layers.append((gathered, current, transform, gate_value))
        current = gate_value * current + (1.0 - gate_value) * jax.nn.silu(transform)
    gathered = spread(current.astype(jnp.bfloat16))
    projected = jnp.dot(
        gathered, proj_weight, preferred_element_type=jnp.float32
    ) + proj_bias.astype(jnp.float32)
    return (
        projected,
        (
            flat_ids,
            taps,
            masked,
            tap_keep,
            pool_weights,
            jax.nn.sigmoid(pooled),
            saved_layers,
            gathered,
        ),
    )


def cnn_backward(grad_base, cnn_saved, cnn_weights):
    char_table, conv_weight, conv_bias, highway_weight, highway_bias, proj_weight, proj_bias = (
        cnn_weights
    )
    flat_ids, taps, masked, tap_keep, pool_weights, pool_slope, saved_layers, gathered = cnn_saved
    proj_weight_grad = lax.dot_general(
        gathered, grad_base, (((0,), (0,)), ((), ())), preferred_element_type=jnp.float32
    )
    proj_bias_grad = jnp.sum(grad_base.astype(jnp.float32), axis=0)
    local_filters = masked.shape[1]
    own_rows = lax.dynamic_slice_in_dim(
        proj_weight, lax.axis_index("mp") * local_filters, local_filters, 0
    )
    grad_current = lax.dot_general(
        grad_base, own_rows, (((1,), (1,)), ((), ())), preferred_element_type=jnp.float32
    )
    weight_grads = []
    bias_grads = []
    for depth_index in range(len(saved_layers) - 1, -1, -1):
        gathered_in, before, transform, gate_value = saved_layers[depth_index]
        sig_transform = jax.nn.sigmoid(transform)
        grad_transform = (
            grad_current
            * (1.0 - gate_value)
            * sig_transform
            * (1.0 + transform * (1.0 - sig_transform))
        )
        grad_gate = (
            grad_current * (before - jax.nn.silu(transform)) * gate_value * (1.0 - gate_value)
        )
        grad_mixed = jnp.concatenate([grad_transform, grad_gate], axis=1).astype(jnp.bfloat16)
        weight_here = highway_weight[depth_index].reshape(gathered_in.shape[1], -1)
        layer_weight_grad = lax.dot_general(
            gathered_in, grad_mixed, (((0,), (0,)), ((), ())), preferred_element_type=jnp.float32
        )
        weight_grads.insert(0, layer_weight_grad.reshape(highway_weight.shape[1:]))
        bias_grads.insert(
            0, jnp.sum(grad_mixed.astype(jnp.float32), axis=0).reshape(highway_bias.shape[1:])
        )
        grad_current = grad_current * gate_value + spread_back(weight_here, grad_mixed)
    grad_scores = (pool_weights * (grad_current * pool_slope)[:, None, :]).astype(jnp.bfloat16)
    grad_flat = grad_scores.reshape(-1, local_filters)
    taps_flat = taps.reshape(grad_flat.shape[0], -1)
    conv_grad = lax.dot_general(
        taps_flat, grad_flat, (((0,), (0,)), ((), ())), preferred_element_type=jnp.float32
    )
    conv_grad = jnp.where(tap_keep[:, None, :], conv_grad.reshape(conv_weight.shape), 0.0)
    conv_bias_grad = jnp.sum(grad_flat.astype(jnp.float32), axis=0)
    grad_taps = lax.dot_general(
        grad_flat, masked, (((1,), (1,)), ((), ())), preferred_element_type=jnp.float32
    )
    tok_count = taps.shape[0]
    per_token = taps.shape[1]
    emb_width = char_table.shape[1]
    grad_taps = grad_taps.reshape(tok_count, per_token, 7, emb_width)
    grad_embedded = jnp.zeros((tok_count, per_token + 6, emb_width), jnp.float32)
    for offset in range(7):
        grad_embedded = grad_embedded + jnp.pad(
            grad_taps[:, :, offset, :], ((0, 0), (offset, 6 - offset), (0, 0))
        )
    grad_embedded = grad_embedded[:, :per_token, :].reshape(-1, emb_width)
    table_grad = jax.ops.segment_sum(grad_embedded, flat_ids, num_segments=char_table.shape[0])
    return (
        table_grad,
        conv_grad,
        conv_bias_grad,
        jnp.stack(weight_grads),
        jnp.stack(bias_grads),
        proj_weight_grad,
        proj_bias_grad,
    )


def to_scan(values):
    forward_part = values[:, :, 0]
    backward_part = jnp.flip(values[:, :, 1], axis=1)
    return jnp.transpose(jnp.stack([forward_part, backward_part], axis=2), (1, 0, 2, 3))


def from_scan(values):
    reordered = jnp.transpose(values, (1, 0, 2, 3))
    return jnp.stack([reordered[:, :, 0], jnp.flip(reordered[:, :, 1], axis=1)], axis=2)


def scan_masks(lengths_here, seq_len):
    step_ids = jnp.arange(seq_len, dtype=jnp.int32)[:, None]
    ahead = step_ids < lengths_here[None, :]
    behind = seq_len - 1 - step_ids < lengths_here[None, :]
    return jnp.stack([ahead, behind], axis=2).astype(jnp.float32)[:, :, :, None]


def project(hidden, proj_here):
    partial_terms = jnp.einsum(
        "bdc,dcp->bdp", hidden, proj_here, preferred_element_type=jnp.float32
    )
    return lax.psum(partial_terms, "mp")


def gate_values(gates, row_count, cell_count):
    gate_parts = gates.reshape(row_count, 2, 4, cell_count)
    in_gate = jax.nn.sigmoid(gate_parts[:, :, 0])
    forget = jax.nn.sigmoid(gate_parts[:, :, 1])
    memory = jnp.tanh(gate_parts[:, :, 2])
    out_gate = jax.nn.sigmoid(gate_parts[:, :, 3])
    return (in_gate, forget, memory, out_gate)


def lstm_forward(inputs_scan, live_scan, layer_weights):
    input_weight, state_weight, bias_here, proj_here = layer_weights
    pre_gates = jnp.einsum(
        "sbdp,dpg->sbdg", inputs_scan, input_weight, preferred_element_type=jnp.float32
    )
    pre_gates = pre_gates + bias_here.astype(jnp.float32)
    row_count = inputs_scan.shape[1]
    cell_count = proj_here.shape[1]
    proj_width = proj_here.shape[2]

    def advance(carry, slices):
        cell_prev, state_prev = carry
        pre_now, live_now = slices
        state_low = state_prev.astype(jnp.bfloat16)
        gates = pre_now + jnp.einsum(
            "bdp,dpg->bdg", state_low, state_weight, preferred_element_type=jnp.float32
        )
        in_gate, forget, memory, out_gate = gate_values(gates, row_count, cell_count)
        cell_new = soft_clip(in_gate * memory + forget * cell_prev)
        hidden = (out_gate * jnp.tanh(cell_new)).astype(jnp.bfloat16)
        projected = project(hidden, proj_here)
        state_new = soft_clip(projected)
        cell_next = live_now * cell_new + (1.0 - live_now) * cell_prev
        state_next = live_now * state_new + (1.0 - live_now) * state_prev
        return (
            (cell_next, state_next),
            (gates, cell_prev, hidden, projected, state_low, live_now * state_new),
        )

    initial = (
        jnp.zeros((row_count, 2, cell_count), jnp.float32),
        jnp.zeros((row_count, 2, proj_width), jnp.float32),
    )
    return lax.scan(advance, initial, (pre_gates, live_scan))[1]


def lstm_backward(inputs_scan, live_scan, grad_out_scan, steps_saved, layer_weights):
    input_weight, state_weight, bias_here, proj_here = layer_weights
    gates_all, cell_prev_all, hidden_all, projected_all, state_low_all, outputs_all = steps_saved
    row_count = inputs_scan.shape[1]
    cell_count = proj_here.shape[1]
    proj_width = proj_here.shape[2]

    def retreat(carry, slices):
        grad_cell, grad_state = carry
        gates, cell_prev, projected, live_now, grad_out = slices
        in_gate, forget, memory, out_gate = gate_values(gates, row_count, cell_count)
        clip_raw = jnp.tanh((in_gate * memory + forget * cell_prev) / 3.0)
        tanh_cell = jnp.tanh(3.0 * clip_raw)
        grad_value = live_now * (grad_state + grad_out)
        clip_proj = jnp.tanh(projected / 3.0)
        grad_projected = (grad_value * (1.0 - clip_proj * clip_proj)).astype(jnp.bfloat16)
        grad_hidden = jnp.einsum(
            "bdp,dcp->bdc", grad_projected, proj_here, preferred_element_type=jnp.float32
        )
        grad_cell_new = live_now * grad_cell + grad_hidden * out_gate * (
            1.0 - tanh_cell * tanh_cell
        )
        grad_raw = grad_cell_new * (1.0 - clip_raw * clip_raw)
        grad_parts = jnp.stack(
            [
                grad_raw * memory * in_gate * (1.0 - in_gate),
                grad_raw * cell_prev * forget * (1.0 - forget),
                grad_raw * in_gate * (1.0 - memory * memory),
                grad_hidden * tanh_cell * out_gate * (1.0 - out_gate),
            ],
            axis=2,
        )
        grad_gates = grad_parts.reshape(row_count, 2, -1).astype(jnp.bfloat16)
        back_terms = jnp.einsum(
            "bdg,dpg->bdp", grad_gates, state_weight, preferred_element_type=jnp.float32
        )
        back_state = lax.psum(back_terms, "mp")
        grad_cell_prev = (1.0 - live_now) * grad_cell + grad_raw * forget
        grad_state_prev = (1.0 - live_now) * grad_state + back_state
        return ((grad_cell_prev, grad_state_prev), (grad_gates, grad_projected))

    initial = (
        jnp.zeros((row_count, 2, cell_count), jnp.float32),
        jnp.zeros((row_count, 2, proj_width), jnp.float32),
    )
    grad_gates_all, grad_projected_all = lax.scan(
        retreat,
        initial,
        (gates_all, cell_prev_all, projected_all, live_scan, grad_out_scan),
        reverse=True,
    )[1]
    input_grad = jnp.einsum(
        "sbdp,sbdg->dpg", inputs_scan, grad_gates_all, preferred_element_type=jnp.float32
    )
    state_grad = jnp.einsum(
        "sbdp,sbdg->dpg", state_low_all, grad_gates_all, preferred_element_type=jnp.float32
    )
    bias_grad = jnp.sum(grad_gates_all.astype(jnp.float32), axis=(0, 1))
    proj_grad = jnp.einsum(
        "sbdc,sbdp->dcp", hidden_all, grad_projected_all, preferred_element_type=jnp.float32
    )
    grad_inputs = jnp.einsum(
        "sbdg,dpg->sbdp", grad_gates_all, input_weight, preferred_element_type=jnp.float32
    )
    return ((input_grad, state_grad, bias_grad, proj_grad), grad_inputs)


def on_device(
    char_ids,
    row_lengths,
    top_grad,
    char_table,
    conv_weight,
    conv_bias,
    highway_weight,
    highway_bias,
    proj_weight,
    proj_bias,
    lstm_input,
    lstm_state,
    lstm_bias,
    lstm_proj,
):
    section_id = lax.axis_index("section")
    seq_len = char_ids.shape[1]
    proj_width = proj_weight.shape[1]
    half_rows = MB_ROWS // 2
    cnn_weights = (
        char_table,
        conv_weight,
        conv_bias,
        highway_weight,
        highway_bias,
        proj_weight,
        proj_bias,
    )
    layer_weights = (
        lstm_input[0].reshape(2, proj_width, -1),
        lstm_state[0].reshape(2, proj_width, -1),
        lstm_bias[0].reshape(2, -1),
        lstm_proj[0],
    )
    first_section = (section_id == 0).astype(jnp.float32)
    layer_shape = (MB_ROWS, seq_len, 2, proj_width)
    received = jnp.zeros(layer_shape, jnp.bfloat16)
    saved_ticks = []
    for tick_number in range(MICRO + 1):
        micro_id = jnp.clip(tick_number - section_id, 0, MICRO - 1)
        chars_here = lax.dynamic_slice_in_dim(char_ids, micro_id * MB_ROWS, MB_ROWS, 0)
        lengths_here = lax.dynamic_slice_in_dim(row_lengths, micro_id * MB_ROWS, MB_ROWS, 0)
        projected, unused_saved = cnn_forward(chars_here, cnn_weights)
        base_low = jnp.broadcast_to(
            projected.astype(jnp.bfloat16).reshape(MB_ROWS, seq_len, 1, proj_width), layer_shape
        )
        inputs_scan = to_scan(jnp.where(section_id == 0, base_low, received))
        live_scan = scan_masks(lengths_here, seq_len)
        steps_saved = lstm_forward(inputs_scan, live_scan, layer_weights)
        if tick_number < MICRO:
            received = from_behind(from_scan(steps_saved[5]).astype(jnp.bfloat16), "section", 1)
        saved_ticks.append((micro_id, inputs_scan, live_scan, steps_saved))
    back_received = jnp.zeros(layer_shape, jnp.bfloat16)
    layer_total = None
    cnn_total = None
    for back_step in range(MICRO + 1):
        tick_number = MICRO - back_step
        micro_id, inputs_scan, live_scan, steps_saved = saved_ticks[tick_number]
        offset_here = tick_number - section_id
        active = ((offset_here >= 0) & (offset_here < MICRO)).astype(jnp.float32)
        top_here = lax.dynamic_slice_in_dim(top_grad, micro_id * MB_ROWS, MB_ROWS, 0).astype(
            jnp.float32
        )
        grad_out = jnp.where(section_id == 1, top_here, back_received.astype(jnp.float32)) * active
        layer_grads, partial_inputs = lstm_backward(
            inputs_scan, live_scan, to_scan(grad_out), steps_saved, layer_weights
        )
        grad_inputs = from_scan(lax.psum(partial_inputs, "mp"))
        if back_step < MICRO:
            back_received = from_behind(
                (grad_inputs + grad_out).astype(jnp.bfloat16), "section", -1
            )
        grad_base = (jnp.sum(grad_inputs, axis=2) * first_section).astype(jnp.bfloat16)
        upper_rows = from_behind(grad_base[half_rows:], "section", 1)
        grad_half = jnp.where(section_id == 0, grad_base[:half_rows], upper_rows).reshape(
            -1, proj_width
        )
        first_micro = min(tick_number, MICRO - 1)
        chars_half = lax.dynamic_slice_in_dim(
            char_ids, first_micro * MB_ROWS + section_id * half_rows, half_rows, 0
        )
        unused_projected, cnn_saved = cnn_forward(chars_half, cnn_weights)
        cnn_grads = cnn_backward(grad_half, cnn_saved, cnn_weights)
        layer_total = (
            layer_grads if layer_total is None else jax.tree.map(jnp.add, layer_total, layer_grads)
        )
        cnn_total = cnn_grads if cnn_total is None else jax.tree.map(jnp.add, cnn_total, cnn_grads)
    input_grad, state_grad, bias_grad, proj_grad = lax.psum(
        (layer_total[0], layer_total[1], layer_total[2], layer_total[3]), "dp"
    )
    conv_grad, conv_bias_grad, highway_grad, highway_bias_grad, proj_weight_grad, proj_bias_grad = (
        lax.psum(
            (cnn_total[1], cnn_total[2], cnn_total[3], cnn_total[4], cnn_total[5], cnn_total[6]),
            ("section", "dp"),
        )
    )
    table_grad = lax.psum(cnn_total[0], ("section", "mp", "dp"))
    return (
        table_grad,
        conv_grad,
        conv_bias_grad,
        highway_grad,
        highway_bias_grad,
        proj_weight_grad,
        proj_bias_grad,
        input_grad.reshape(lstm_input.shape),
        state_grad.reshape(lstm_state.shape),
        bias_grad.reshape(lstm_bias.shape),
        proj_grad.reshape(lstm_proj.shape),
    )


def solution(mesh):
    return jax.shard_map(
        on_device,
        mesh=mesh,
        in_specs=(
            P("dp", None, None),
            P("dp"),
            P("dp", None, None, None),
            P(),
            P(None, None, "mp"),
            P("mp"),
            P(None, None, None, "mp"),
            P(None, None, "mp"),
            P(),
            P(),
            P("section", None, None, None, "mp"),
            P("section", None, None, None, "mp"),
            P("section", None, None, "mp"),
            P("section", None, "mp", None),
        ),
        out_specs=(
            P(),
            P(None, None, "mp"),
            P("mp"),
            P(None, None, None, "mp"),
            P(None, None, "mp"),
            P(),
            P(),
            P("section", None, None, None, "mp"),
            P("section", None, None, None, "mp"),
            P("section", None, None, "mp"),
            P("section", None, "mp", None),
        ),
        check_vma=False,
    )
```

profile of v0, /device:TPU:0, one launch (start us, length us, event | category | flops | bytes accessed | tf_op | source)
XLA Modules:
  0.0 5411.4 jit_solution(13085402164773498509)
XLA Ops:
  116.8 19.6 select_reduce_fusion.2
  152.4 19.6 all_gather.51
  294.6 495.2 %while.136 = (s32[]{:T(128)}, f32[8,2,1024]{2,0,1:T(8,128)S(1)}, f32[8,2,512]{2,0,1:T(8,128)S(1)}, f32[20,8,2,4096]{3,1,2,0:T(8,128)}, f32[20,8,2,1024]{3,1,2,0:...) while((s32[]{:T(128)}, f32[8,2,1024]{2,0,1:T(8,128)S(1)}, ...), condition=%wide.region_10.11_spmd.clone, body=%wide.region_8.10_spmd.clone.sunk | while | flops 84394016 | bytes 20893312 | solution.py:250
  301.2 18.8 psum.184
  351.8 17.5 psum.184
  401.2 17.5 psum.184
  450.7 17.5 psum.184
  500.0 17.5 psum.184
  549.4 17.5 psum.184
  598.7 17.5 psum.184
  648.1 17.5 psum.184
  697.5 17.5 psum.184
  746.9 17.5 psum.184
  1082.3 521.4 %while.137 = (s32[]{:T(128)}, f32[8,2,1024]{2,0,1:T(8,128)S(1)}, f32[8,2,512]{2,0,1:T(8,128)S(1)}, f32[20,8,2,4096]{3,1,2,0:T(8,128)}, f32[20,8,2,1024]{3,1,2,0:...) while((s32[]{:T(128)}, f32[8,2,1024]{2,0,1:T(8,128)S(1)}, ...), condition=%wide.region_13.14_spmd.clone, body=%wide.region_11.13_spmd.clone.sunk | while | flops 84394016 | bytes 20893820 | solution.py:250
  1088.9 19.6 psum.185
  1142.9 17.6 psum.185
  1194.8 17.5 psum.185
  1246.8 17.5 psum.185
  1298.7 17.5 psum.185
  1350.6 17.5 psum.185
  1402.6 17.5 psum.185
  1454.5 17.5 psum.185
  1506.4 17.5 psum.185
  1558.3 17.5 psum.185
  1622.7 505.8 %while.138 = (s32[]{:T(128)}, f32[8,2,1024]{2,0,1:T(8,128)S(1)}, f32[8,2,512]{2,0,1:T(8,128)S(1)}, f32[20,8,2,4096]{3,1,2,0:T(8,128)}, f32[20,8,2,1024]{3,1,2,0:...) while((s32[]{:T(128)}, f32[8,2,1024]{2,0,1:T(8,128)S(1)}, ...), condition=%wide.region_16.17_spmd.clone, body=%wide.region_14.16_spmd.clone.sunk | while | flops 84377632 | bytes 20826740 | solution.py:250
  1629.3 17.5 psum.186
  2131.1 619.9 %while.139 = (s32[]{:T(128)}, f32[8,2,1024]{2,0,1:T(8,128)S(1)}, f32[8,2,512]{2,0,1:T(8,128)S(1)}, bf16[20,8,2,4096]{3,1,2,0:T(8,128)(2,1)}, bf16[20,8,2,512]{3,...) while((s32[]{:T(128)}, f32[8,2,1024]{2,0,1:T(8,128)S(1)}, ...), condition=%wide.region_19.20_spmd.clone, body=%wide.region_17.19_spmd.clone.sunk | while | flops 85377040 | bytes 15680126 | solution.py:298
  2778.0 20.9 all-reduce.35.cloned.1.call-done
  2816.3 647.5 %while.140 = (s32[]{:T(128)}, f32[8,2,1024]{2,0,1:T(8,128)S(1)}, f32[8,2,512]{2,0,1:T(8,128)}, bf16[20,8,2,4096]{3,1,2,0:T(8,128)(2,1)}, bf16[20,8,2,512]{3,1,2,...) while((s32[]{:T(128)}, f32[8,2,1024]{2,0,1:T(8,128)S(1)}, ...), condition=%wide.region_26.27_spmd.clone, body=%wide.region_24.26_spmd.clone.sunk | while | flops 85377040 | bytes 15680126 | solution.py:298
  2830.5 17.6 psum.188
  2894.6 17.5 psum.188
  2959.5 17.5 psum.188
  3024.3 17.5 psum.188
  3089.1 17.5 psum.188
  3153.9 17.4 psum.188
  3496.5 25.7 all-reduce.37.cloned.1.call-done
  3535.4 620.1 %while.141 = (s32[]{:T(128)}, f32[8,2,1024]{2,0,1:T(8,128)S(1)}, f32[8,2,512]{2,0,1:T(8,128)S(1)}, bf16[20,8,2,4096]{3,1,2,0:T(8,128)(2,1)}, bf16[20,8,2,512]{3,...) while((s32[]{:T(128)}, f32[8,2,1024]{2,0,1:T(8,128)S(1)}, ...), condition=%wide.region_35.36_spmd.clone, body=%wide.region_33.35_spmd.clone.sunk | while | flops 85377040 | bytes 15680126 | solution.py:298
  4354.9 23.1 fusion.144
  4441.2 20.6 bitcast_add_fusion.3
  4461.8 21.3 reshape.1056
  4483.2 20.0 bitcast_add_fusion.5
  4503.2 20.6 reshape.1055
  4574.5 22.7 scatter_custom_fusion.1
  4597.2 22.7 scatter_custom_fusion
  4620.0 23.0 scatter_fusion
  4643.1 41.6 psum.161
  4685.4 26.6 all-reduce.26
  4711.9 652.0 %all-reduce.43.cloned.1.call-done = (f32[1,2,512,4,1024]{4,3,2,1,0:T(4,128)}, f32[1,2,512,4,1024]{4,3,2,1,0:T(4,128)}, f32[1,2,1024,512]{3,2,1,0:T(8,128)}) async-done(((f32[1,2,512,4,1024]{4,3,2,1,0:T(4,128)}, f32[1,2,512,4,1024]{4,3,2,1,0:T(4,128)}, f32[1,2,1024,512]{3,2,1,0:T(8,128)}), (f32[1,2,512,4,1024]{4,3,2,1,0:T(4,128)}, f32[1,2,512,4,1024]{4,3,2,1,0:T(4,128)}, ...) | async-done | bytes 37748752 | tf_op jit(solution)/shard_map/psum | solution.py:408
  (2475 shorter events, 3933.6 us)
Async XLA Ops:
  7.2 242.9 %copy-start = (bf16[2048,512]{1,0:T(8,128)(2,1)S(1)}, bf16[2048,512]{1,0:T(8,128)(2,1)}, u32[]{:S(2)}) copy-start(bf16[2048,512]{1,0:T(8,128)(2,1)} %param.34) | copy-start | bytes 6291460
  7.2 2791.7 %all-reduce.35.cloned.1.call-start = ((), (), s32[]{:S(2)}) async-start(), calls=%async_computation.6 | async-start | bytes 1310720 | tf_op jit(solution)/shard_map/psum | solution.py:388
  7.3 950.9 %copy-start.121 = (f32[512]{0:T(512)}, f32[512]{0:T(512)S(1)}, u32[]{:S(2)}) copy-start(f32[512]{0:T(512)S(1)} %convert_log_fusion) | copy-start | bytes 6148
  24.6 31.4 copy-start.115
  24.7 111.7 %copy-start.74 = (pred[50,512]{1,0:T(8,128)(4,1)}, pred[50,512]{1,0:T(8,128)(4,1)S(1)}, u32[]{:S(2)}) copy-start(pred[50,512]{1,0:T(8,128)(4,1)S(1)} %iota_compare_fusion.10) | copy-start | bytes 76804
  24.7 929.1 %copy-start.117 = (f32[512]{0:T(512)}, f32[512]{0:T(512)S(1)}, u32[]{:S(2)}) copy-start(f32[512]{0:T(512)S(1)} %convert_element_type.568) | copy-start | bytes 6148
  56.0 894.5 %copy-start.20 = (bf16[7,16,512]{2,1,0:T(8,128)(2,1)}, bf16[7,16,512]{2,1,0:T(8,128)(2,1)S(1)}, u32[]{:S(2)}) copy-start(bf16[7,16,512]{2,1,0:T(8,128)(2,1)S(1)} %broadcast_select_fusion.2) | copy-start | bytes 344068
  136.4 35.7 slice-start.8
  136.4 35.7 slice-start.9
  179.6 33.6 copy-start.4
  250.8 30.5 copy-start.94
  250.9 30.4 copy-start.96
  790.8 277.2 %collective-permute-start = (bf16[8,20,2,512]{3,0,1,2:T(8,128)(2,1)}, bf16[8,20,2,512]{3,0,1,2:T(8,128)(2,1)}, u32[]{:S(2)}, u32[]{:S(2)}) collective-permute-start(bf16[8,20,2,512]{3,0,1,2:T(8,128)(2,1)} %pad_maximum_fusion), channel_id=1, source_target_pairs={{0,16},{1,17},{2,18},{3,19},{4,20},{5,21},{6,22},{7,23},{8,24},{9,... | collective-permute-start | bytes 983048 | tf_op jit(solution)/shard_map/ppermute | solution.py:14
  974.1 34.6 copy-start.22
  989.1 75.1 %copy-start.38 = (bf16[80,2048]{1,0:T(8,128)(2,1)}, bf16[80,2048]{1,0:T(8,128)(2,1)S(1)}, u32[]{:S(2)}) copy-start(bf16[80,2048]{1,0:T(8,128)(2,1)S(1)} %all_gather.60) | copy-start | bytes 983044
  1022.8 582.7 %copy-start.18 = (bf16[80,2048]{1,0:T(8,128)(2,1)}, bf16[80,2048]{1,0:T(8,128)(2,1)S(1)}, u32[]{:S(2)}) copy-start(bf16[80,2048]{1,0:T(8,128)(2,1)S(1)} %all_gather.58) | copy-start | bytes 983044
  1603.8 5.5 collective-permute-start.1
  2759.1 763.1 %all-reduce.37.cloned.1.call-start = ((), (), s32[]{:S(2)}) async-start(), calls=%async_computation.9 | async-start | bytes 1310720 | tf_op jit(solution)/shard_map/psum | solution.py:388
  2769.4 31.6 copy-start.41
  2769.4 36.9 copy-start.108
  2801.2 10.4 collective-permute-start.3
  2802.6 7.7 collective-permute-start.2
  3482.2 722.2 %all-reduce.39.cloned.1.call-start = ((), (), s32[]{:S(2)}) async-start(), calls=%async_computation.12 | async-start | bytes 1310720 | tf_op jit(solution)/shard_map/psum | solution.py:388
  3496.5 34.3 copy-start.60
  3524.4 3.8 collective-permute-start.4
  3526.9 3.9 collective-permute-start.5
  4163.6 115.3 %reduce-scatter.7.cloned.1.call-start = ((), (), s32[]{:S(2)}) async-start(), calls=%async_computation.7 | async-start | bytes 819200 | tf_op jit(solution)/shard_map/reduce_scatter | solution.py:36
  4164.7 26.7 copy-start.84
  4164.7 26.7 copy-start.86
  4164.7 31.3 copy-start.80
  4164.7 31.3 copy-start.82
  4185.4 93.6 %reduce-scatter.11.cloned.1.call-start = ((), (), s32[]{:S(2)}) async-start(), calls=%async_computation.10 | async-start | bytes 819200 | tf_op jit(solution)/shard_map/reduce_scatter | solution.py:36
  4200.7 129.4 %reduce-scatter.15.cloned.1.call-start = ((), (), s32[]{:S(2)}) async-start(), calls=%async_computation.13 | async-start | bytes 819200 | tf_op jit(solution)/shard_map/reduce_scatter | solution.py:36
  4206.5 30.9 collective-permute-start.6
  4243.6 134.4 %reduce-scatter.9.cloned.1.call-start = ((), (), s32[]{:S(2)}) async-start(), calls=%async_computation.8 | async-start | bytes 819200 | tf_op jit(solution)/shard_map/reduce_scatter | solution.py:36
  4248.4 30.6 copy-start.25
  4248.4 30.6 copy-start.110
  4248.4 32.5 copy-start.55
  4285.5 92.5 %reduce-scatter.13.cloned.1.call-start = ((), (), s32[]{:S(2)}) async-start(), calls=%async_computation.11 | async-start | bytes 819200 | tf_op jit(solution)/shard_map/reduce_scatter | solution.py:36
  4298.9 79.2 %reduce-scatter.17.cloned.1.call-start = ((), (), s32[]{:S(2)}) async-start(), calls=%async_computation.14 | async-start | bytes 819200 | tf_op jit(solution)/shard_map/reduce_scatter | solution.py:36
  4354.4 25.2 copy-start.76
  4354.4 25.2 copy-start.118
  4354.4 357.5 %all-reduce.41.cloned.1.call-start = ((), (), s32[]{:S(2)}) async-start(), calls=%async_computation.15 | async-start | bytes 42401792 | tf_op jit(solution)/shard_map/psum | solution.py:412
  4440.3 923.6 %all-reduce.43.cloned.1.call-start = ((), (), s32[]{:S(2)}) async-start(), calls=%async_computation.16 | async-start | bytes 75497472 | tf_op jit(solution)/shard_map/psum | solution.py:408
  4571.8 48.2 copy-start.120
  4620.0 65.4 %copy-start.129 = (f32[512]{0:T(512)S(1)}, f32[512]{0:T(512)}, u32[]{:S(2)}) copy-start(f32[512]{0:T(512)} %get-tuple-element.1985) | copy-start | bytes 6148
  4620.0 65.3 %copy-start.130 = (f32[512]{0:T(512)S(1)}, f32[512]{0:T(512)}, u32[]{:S(2)}) copy-start(f32[512]{0:T(512)} %get-tuple-element.2139) | copy-start | bytes 6148
  4620.0 65.3 %copy-start.131 = (f32[512]{0:T(512)S(1)}, f32[512]{0:T(512)}, u32[]{:S(2)}) copy-start(f32[512]{0:T(512)} %get-tuple-element.2141) | copy-start | bytes 6148
  (174 other events, 1663.1 us)
Sparse Core Ops, SparseCore 0:
  2759.2 39.6 all-reduce.34
  3482.3 39.7 all-reduce.36
  4163.7 40.6 all-reduce.38
  4206.5 21.6 reduce-scatter.6
  4230.4 21.1 reduce-scatter.10
  4253.7 24.4 reduce-scatter.14
  4285.6 20.6 reduce-scatter.8
  4308.7 21.0 reduce-scatter.12
  4354.5 20.6 reduce-scatter.16
  4440.4 268.4 all-reduce.40
  4714.0 649.8 all-reduce.42
where the time goes:
time: 5440 us; the launch traced here: 5410 us
  blocking collectives  2320 us (43%)
  matrix products  1120 us (21%)
  waiting for transfers between devices  704 us (13%)
  local copies, waits for them, and re-layouts  647 us (12%)
  other arithmetic  582 us (11%)
    psum x60, blocking collectives, project(): return lax.psum(partial_terms, 'mp')  1000 us
    psum x60, blocking collectives, retreat(): back_state = lax.psum(back_terms, 'mp')  999 us
    psum x1, waiting for transfers between devices, on_device(): lax.psum((layer_total[0], layer_total[1], layer_total[2], layer_total[3])...  652 us
    dot_general x60, matrix products, retreat(): jnp.einsum('bdg,dpg->bdp', grad_gates, state_weight, preferred_element_ty...  338 us
    dot_general x60, matrix products, advance(): jnp.einsum('bdp,dpg->bdg', state_low, state_weight, preferred_element_typ...  327 us
    all_gather x15, blocking collectives, spread(): return lax.all_gather(values, 'mp', axis=1, tiled=True)  236 us
    dynamic_update_slice x280, other arithmetic, lstm_forward(): return lax.scan(advance, initial, (pre_gates, live_scan))[1]  195 us
    dot_general x60, matrix products, retreat(): jnp.einsum('bdp,dcp->bdc', grad_projected, proj_here, preferred_element_t...  134 us
  transfers between devices with their start and end apart: 18, of which 5 were waited for; matrix products, arithmetic and copies ran while one was open for 10% of the time, Pallas kernels for 0%

commit v1 on v0

v1 whole, which is shorter than its diff:
```python
import jax
import jax.numpy as jnp
from jax import lax
from jax.experimental import pallas as pl
from jax.experimental.pallas import tpu as pltpu
from jax.sharding import PartitionSpec as P

F32 = jnp.float32
BF16 = jnp.bfloat16
PERIODS = 32
TAPS = 7
VMEM_LIMIT = 62 * 1024 * 1024


def dot(left, right, left_dim, right_dim):
    return lax.dot_general(
        left, right, (((left_dim,), (right_dim,)), ((), ())), preferred_element_type=F32
    )


def soft_clip(values):
    return 3.0 * jnp.tanh(values / 3.0)


def filter_widths(offset, amount, total):
    period = total // PERIODS
    in_period = (offset + jnp.arange(amount, dtype=jnp.int32)) % period
    widths = jnp.ones((amount,), jnp.int32)
    for exponent in range(6):
        widths = widths + (in_period * 64 >= period * 2**exponent).astype(jnp.int32)
    return widths


def shift_up(values, amount):
    return jnp.pad(values[:, amount:, :], ((0, 0), (0, amount), (0, 0)))


def shift_down(values, amount):
    count = values.shape[1]
    return jnp.pad(values[:, : count - amount, :], ((0, 0), (amount, 0), (0, 0)))


def spread(values):
    return lax.all_gather(values, "mp", axis=1, tiled=True)


def cnn_forward(chars, weights):
    table, conv_weight, conv_bias, high_weight, high_bias, proj_weight, proj_bias = weights
    tokens, per_token = chars.shape
    emb = table.shape[1]
    local = conv_weight.shape[2]
    one_hot = (chars[:, :, None] == jnp.arange(table.shape[0], dtype=jnp.int32)).astype(BF16)
    one_hot = one_hot.reshape(tokens * per_token, -1)
    repeated = jnp.dot(one_hot, jnp.tile(table, (1, TAPS)), preferred_element_type=F32)
    repeated = repeated.astype(BF16).reshape(tokens, per_token, TAPS * emb)
    group = (jnp.arange(TAPS * emb, dtype=jnp.int32) // emb)[None, None, :]
    taps = repeated
    for offset in range(1, TAPS):
        taps = jnp.where(group == offset, shift_up(repeated, offset), taps)
    widths = filter_widths(lax.axis_index("mp") * local, local, local * lax.axis_size("mp"))
    tap_keep = jnp.arange(TAPS, dtype=jnp.int32)[:, None] < widths[None, :]
    position_keep = jnp.arange(per_token, dtype=jnp.int32)[:, None] <= (per_token - widths)[None, :]
    masked = jnp.where(tap_keep[:, None, :], conv_weight, jnp.zeros_like(conv_weight))
    masked = masked.reshape(-1, local)
    scores = jnp.dot(taps.reshape(tokens * per_token, -1), masked, preferred_element_type=F32)
    scores = scores.reshape(tokens, per_token, local) + conv_bias.astype(F32)
    guarded = jnp.where(position_keep[None], scores, -1e30)
    top_score = jnp.max(guarded, axis=1, keepdims=True)
    exp_terms = jnp.where(position_keep[None], jnp.exp(guarded - top_score), 0.0)
    exp_total = jnp.sum(exp_terms, axis=1)
    positions = (per_token - widths + 1).astype(F32)
    pooled = top_score[:, 0, :] + jnp.log(exp_total) - jnp.log(positions)
    current = jax.nn.softplus(pooled)
    layers = []
    for depth in range(high_weight.shape[0]):
        gathered = spread(current.astype(BF16))
        mixed = jnp.dot(
            gathered, high_weight[depth].reshape(gathered.shape[1], -1), preferred_element_type=F32
        )
        mixed = mixed + high_bias[depth].reshape(-1).astype(F32)
        transform = mixed[:, :local]
        gate = jax.nn.sigmoid(mixed[:, local:])
        layers.append((gathered, current, transform, gate))
        current = gate * current + (1.0 - gate) * jax.nn.silu(transform)
    gathered = spread(current.astype(BF16))
    base = jnp.dot(gathered, proj_weight, preferred_element_type=F32) + proj_bias.astype(F32)
    saved = (one_hot, taps, masked, tap_keep, exp_terms, exp_total, pooled, layers, gathered)
    return base.astype(BF16), saved


def cnn_backward(grad_base, saved, weights):
    table, conv_weight, conv_bias, high_weight, high_bias, proj_weight, proj_bias = weights
    one_hot, taps, masked, tap_keep, exp_terms, exp_total, pooled, layers, gathered = saved
    tokens, per_token, width = taps.shape
    local = masked.shape[1]
    own_rows = lax.dynamic_slice_in_dim(proj_weight, lax.axis_index("mp") * local, local, 0)
    grad_current = dot(grad_base, own_rows, 1, 1)
    mixed_grads = []
    for depth in range(len(layers) - 1, -1, -1):
        gathered_in, before, transform, gate = layers[depth]
        slope = jax.nn.sigmoid(transform)
        grad_transform = grad_current * (1.0 - gate) * slope * (1.0 + transform * (1.0 - slope))
        grad_gate = grad_current * (before - transform * slope) * gate * (1.0 - gate)
        grad_mixed = jnp.concatenate([grad_transform, grad_gate], axis=1).astype(BF16)
        mixed_grads.insert(0, grad_mixed)
        weight_here = high_weight[depth].reshape(gathered_in.shape[1], -1)
        back = lax.psum_scatter(
            dot(weight_here, grad_mixed, 1, 1), "mp", scatter_dimension=0, tiled=True
        )
        grad_current = grad_current * gate + back.T
    scale = grad_current * jax.nn.sigmoid(pooled) / exp_total
    grad_scores = (exp_terms * scale[:, None, :]).astype(BF16)
    grad_flat = grad_scores.reshape(tokens * per_token, local)
    conv_grad = dot(taps.reshape(tokens * per_token, width), grad_flat, 0, 0)
    conv_grad = jnp.where(tap_keep[:, None, :], conv_grad.reshape(conv_weight.shape), 0.0)
    conv_bias_grad = jnp.sum(grad_flat.astype(F32), axis=0)
    grad_taps = dot(grad_flat, masked, 1, 1).reshape(tokens, per_token, width)
    emb = width // TAPS
    group = (jnp.arange(width, dtype=jnp.int32) // emb)[None, None, :]
    moved = grad_taps
    for offset in range(1, TAPS):
        moved = jnp.where(group == offset, shift_down(grad_taps, offset), moved)
    moved = moved.astype(BF16).reshape(tokens * per_token, width)
    table_grad = dot(one_hot, moved, 0, 0).reshape(-1, TAPS, emb).sum(axis=1)
    return table_grad, conv_grad, conv_bias_grad, mixed_grads


MESH = pl.DeviceIdType.MESH
VMEM_SPEC = pl.BlockSpec(memory_space=pltpu.VMEM)
ANY_SPEC = pl.BlockSpec(memory_space=pl.ANY)


def recurrence_kernel(
    base_ref,
    live_ref,
    top_ref,
    w_in,
    w_state,
    bias_ref,
    proj_ref,
    w_in_t,
    w_state_t,
    proj_t,
    x_out,
    state_out,
    hidden_out,
    gates_out,
    projected_out,
    input_out,
    acts,
    cells,
    clips,
    pre,
    grad_cell,
    parts,
    back_parts,
    above,
    gate_buf,
    base_sem,
    send_sem,
    recv_sem,
    back_send,
    back_recv,
    x_send,
    x_recv,
    above_send,
    above_recv,
    gate_sem,
):
    count = lax.axis_size("mp")
    me = lax.axis_index("mp")
    section = lax.axis_index("section")
    steps = x_out.shape[1]
    cell_count = proj_ref.shape[1]
    chunk = min(256, cell_count)
    peers = [lax.rem(me + j, count) for j in range(1, count)]

    barrier = pltpu.get_barrier_semaphore()
    for peer in peers:
        pl.semaphore_signal(barrier, inc=1, device_id={"mp": peer}, device_id_type=MESH)
    pl.semaphore_signal(barrier, inc=1, device_id={"section": 1 - section}, device_id_type=MESH)
    pl.semaphore_wait(barrier, count)

    def wide(values, width):
        return jnp.concatenate([values] * (width // values.shape[1]), axis=1)

    def copy_part(buffer, send, recv, d, parity, source, j, target):
        return pltpu.make_async_remote_copy(
            src_ref=buffer.at[d, parity, source],
            dst_ref=buffer.at[d, parity, source],
            send_sem=send.at[d, parity, j],
            recv_sem=recv.at[d, parity, source],
            device_id={"mp": target},
            device_id_type=MESH,
        )

    def exchange_start(buffer, send, recv, d, parity, value):
        buffer[d, parity, me] = value.astype(BF16)
        for j, peer in enumerate(peers):
            copy_part(buffer, send, recv, d, parity, me, j, peer).start()

    def exchange_wait(buffer, send, recv, d, parity):
        for j, peer in enumerate(peers):
            copy_part(buffer, send, recv, d, parity, peer, j, peer).wait_recv()
        total = buffer[d, parity, 0].astype(F32)
        for source in range(1, count):
            total = total + buffer[d, parity, source].astype(F32)
        for j, peer in enumerate(peers):
            copy_part(buffer, send, recv, d, parity, me, j, peer).wait_send()
        return total

    def pass_up(d, k):
        return pltpu.make_async_remote_copy(
            src_ref=state_out.at[d, k + 1],
            dst_ref=x_out.at[d, k],
            send_sem=x_send.at[d],
            recv_sem=x_recv.at[d, k],
            device_id={"section": 1 - section},
            device_id_type=MESH,
        )

    def pass_down(d, k):
        return pltpu.make_async_remote_copy(
            src_ref=above.at[d, k],
            dst_ref=above.at[d, k],
            send_sem=above_send.at[d],
            recv_sem=above_recv.at[d, k],
            device_id={"section": 1 - section},
            device_id_type=MESH,
        )

    def gates_copy(d, k, parity):
        return pltpu.make_async_copy(
            gate_buf.at[d, parity], gates_out.at[d, k], gate_sem.at[d, parity]
        )

    @pl.when(section == 0)
    def _():
        copy = pltpu.make_async_copy(base_ref, x_out, base_sem)
        copy.start()
        copy.wait()

    for d in range(2):
        state_out[d, 0] = jnp.zeros(state_out.shape[2:], BF16)
        cells[d, 0] = jnp.zeros(cells.shape[2:], F32)
        grad_cell[d] = jnp.zeros(grad_cell.shape[1:], F32)

    def input_part(d, k):
        @pl.when(section == 1)
        def _():
            pass_up(d, k).wait_recv()

        x = x_out[d, k]
        for start in range(0, 4 * cell_count, 2 * chunk):
            cols = slice(start, start + 2 * chunk)
            pre[d, :, cols] = bias_ref[d, :, cols] + jnp.dot(
                x, w_in[d, :, cols], preferred_element_type=F32
            )

    def forward_cells(d, k):
        state = state_out[d, k]
        live = live_ref[d, k]
        for start in range(0, cell_count, chunk):
            raw = []
            for block in range(4):
                cols = slice(block * cell_count + start, block * cell_count + start + chunk)
                raw.append(
                    pre[d, :, cols]
                    + jnp.dot(state, w_state[d, :, cols], preferred_element_type=F32)
                )
            own = slice(start, start + chunk)
            in_gate = jax.nn.sigmoid(raw[0])
            forget = jax.nn.sigmoid(raw[1])
            memory = jnp.tanh(raw[2])
            out_gate = jax.nn.sigmoid(raw[3])
            for block, value in enumerate((in_gate, forget, memory, out_gate)):
                acts[d, k, block, :, own] = value
            cell_new = soft_clip(in_gate * memory + forget * cells[d, k, :, own])
            cells[d, k + 1, :, own] = wide(live, chunk) * cell_new
            hidden_out[d, k, :, own] = (out_gate * jnp.tanh(cell_new)).astype(BF16)
        part = jnp.dot(hidden_out[d, k], proj_ref[d], preferred_element_type=F32)
        exchange_start(parts, send_sem, recv_sem, d, lax.rem(k, 2), part)

    def forward_state(d, k):
        total = exchange_wait(parts, send_sem, recv_sem, d, lax.rem(k, 2))
        clip = jnp.tanh(total / 3.0)
        clips[d, k] = clip
        live = wide(live_ref[d, k], clip.shape[1])
        state_out[d, k + 1] = (live * 3.0 * clip).astype(BF16)

        @pl.when(section == 0)
        def _():
            @pl.when(k > 0)
            def _():
                pass_up(d, k - 1).wait_send()

            pass_up(d, k).start()

    for d in range(2):
        input_part(d, 0)
    for d in range(2):
        forward_cells(d, 0)
    for d in range(2):
        input_part(d, 1)

    @pl.loop(1, steps)
    def _(k):
        for d in range(2):
            forward_state(d, k - 1)
            forward_cells(d, k)

        @pl.when(k + 1 < steps)
        def _():
            for d in range(2):
                input_part(d, k + 1)

    for d in range(2):
        forward_state(d, steps - 1)

    @pl.when(section == 0)
    def _():
        for d in range(2):
            pass_up(d, steps - 1).wait_send()

    def back_wait(d, parity):
        return exchange_wait(back_parts, back_send, back_recv, d, parity)

    def back_start(d, parity, value):
        exchange_start(back_parts, back_send, back_recv, d, parity, value)

    def backward_cells(d, k, total):
        parity = lax.rem(k, 2)
        live = live_ref[d, k]
        clip = clips[d, k]
        grad_out = wide(live, clip.shape[1]) * (total + top_ref[d, k].astype(F32))
        grad_projected = (grad_out * (1.0 - clip * clip)).astype(BF16)
        projected_out[d, k] = grad_projected

        @pl.when(k < steps - 2)
        def _():
            gates_copy(d, k + 2, parity).wait()

        for start in range(0, cell_count, chunk):
            own = slice(start, start + chunk)
            grad_hidden = jnp.dot(grad_projected, proj_t[d, :, own], preferred_element_type=F32)
            in_gate, forget, memory, out_gate = [acts[d, k, block, :, own] for block in range(4)]
            cell = cells[d, k, :, own]
            clip_raw = jnp.tanh((in_gate * memory + forget * cell) / 3.0)
            tanh_cell = jnp.tanh(3.0 * clip_raw)
            grad_new = wide(live, chunk) * grad_cell[d, :, own] + grad_hidden * out_gate * (
                1.0 - tanh_cell * tanh_cell
            )
            grad_raw = grad_new * (1.0 - clip_raw * clip_raw)
            grad_cell[d, :, own] = grad_raw * forget
            grads = (
                grad_raw * memory * in_gate * (1.0 - in_gate),
                grad_raw * cell * forget * (1.0 - forget),
                grad_raw * in_gate * (1.0 - memory * memory),
                grad_hidden * tanh_cell * out_gate * (1.0 - out_gate),
            )
            for block, value in enumerate(grads):
                cols = slice(block * cell_count + start, block * cell_count + start + chunk)
                gate_buf[d, parity, :, cols] = value.astype(BF16)
        gates_copy(d, k, parity).start()

    def backward_state(d, k):
        @pl.when(k > 0)
        def _():
            parity = lax.rem(k, 2)
            back = jnp.dot(gate_buf[d, parity], w_state_t[d], preferred_element_type=F32)
            pre[d, :, : back.shape[1]] = back

            @pl.when(section == 0)
            def _():
                pass_down(d, k - 1).wait_recv()
                pre[d, :, : back.shape[1]] = back + above[d, k - 1]

            back_start(d, lax.rem(k - 1, 2), pre[d, :, : back.shape[1]])

    def backward_input(d, k):
        parity = lax.rem(k, 2)
        part = jnp.dot(gate_buf[d, parity], w_in_t[d], preferred_element_type=F32)

        @pl.when(section == 1)
        def _():
            above[d, k] = part

            @pl.when(k < steps - 1)
            def _():
                pass_down(d, k + 1).wait_send()

            pass_down(d, k).start()

        @pl.when(section == 0)
        def _():
            input_out[d, k] = part

    last = steps - 1

    @pl.when(section == 0)
    def _():
        for d in range(2):
            pass_down(d, last).wait_recv()
            back_start(d, lax.rem(last, 2), above[d, last])

    for d in range(2):

        @pl.when(section == 0)
        def _():
            pre[d, :, : clips.shape[3]] = back_wait(d, lax.rem(last, 2))

        @pl.when(section == 1)
        def _():
            pre[d, :, : clips.shape[3]] = jnp.zeros(clips.shape[2:], F32)

        backward_cells(d, last, pre[d, :, : clips.shape[3]])
        backward_state(d, last)
    for d in range(2):
        backward_input(d, last)

    @pl.loop(1, steps)
    def _(tick):
        k = last - tick
        for d in range(2):
            backward_cells(d, k, back_wait(d, lax.rem(k, 2)))
            backward_state(d, k)
        for d in range(2):
            backward_input(d, k)

    for d in range(2):
        for k in range(min(2, steps)):
            gates_copy(d, k, k % 2).wait()

    @pl.when(section == 1)
    def _():
        for d in range(2):
            pass_down(d, 0).wait_send()


def recurrence(base_seq, live_seq, top_seq, layer_weights):
    w_in, w_state, bias, proj = layer_weights
    _, steps, rows, width = base_seq.shape
    cell_count = proj.shape[1]
    count = lax.axis_size("mp")
    weights = (
        w_in,
        w_state,
        bias.astype(F32)[:, None, :],
        proj,
        jnp.swapaxes(w_in, 1, 2),
        jnp.swapaxes(w_state, 1, 2),
        jnp.swapaxes(proj, 1, 2),
    )
    dma = pltpu.SemaphoreType.DMA
    return pl.pallas_call(
        recurrence_kernel,
        out_shape=(
            jax.ShapeDtypeStruct((2, steps, rows, width), BF16),
            jax.ShapeDtypeStruct((2, steps + 1, rows, width), BF16),
            jax.ShapeDtypeStruct((2, steps, rows, cell_count), BF16),
            jax.ShapeDtypeStruct((2, steps, rows, 4 * cell_count), BF16),
            jax.ShapeDtypeStruct((2, steps, rows, width), BF16),
            jax.ShapeDtypeStruct((2, steps, rows, width), F32),
        ),
        in_specs=[ANY_SPEC] + [VMEM_SPEC] * 9,
        out_specs=(VMEM_SPEC, VMEM_SPEC, VMEM_SPEC, ANY_SPEC, VMEM_SPEC, VMEM_SPEC),
        scratch_shapes=[
            pltpu.VMEM((2, steps, 4, rows, cell_count), F32),
            pltpu.VMEM((2, steps + 1, rows, cell_count), F32),
            pltpu.VMEM((2, steps, rows, width), F32),
            pltpu.VMEM((2, rows, 4 * cell_count), F32),
            pltpu.VMEM((2, rows, cell_count), F32),
            pltpu.VMEM((2, 2, count, rows, width), BF16),
            pltpu.VMEM((2, 2, count, rows, width), BF16),
            pltpu.VMEM((2, steps, rows, width), F32),
            pltpu.VMEM((2, 2, rows, 4 * cell_count), BF16),
            dma,
            dma((2, 2, count - 1)),
            dma((2, 2, count)),
            dma((2, 2, count - 1)),
            dma((2, 2, count)),
            dma((2,)),
            dma((2, steps)),
            dma((2,)),
            dma((2, steps)),
            dma((2, 2)),
        ],
        compiler_params=pltpu.CompilerParams(
            collective_id=0, has_side_effects=True, vmem_limit_bytes=VMEM_LIMIT
        ),
        name="recurrence",
    )(base_seq, live_seq, top_seq, *weights)


def on_device(
    char_ids,
    row_lengths,
    top_grad,
    char_table,
    conv_weight,
    conv_bias,
    highway_weight,
    highway_bias,
    proj_weight,
    proj_bias,
    lstm_input,
    lstm_state,
    lstm_bias,
    lstm_proj,
):
    section = lax.axis_index("section")
    rows, steps, per_token = char_ids.shape
    proj_width = proj_weight.shape[1]
    half = rows // 2
    weights = (
        char_table,
        conv_weight,
        conv_bias,
        highway_weight,
        highway_bias,
        proj_weight,
        proj_bias,
    )
    chars = lax.dynamic_slice_in_dim(char_ids, section * half, half, 0)
    base_half, saved = cnn_forward(chars.reshape(half * steps, per_token), weights)
    base = lax.all_gather(base_half.reshape(half, steps, proj_width), "section", axis=0, tiled=True)
    by_step = jnp.transpose(base, (1, 0, 2))
    base_seq = jnp.stack([by_step, jnp.flip(by_step, axis=0)])
    top_step = jnp.transpose(top_grad, (2, 1, 0, 3))
    top_seq = jnp.stack([top_step[0], jnp.flip(top_step[1], axis=0)])
    live = (jnp.arange(steps, dtype=jnp.int32)[:, None] < row_lengths[None, :]).astype(F32)
    live_seq = jnp.stack([live, jnp.flip(live, axis=0)])[..., None]
    live_seq = jnp.broadcast_to(live_seq, (*live_seq.shape[:3], 128))
    layer_weights = (
        lstm_input[0].reshape(2, proj_width, -1),
        lstm_state[0].reshape(2, proj_width, -1),
        lstm_bias[0].reshape(2, -1),
        lstm_proj[0],
    )
    inputs_all, state_all, hidden_all, grad_gates, grad_projected, input_parts = recurrence(
        base_seq, live_seq, top_seq, layer_weights
    )

    state_all = state_all[:, :steps]
    both = input_parts[0] + jnp.flip(input_parts[1], axis=0)
    grad_base = lax.psum(both, "mp").astype(BF16)
    lower, upper = grad_base[:, :half], grad_base[:, half:]
    passed = lax.ppermute(upper, "section", [(0, 1)])
    grad_half = jnp.where(section == 0, lower, passed)
    grad_half = jnp.transpose(grad_half, (1, 0, 2)).reshape(half * steps, proj_width)
    table_grad, conv_grad, conv_bias_grad, mixed_grads = cnn_backward(grad_half, saved, weights)

    def all_rows(values):
        return lax.all_gather(values, "dp", axis=0, tiled=False)

    def weight_grad(left, right):
        return lax.dot_general(
            left, right, (((0, 2, 3), (0, 2, 3)), ((1,), (1,))), preferred_element_type=F32
        )

    all_inputs, all_states, all_hidden, all_gates, all_projected = [
        all_rows(item) for item in (inputs_all, state_all, hidden_all, grad_gates, grad_projected)
    ]
    input_grad = weight_grad(all_inputs, all_gates)
    state_grad = weight_grad(all_states, all_gates)
    proj_grad = weight_grad(all_hidden, all_projected)

    def all_tokens(values):
        return lax.all_gather(values, ("section", "dp"), axis=0, tiled=True)

    layers, gathered_last = saved[7], saved[8]
    high_grad = jnp.stack(
        [
            dot(all_tokens(layer[0]), all_tokens(grad_mixed), 0, 0)
            for layer, grad_mixed in zip(layers, mixed_grads)
        ]
    )
    proj_weight_grad = dot(all_tokens(gathered_last), all_tokens(grad_half), 0, 0)
    small = lax.psum(
        (
            conv_grad,
            conv_bias_grad,
            jnp.stack([jnp.sum(item.astype(F32), axis=0) for item in mixed_grads]),
            jnp.sum(grad_half.astype(F32), axis=0),
        ),
        ("section", "dp"),
    )
    bias_grad = lax.psum(jnp.sum(grad_gates.astype(F32), axis=(1, 2)), "dp")
    table_grad = lax.psum(table_grad, ("section", "mp", "dp"))
    return (
        table_grad,
        small[0],
        small[1],
        high_grad.reshape(highway_weight.shape),
        small[2].reshape(highway_bias.shape),
        proj_weight_grad,
        small[3],
        input_grad.reshape(lstm_input.shape),
        state_grad.reshape(lstm_state.shape),
        bias_grad.reshape(lstm_bias.shape),
        proj_grad.reshape(lstm_proj.shape),
    )


def solution(mesh):
    return jax.shard_map(
        on_device,
        mesh=mesh,
        in_specs=(
            P("dp", None, None),
            P("dp"),
            P("dp", None, None, None),
            P(),
            P(None, None, "mp"),
            P("mp"),
            P(None, None, None, "mp"),
            P(None, None, "mp"),
            P(),
            P(),
            P("section", None, None, None, "mp"),
            P("section", None, None, None, "mp"),
            P("section", None, None, "mp"),
            P("section", None, "mp", None),
        ),
        out_specs=(
            P(),
            P(None, None, "mp"),
            P("mp"),
            P(None, None, None, "mp"),
            P(None, None, "mp"),
            P(),
            P(),
            P("section", None, None, None, "mp"),
            P("section", None, None, None, "mp"),
            P("section", None, None, "mp"),
            P("section", None, "mp", None),
        ),
        check_vma=False,
    )
```

time: 5440 us -> 1170 us (0.22)
  blocking collectives: 2320 us -> 166 us
  matrix products: 1120 us -> 109 us
  other arithmetic: 582 us -> 63.2 us
  local copies, waits for them, and re-layouts: 647 us -> 226 us
  waiting for transfers between devices: 704 us -> 363 us
  Pallas kernels: 0 us -> 226 us
    psum x123 -> x4, blocking collectives: 2090 us -> 112 us  [the longest x1 38.7 us: on_device(): table_grad = lax.psum(table_grad, ('section', 'mp', 'dp'))]
    dot_general x302 -> x17, matrix products: 1120 us -> 109 us  [the longest x9 50 us: dot(): lax.dot_general(left, right, (((left_dim,), (right_dim,)), ((), ())), pre...]
    psum x5 -> x1, waiting for transfers between devices: 702 us -> 0.01 us  [on_device(): lax.psum((conv_grad, conv_bias_grad, jnp.stack([jnp.sum(item.astype(F32),...]
    all_gather x0 -> x11, waiting for transfers between devices: none -> 328 us  [the longest x5 250 us: all_rows(): return lax.all_gather(values, 'dp', axis=0, tiled=False)]
    pallas_call x0 -> x1, Pallas kernels: none -> 226 us  [recurrence(): pl.pallas_call(recurrence_kernel, out_shape=(jax.ShapeDtypeStruct((2, ste...]
    dynamic_update_slice x280 -> x0, other arithmetic: 195 us -> none  [lstm_forward(): return lax.scan(advance, initial, (pre_gates, live_scan))[1]]
    all_gather x15 -> x3, blocking collectives: 236 us -> 51.5 us  [spread(): return lax.all_gather(values, 'mp', axis=1, tiled=True)]
    another operation x129 -> x7, other arithmetic: 121 us -> 16.1 us  [the longest x1 12.8 us: on_device(): jnp.stack([dot(all_tokens(layer[0]), all_tokens(grad_mixed), 0, 0) for la...]
  transfers between devices with their start and end apart: 18 -> 15, of which waited for: 5 -> 8; matrix products, arithmetic and copies ran while one was open for 10% -> 21% of each run, Pallas kernels for 0% -> 0%
where the time goes in v1:
time: 1170 us
  waiting for transfers between devices  363 us (31%)
  local copies, waits for them, and re-layouts  226 us (19%)
  Pallas kernels  226 us (19%)
  blocking collectives  166 us (14%)
  matrix products  109 us (9%)
  other arithmetic  63.2 us (5%)
  between operations  16.8 us (1%)
    all_gather x5, waiting for transfers between devices, all_rows(): return lax.all_gather(values, 'dp', axis=0, tiled=False)  250 us
    pallas_call x1, Pallas kernels, recurrence(): pl.pallas_call(recurrence_kernel, out_shape=(jax.ShapeDtypeStruct((2, ste...  226 us
    all_gather x6, waiting for transfers between devices, all_tokens(): return lax.all_gather(values, ('section', 'dp'), axis=0, tiled=True)  77.9 us
    all_gather x3, blocking collectives, spread(): return lax.all_gather(values, 'mp', axis=1, tiled=True)  51.5 us
    dot_general x9, matrix products, dot(): lax.dot_general(left, right, (((left_dim,), (right_dim,)), ((), ())), pre...  50 us
    unnamed x109, local copies, waits for them, and re-layouts  48.1 us
    dot_general x3, matrix products, weight_grad(): lax.dot_general(left, right, (((0, 2, 3), (0, 2, 3)), ((1,), (1,))), pref...  47.7 us
    psum x1, blocking collectives, on_device(): table_grad = lax.psum(table_grad, ('section', 'mp', 'dp'))  38.7 us
  transfers between devices with their start and end apart: 15, of which 8 were waited for; matrix products, arithmetic and copies ran while one was open for 21% of the time, Pallas kernels for 0%

profile of v1, /device:TPU:0, one launch (start us, length us, event | category | flops | bytes accessed | tf_op | source)
XLA Modules:
  0.0 1171.9 jit_solution(11573862019899983837)
XLA Ops:
  12.1 15.3 %reshape.288 = bf16[160,50,112]{1,0,2:T(8,128)(2,1)} reshape(bf16[8000,112]{0,1:T(8,128)(2,1)S(1)} %convolution_convert_fusion) | data formatting | bytes 3584000 | tf_op jit(solution)/shard_map/reshape | solution.py:55
  27.4 8.3 copy.106
  37.2 8.7 fusion.33
  45.9 3.3 copy.135
  55.7 17.1 %fusion.1 = f32[160,512]{1,0:T(8,128)S(1)} fusion(f32[160,50,512]{2,0,1:T(8,128)S(1)} %get-tuple-element.45, f32[160,512]{1,0:T(8,128)S(1)} %get-tuple-element.44, f32[512]{0:T(512)S(1)} %convert_element_type.211, pred[50,512]{1,0:T(8,128)(4,1)S(1)} %iota_compare_fusion.2), kind=kLoop, calls=%fused_computation.6 | loop fusion | flops 20398080 | bytes 17067008 | tf_op jit(solution)/shard_map/reduce_sum | solution.py:70
  73.1 19.6 %all_gather.60 = bf16[160,2048]{1,0:T(8,128)(2,1)S(1)} all-gather(bf16[160,512]{1,0:T(8,128)(2,1)S(1)} %get-tuple-element.34), channel_id=1, replica_groups=mesh['section'=2,'mp'=4,'dp'=4] {'mp'}, dimensions={1}, use_global_device_ids=true | all-gather | bytes 819200 | tf_op jit(solution)/shard_map/all_gather | solution.py:44
  92.8 5.7 copy.137
  99.5 16.3 %all_gather.61 = bf16[160,2048]{1,0:T(8,128)(2,1)S(1)} all-gather(bf16[160,512]{1,0:T(8,128)(2,1)S(1)} %get-tuple-element.32), channel_id=1, replica_groups=mesh['section'=2,'mp'=4,'dp'=4] {'mp'}, dimensions={1}, use_global_device_ids=true | all-gather | bytes 819200 | tf_op jit(solution)/shard_map/all_gather | solution.py:44
  115.8 3.3 convolution_add_fusion
  120.1 15.7 %all_gather.62 = bf16[160,2048]{1,0:T(8,128)(2,1)S(1)} all-gather(bf16[160,512]{1,0:T(8,128)(2,1)S(1)} %add_convert_fusion), channel_id=1, replica_groups=mesh['section'=2,'mp'=4,'dp'=4] {'mp'}, dimensions={1}, use_global_device_ids=true | all-gather | bytes 819200 | tf_op jit(solution)/shard_map/all_gather | solution.py:44
  142.4 13.7 %copy.115 = bf16[1,2,512,4,1024]{2,4,3,1,0:T(8,128)(2,1)} copy(bf16[1,2,512,4,1024]{4,3,2,1,0:T(4,128)(2,1)} %param.24) | data formatting | bytes 16777216 | tf_op args[10]
  156.1 11.9 %copy.118.w_in = bf16[2,512,4096]{2,1,0:T(8,128)(2,1)} copy(bf16[2,512,4096]{1,2,0:T(8,128)(2,1)} %bitcast.122) | data formatting | bytes 16777216 | tf_op jit(solution)/shard_map/reshape;squeeze | solution.py:535
  168.0 13.7 %copy.116 = bf16[1,2,512,4,1024]{2,4,3,1,0:T(8,128)(2,1)} copy(bf16[1,2,512,4,1024]{4,3,2,1,0:T(4,128)(2,1)} %param.25) | data formatting | bytes 16777216 | tf_op args[11]
  181.8 11.4 copy.119.w_state
  193.9 3.9 copy.117
  200.5 225.9 %recurrence.1 = (bf16[2,20,16,512]{3,2,1,0:T(8,128)(2,1)}, bf16[2,21,16,512]{3,2,1,0:T(8,128)(2,1)}, bf16[2,20,16,1024]{3,2,1,0:T(8,128)(2,1)}, bf16[2,20,16,409...) custom-call(bf16[2,20,16,512]{3,2,1,0:T(8,128)(2,1)} %pad_maximum_fusion.1.base_ref, ...), custom_call_target="tpu_custom_call" | custom-call | tf_op jit(solution)/shard_map/recurrence/pallas_call | solution.py:455
  429.7 27.5 %all-reduce.17 = bf16[20,16,512]{2,1,0:T(8,128)(2,1)S(1)} all-reduce(f32[20,16,512]{2,1,0:T(8,128)} %bitcast_add_fusion), channel_id=1, replica_groups=mesh['section'=2,'mp'=4,'dp'=4] {'mp'}, use_global_device_ids=true, to_apply=%region_2.3 | all-reduce | flops 163840 | bytes 983040 | tf_op jit(solution)/shard_map/psum | solution.py:546
  465.3 29.8 %reduce-scatter.3.cloned.1.call-done = f32[512,160]{0,1:T(8,128)} async-done(((f32[2048,160]{0,1:T(8,128)}), f32[512,160]{0,1:T(8,128)}) %reduce-scatter.3.cloned.1.call-update) | async-done | bytes 327696 | tf_op jit(solution)/shard_map/reduce_scatter | solution.py:107
  496.6 4.8 convolution_bitcast_fusion.2
  512.8 4.2 convert_reduce_fusion.1
  517.0 2.8 reshape.266
  523.2 18.0 %psum.55 = f32[1,2,4,1024]{3,2,1,0:T(4,128)} all-reduce(f32[1,2,4,1024]{3,2,1,0:T(4,128)S(1)} %reshape.271), channel_id=1, replica_groups=mesh['section'=2,'mp'=4,'dp'=4] {'dp'}, use_global_device_ids=true, to_apply=%region_16.17 | all-reduce | flops 8192 | bytes 65536 | tf_op jit(solution)/shard_map/psum | solution.py:588
  544.7 9.3 convert_reduce_fusion
  564.4 12.1 %copy.126 = bf16[160,50,512]{2,1,0:T(8,128)(2,1)} copy(bf16[160,50,512]{2,0,1:T(8,128)(2,1)} %copy-done.4) | data formatting | bytes 16384000 | tf_op jit(solution)/shard_map/convert_element_type | solution.py:112
  576.6 5.8 select_convert_fusion
  585.3 4.0 copy.123
  589.3 11.9 %reshape.283 = bf16[8000,512,1]{1,0,2:T(8,128)(2,1)} reshape(bf16[160,50,512]{2,1,0:T(8,128)(2,1)} %copy.126) | data formatting | bytes 16384000 | tf_op jit(solution)/shard_map/reshape | solution.py:113
  601.2 3.5 fusion.8
  604.7 38.7 %psum.50 = f32[262,16]{0,1:T(8,128)} all-reduce(f32[262,16]{0,1:T(8,128)S(1)} %fusion.8), channel_id=1, replica_groups=mesh['section'=2,'mp'=4,'dp'=4] {'section','mp','dp'}, use_global_device_ids=true, to_apply=%region_6.7 | all-reduce | flops 4192 | bytes 33536 | tf_op jit(solution)/shard_map/psum | solution.py:589
  643.4 5.6 convolution_select_fusion
  649.1 28.3 %all-reduce.12 = (f32[512]{0:T(512)}, f32[2,2,512]{2,1,0:T(2,128)}, f32[512]{0:T(512)}) all-reduce(f32[512]{0:T(512)S(1)} %get-tuple-element.28, f32[2,2,512]{2,1,0:T(2,128)S(1)} %reshape.268, f32[512]{0:T(512)S(1)} %copy-done.33), channel_id=1, replica_groups=mesh['section'=2,'mp'=4,'dp'=4] {'section','dp'}, use_global_device_ids=true, to_apply=%region_9.10 | all-reduce | flops 3072 | bytes 24576 | tf_op jit(solution)/shard_map/psum | solution.py:579
  677.4 8.3 convolution_bitcast_fusion.4
  685.7 10.8 fusion.37
  696.5 13.3 %copy.128 = f32[1,2048,2,512]{3,2,1,0:T(2,128)} copy(f32[1,2048,2,512]{1,3,2,0:T(8,128)} %bitcast.135) | data formatting | bytes 16777216 | tf_op jit(solution)/shard_map/stack | solution.py:572
  709.8 2.9 all-gather.19.cloned.1.call-done
  712.7 42.9 %all-gather.17.cloned.1.call-done = bf16[1280,2048]{1,0:T(8,128)(2,1)} async-done(((bf16[160,2048]{1,0:T(8,128)(2,1)}), bf16[1280,2048]{1,0:T(8,128)(2,1)}) %all-gather.17.cloned.1.call-update) | async-done | bytes 5242896 | tf_op jit(solution)/shard_map/all_gather | solution.py:569
  755.6 10.8 fusion.36
  766.4 13.2 %copy.127 = f32[1,2048,2,512]{3,2,1,0:T(2,128)} copy(f32[1,2048,2,512]{1,3,2,0:T(8,128)} %bitcast.136) | data formatting | bytes 16777216 | tf_op jit(solution)/shard_map/stack | solution.py:572
  779.7 12.8 %pad_maximum_fusion = f32[2,2048,2,512]{3,2,1,0:T(2,128)} fusion(f32[1,2048,2,512]{3,2,1,0:T(2,128)} %copy.128, f32[1,2048,2,512]{3,2,1,0:T(2,128)} %copy.127), kind=kLoop, calls=%fused_computation | loop fusion | flops 4194304 | bytes 33554432 | tf_op jit(solution)/shard_map/stack | solution.py:572
  792.5 32.1 %all-gather.25.cloned.1.call-done = bf16[1280,2048]{1,0:T(8,128)(2,1)} async-done(((bf16[160,2048]{1,0:T(8,128)(2,1)}), bf16[1280,2048]{1,0:T(8,128)(2,1)}) %all-gather.25.cloned.1.call-update) | async-done | bytes 5242896 | tf_op jit(solution)/shard_map/all_gather | solution.py:569
  824.6 7.8 fusion.38
  832.4 33.4 %all-gather.29.cloned.1.call-done = bf16[8,20,16,512]{3,2,1,0:T(8,128)(2,1)} async-done(((bf16[2,20,16,512]{3,2,1,0:T(8,128)(2,1)}), bf16[8,20,16,512]{3,2,1,0:T(8,128)(2,1)}) %all-gather.29.cloned.1.call-update) | async-done | bytes 2621456 | tf_op jit(solution)/shard_map/all_gather | solution.py:554
  865.8 194.9 %all-gather.31.cloned.1.call-done = bf16[8,20,16,4096]{3,2,1,0:T(8,128)(2,1)} async-done(((bf16[2,20,16,4096]{3,2,1,0:T(8,128)(2,1)}), bf16[8,20,16,4096]{3,2,1,0:T(8,128)(2,1)}) %all-gather.31.cloned.1.call-update) | async-done | bytes 20971536 | tf_op jit(solution)/shard_map/all_gather | solution.py:554
  1060.7 19.6 %convolution_bitcast_fusion.1 = f32[2,512,4096]{2,1,0:T(8,128)} fusion(bf16[4,2,20,16,512]{4,3,2,1,0:T(8,128)(2,1)} %bitcast.155, bf16[4,2,20,16,4096]{4,3,2,1,0:T(8,128)(2,1)} %bitcast.151), kind=kOutput, calls=%fused_computation.10 | convolution fusion | flops 10737418240 | bytes 40370176 | tf_op jit(solution)/shard_map/dot_general | solution.py:557
  1080.3 21.6 %all-gather.33.cloned.1.call-done = bf16[8,20,16,512]{3,2,1,0:T(8,128)(2,1)} async-done(((bf16[2,20,16,512]{3,2,1,0:T(8,128)(2,1)}), bf16[8,20,16,512]{3,2,1,0:T(8,128)(2,1)}) %all-gather.33.cloned.1.call-update) | async-done | bytes 2621456 | tf_op jit(solution)/shard_map/all_gather | solution.py:554
  1101.9 19.8 %convolution_bitcast_fusion = f32[2,512,4096]{2,1,0:T(8,128)} fusion(bf16[4,2,20,16,512]{4,3,2,1,0:T(8,128)(2,1)} %bitcast.156, bf16[4,2,20,16,4096]{4,3,2,1,0:T(8,128)(2,1)} %bitcast.152), kind=kOutput, calls=%fused_computation.9 | convolution fusion | flops 10737418240 | bytes 40370176 | tf_op jit(solution)/shard_map/dot_general | solution.py:557
  1121.7 20.4 %reshape.269 = f32[1,2,512,4,1024]{4,3,2,1,0:T(4,128)} reshape(f32[2,512,4096]{2,1,0:T(8,128)} %convolution_bitcast_fusion.1) | data formatting | bytes 33554432 | tf_op jit(solution)/shard_map/reshape | solution.py:598
  1142.1 20.5 %reshape.270 = f32[1,2,512,4,1024]{4,3,2,1,0:T(4,128)} reshape(f32[2,512,4096]{2,1,0:T(8,128)} %convolution_bitcast_fusion) | data formatting | bytes 33554432 | tf_op jit(solution)/shard_map/reshape | solution.py:599
  (221 shorter events, 70.0 us)
Async XLA Ops:
  8.0 487.1 %reduce-scatter.3.cloned.1.call-start = ((), (), s32[]{:S(2)}) async-start(), calls=%async_computation.2 | async-start | bytes 1638400 | tf_op jit(solution)/shard_map/reduce_scatter | solution.py:107
  9.1 18.3 %copy-start.28 = (s32[8000]{0:T(1024)}, s32[8000]{0:T(1024)S(1)}, u32[]{:S(2)}) copy-start(s32[8000]{0:T(1024)S(1)} %eq.87) | copy-start | bytes 96004
  36.9 12.4 %copy-start.35 = (pred[112]{0:T(512)(128)(4,1)}, pred[112]{0:T(512)(128)(4,1)S(1)}, u32[]{:S(2)}) copy-start(pred[112]{0:T(512)(128)(4,1)S(1)} %get-tuple-element.53) | copy-start | bytes 340
  36.9 12.4 %copy-start.37 = (pred[112]{0:T(512)(128)(4,1)}, pred[112]{0:T(512)(128)(4,1)S(1)}, u32[]{:S(2)}) copy-start(pred[112]{0:T(512)(128)(4,1)S(1)} %get-tuple-element.54) | copy-start | bytes 340
  37.0 12.4 %copy-start.39 = (pred[112]{0:T(512)(128)(4,1)}, pred[112]{0:T(512)(128)(4,1)S(1)}, u32[]{:S(2)}) copy-start(pred[112]{0:T(512)(128)(4,1)S(1)} %get-tuple-element.49) | copy-start | bytes 340
  37.0 12.4 %copy-start.41 = (pred[112]{0:T(512)(128)(4,1)}, pred[112]{0:T(512)(128)(4,1)S(1)}, u32[]{:S(2)}) copy-start(pred[112]{0:T(512)(128)(4,1)S(1)} %get-tuple-element.50) | copy-start | bytes 340
  37.0 12.4 %copy-start.43 = (pred[112]{0:T(512)(128)(4,1)}, pred[112]{0:T(512)(128)(4,1)S(1)}, u32[]{:S(2)}) copy-start(pred[112]{0:T(512)(128)(4,1)S(1)} %get-tuple-element.51) | copy-start | bytes 340
  37.0 12.4 %copy-start.45 = (pred[112]{0:T(512)(128)(4,1)}, pred[112]{0:T(512)(128)(4,1)S(1)}, u32[]{:S(2)}) copy-start(pred[112]{0:T(512)(128)(4,1)S(1)} %get-tuple-element.52) | copy-start | bytes 340
  37.1 35.8 %copy-start.31 = (f32[512]{0:T(512)}, f32[512]{0:T(512)S(1)}, u32[]{:S(2)}) copy-start(f32[512]{0:T(512)S(1)} %convert_log_fusion) | copy-start | bytes 6148
  37.1 18.6 %copy-start.30 = (f32[512]{0:T(512)}, f32[512]{0:T(512)S(1)}, u32[]{:S(2)}) copy-start(f32[512]{0:T(512)S(1)} %convert_element_type.211) | copy-start | bytes 6148
  37.2 12.2 %copy-start.6 = (bf16[160,50,112]{2,0,1:T(8,128)(2,1)S(1)}, bf16[160,50,112]{2,0,1:T(8,128)(2,1)}, u32[]{:S(2)}) copy-start(bf16[160,50,112]{2,0,1:T(8,128)(2,1)} %copy-done.5) | copy-start | bytes 5376004
  37.2 12.2 %slice-start.5 = ((bf16[160,50,112]{2,0,1:T(8,128)(2,1)}), bf16[160,45,112]{2,0,1:T(8,128)(2,1)S(1)}, s32[]{:S(2)}) async-start(bf16[160,50,112]{2,0,1:T(8,128)(2,1)} %copy-done.5), calls=%async_computation.21 | async-start | bytes 3686400 | tf_op jit(solution)/shard_map/slice | solution.py:35
  37.2 12.2 %slice-start.6 = ((bf16[160,50,112]{2,0,1:T(8,128)(2,1)}), bf16[160,44,112]{2,0,1:T(8,128)(2,1)S(1)}, s32[]{:S(2)}) async-start(bf16[160,50,112]{2,0,1:T(8,128)(2,1)} %copy-done.5), calls=%async_computation.22 | async-start | bytes 3604480 | tf_op jit(solution)/shard_map/slice | solution.py:35
  55.7 17.2 %copy-start.3 = (f32[160,50,512]{2,0,1:T(8,128)}, f32[160,50,512]{2,0,1:T(8,128)S(1)}, u32[]{:S(2)}) copy-start(f32[160,50,512]{2,0,1:T(8,128)S(1)} %get-tuple-element.45) | copy-start | bytes 49152004
  55.7 37.0 %copy-start.34 = (bf16[2,2,512]{2,1,0:T(2,128)(2,1)S(1)}, bf16[2,2,512]{2,1,0:T(2,128)(2,1)}, u32[]{:S(2)}) copy-start(bf16[2,2,512]{2,1,0:T(2,128)(2,1)} %param.21) | copy-start | bytes 12292
  72.9 25.6 %copy-start.17 = (f32[160,512]{1,0:T(8,128)}, f32[160,512]{1,0:T(8,128)S(1)}, u32[]{:S(2)}) copy-start(f32[160,512]{1,0:T(8,128)S(1)} %fusion.1) | copy-start | bytes 983044
  99.5 36.3 %copy-start.22 = (f32[160,512]{1,0:T(8,128)}, f32[160,512]{1,0:T(8,128)S(1)}, u32[]{:S(2)}) copy-start(f32[160,512]{1,0:T(8,128)S(1)} %get-tuple-element.33) | copy-start | bytes 983044
  99.5 36.3 %copy-start.49 = (bf16[512]{0:T(512)(128)(2,1)S(1)}, bf16[512]{0:T(512)(128)(2,1)}, u32[]{:S(2)}) copy-start(bf16[512]{0:T(512)(128)(2,1)} %param.23) | copy-start | bytes 3076
  115.8 22.3 %copy-start.13 = (bf16[160,2048]{1,0:T(8,128)(2,1)}, bf16[160,2048]{1,0:T(8,128)(2,1)S(1)}, u32[]{:S(2)}) copy-start(bf16[160,2048]{1,0:T(8,128)(2,1)S(1)} %all_gather.61) | copy-start | bytes 1966084
  135.8 20.3 %copy-start.14 = (bf16[160,2048]{1,0:T(8,128)(2,1)}, bf16[160,2048]{1,0:T(8,128)(2,1)S(1)}, u32[]{:S(2)}) copy-start(bf16[160,2048]{1,0:T(8,128)(2,1)S(1)} %all_gather.62) | copy-start | bytes 1966084
  426.4 33.8 %copy-start.16 = (f32[160,1024]{1,0:T(8,128)S(1)}, f32[160,1024]{1,0:T(8,128)}, u32[]{:S(2)}) copy-start(f32[160,1024]{1,0:T(8,128)} %copy-done.15) | copy-start | bytes 1966084
  426.4 33.8 %copy-start.23 = (f32[160,512]{1,0:T(8,128)S(1)}, f32[160,512]{1,0:T(8,128)}, u32[]{:S(2)}) copy-start(f32[160,512]{1,0:T(8,128)} %copy-done.22) | copy-start | bytes 983044
  457.2 2.3 collective-permute-start
  461.9 40.7 %copy-start.19 = (bf16[160,512]{1,0:T(8,128)(2,1)}, bf16[160,512]{1,0:T(8,128)(2,1)S(1)}, u32[]{:S(2)}) copy-start(bf16[160,512]{1,0:T(8,128)(2,1)S(1)} %get-tuple-element.38) | copy-start | bytes 491524
  461.9 40.7 %copy-start.20 = (bf16[160,512]{1,0:T(8,128)(2,1)}, bf16[160,512]{1,0:T(8,128)(2,1)S(1)}, u32[]{:S(2)}) copy-start(bf16[160,512]{1,0:T(8,128)(2,1)S(1)} %get-tuple-element.39) | copy-start | bytes 491524
  465.3 78.0 %reduce-scatter.5.cloned.1.call-start = ((), (), s32[]{:S(2)}) async-start(), calls=%async_computation.3 | async-start | bytes 1638400 | tf_op jit(solution)/shard_map/reduce_scatter | solution.py:107
  501.4 175.9 %all-gather.37.cloned.1.call-start = ((), (), s32[]{:S(2)}) async-start(), calls=%async_computation.15 | async-start | bytes 3276800 | tf_op jit(solution)/shard_map/all_gather | solution.py:554
  502.0 175.3 %all-gather.35.cloned.1.call-start = ((), (), s32[]{:S(2)}) async-start(), calls=%async_computation.14 | async-start | bytes 6553600 | tf_op jit(solution)/shard_map/all_gather | solution.py:554
  502.6 183.1 %all-gather.23.cloned.1.call-start = ((), (), s32[]{:S(2)}) async-start(), calls=%async_computation.8 | async-start | bytes 2949120 | tf_op jit(solution)/shard_map/all_gather | solution.py:569
  503.5 182.2 %all-gather.21.cloned.1.call-start = ((), (), s32[]{:S(2)}) async-start(), calls=%async_computation.7 | async-start | bytes 5898240 | tf_op jit(solution)/shard_map/all_gather | solution.py:569
  504.2 208.5 %all-gather.19.cloned.1.call-start = ((), (), s32[]{:S(2)}) async-start(), calls=%async_computation.6 | async-start | bytes 2949120 | tf_op jit(solution)/shard_map/all_gather | solution.py:569
  505.1 250.5 %all-gather.17.cloned.1.call-start = ((), (), s32[]{:S(2)}) async-start(), calls=%async_computation.5 | async-start | bytes 5898240 | tf_op jit(solution)/shard_map/all_gather | solution.py:569
  505.8 286.6 %all-gather.27.cloned.1.call-start = ((), (), s32[]{:S(2)}) async-start(), calls=%async_computation.10 | async-start | bytes 1474560 | tf_op jit(solution)/shard_map/all_gather | solution.py:569
  506.4 318.1 %all-gather.25.cloned.1.call-start = ((), (), s32[]{:S(2)}) async-start(), calls=%async_computation.9 | async-start | bytes 5898240 | tf_op jit(solution)/shard_map/all_gather | solution.py:569
  507.0 358.7 %all-gather.29.cloned.1.call-start = ((), (), s32[]{:S(2)}) async-start(), calls=%async_computation.11 | async-start | bytes 3276800 | tf_op jit(solution)/shard_map/all_gather | solution.py:554
  507.6 553.1 %all-gather.31.cloned.1.call-start = ((), (), s32[]{:S(2)}) async-start(), calls=%async_computation.12 | async-start | bytes 26214400 | tf_op jit(solution)/shard_map/all_gather | solution.py:554
  508.4 593.6 %all-gather.33.cloned.1.call-start = ((), (), s32[]{:S(2)}) async-start(), calls=%async_computation.13 | async-start | bytes 3276800 | tf_op jit(solution)/shard_map/all_gather | solution.py:554
  510.5 652.1 %all-reduce.16.cloned.1.call-start = ((), (), s32[]{:S(2)}) async-start(), calls=%async_computation.4 | async-start | bytes 458752 | tf_op jit(solution)/shard_map/psum | solution.py:579
  564.4 12.1 %slice-start = ((bf16[160,50,112]{2,0,1:T(8,128)(2,1)}), bf16[160,49,112]{2,0,1:T(8,128)(2,1)S(1)}, s32[]{:S(2)}) async-start(bf16[160,50,112]{2,0,1:T(8,128)(2,1)} %copy-done.2), calls=%async_computation.16 | async-start | bytes 4014080 | tf_op jit(solution)/shard_map/slice | solution.py:40
  564.4 12.1 %copy-start.36 = (pred[112]{0:T(512)(128)(4,1)S(1)}, pred[112]{0:T(512)(128)(4,1)}, u32[]{:S(2)}) copy-start(pred[112]{0:T(512)(128)(4,1)} %copy-done.35) | copy-start | bytes 340
  564.4 12.1 %copy-start.38 = (pred[112]{0:T(512)(128)(4,1)S(1)}, pred[112]{0:T(512)(128)(4,1)}, u32[]{:S(2)}) copy-start(pred[112]{0:T(512)(128)(4,1)} %copy-done.37) | copy-start | bytes 340
  564.4 12.1 %copy-start.40 = (pred[112]{0:T(512)(128)(4,1)S(1)}, pred[112]{0:T(512)(128)(4,1)}, u32[]{:S(2)}) copy-start(pred[112]{0:T(512)(128)(4,1)} %copy-done.39) | copy-start | bytes 340
  564.4 12.2 %copy-start.42 = (pred[112]{0:T(512)(128)(4,1)S(1)}, pred[112]{0:T(512)(128)(4,1)}, u32[]{:S(2)}) copy-start(pred[112]{0:T(512)(128)(4,1)} %copy-done.41) | copy-start | bytes 340
  564.4 12.2 %copy-start.44 = (pred[112]{0:T(512)(128)(4,1)S(1)}, pred[112]{0:T(512)(128)(4,1)}, u32[]{:S(2)}) copy-start(pred[112]{0:T(512)(128)(4,1)} %copy-done.43) | copy-start | bytes 340
  564.4 12.2 %copy-start.46 = (pred[112]{0:T(512)(128)(4,1)S(1)}, pred[112]{0:T(512)(128)(4,1)}, u32[]{:S(2)}) copy-start(pred[112]{0:T(512)(128)(4,1)} %copy-done.45) | copy-start | bytes 340
  589.3 11.9 %copy-start.29 = (s32[8000]{0:T(1024)S(1)}, s32[8000]{0:T(1024)}, u32[]{:S(2)}) copy-start(s32[8000]{0:T(1024)} %copy-done.28) | copy-start | bytes 96004
  601.2 42.2 %copy-start.11 = (bf16[112,8000]{1,0:T(8,128)(2,1)S(1)}, bf16[112,8000]{1,0:T(8,128)(2,1)}, u32[]{:S(2)}) copy-start(bf16[112,8000]{1,0:T(8,128)(2,1)} %copy.125) | copy-start | bytes 5376004
  1142.1 22.1 %copy-start.1 = (s32[16,20,50]{2,0,1:T(8,128)S(1)}, s32[16,20,50]{2,0,1:T(8,128)}, u32[]{:S(2)}) copy-start(s32[16,20,50]{2,0,1:T(8,128)} %param.14) | copy-start | bytes 192004
  (24 other events, 102.7 us)
Sparse Core Ops, SparseCore 0:
  465.4 29.6 reduce-scatter.2
  501.6 29.9 reduce-scatter.4
Sparse Core Ops, SparseCore 1:
  503.8 39.3 all-gather.36
  544.8 60.9 all-gather.34
  607.5 30.0 all-gather.22
  639.4 41.5 all-gather.20
  682.9 29.8 all-gather.18
  714.6 40.9 all-gather.16
  757.4 24.4 all-gather.26
  783.6 40.9 all-gather.24
  826.3 39.4 all-gather.28
  867.7 193.0 all-gather.30
  1062.4 39.4 all-gather.32
  1105.6 51.8 all-reduce.15

commit v2 on v1

--- a/solution.py
+++ b/solution.py
@@ -1,3 +1,5 @@
+import functools
+
 import jax
 import jax.numpy as jnp
 from jax import lax
@@ -10,6 +12,7 @@
 PERIODS = 32
 TAPS = 7
 VMEM_LIMIT = 62 * 1024 * 1024
+SLOTS = 4
 
 
 def dot(left, right, left_dim, right_dim):
@@ -141,12 +144,16 @@
     w_in_t,
     w_state_t,
     proj_t,
+    x_all,
+    state_all,
+    hidden_all,
+    gates_all,
+    projected_all,
+    input_out,
     x_out,
     state_out,
     hidden_out,
-    gates_out,
     projected_out,
-    input_out,
     acts,
     cells,
     clips,
@@ -166,6 +173,14 @@
     above_send,
     above_recv,
     gate_sem,
+    gate_send,
+    own_sem,
+    row_send,
+    row_recv,
+    relay_send,
+    relay_recv,
+    lift_send,
+    lift_recv,
 ):
     count = lax.axis_size("mp")
     me = lax.axis_index("mp")
@@ -174,12 +189,21 @@
     cell_count = proj_ref.shape[1]
     chunk = min(256, cell_count)
     peers = [lax.rem(me + j, count) for j in range(1, count)]
+    groups = lax.axis_size("dp")
+    group = lax.axis_index("dp")
+    others = [lax.rem(group + j, groups) for j in range(1, groups)]
+    relayed = groups == 4
+    beside = group + 1 - 2 * lax.rem(group, 2)
+    across = lax.rem(group + 2, 4)
+    near = [beside, across] if relayed else others
 
     barrier = pltpu.get_barrier_semaphore()
     for peer in peers:
         pl.semaphore_signal(barrier, inc=1, device_id={"mp": peer}, device_id_type=MESH)
     pl.semaphore_signal(barrier, inc=1, device_id={"section": 1 - section}, device_id_type=MESH)
-    pl.semaphore_wait(barrier, count)
+    for other in others:
+        pl.semaphore_signal(barrier, inc=1, device_id={"dp": other}, device_id_type=MESH)
+    pl.semaphore_wait(barrier, count + groups - 1)
 
     def wide(values, width):
         return jnp.concatenate([values] * (width // values.shape[1]), axis=1)
@@ -229,9 +253,44 @@
             device_id_type=MESH,
         )
 
-    def gates_copy(d, k, parity):
+    def gates_copy(d, k, slot):
         return pltpu.make_async_copy(
-            gate_buf.at[d, parity], gates_out.at[d, k], gate_sem.at[d, parity]
+            gate_buf.at[d, slot], gates_all.at[d, group, k], gate_sem.at[d, slot]
+        )
+
+    def gates_row(d, k, slot, j, other):
+        return pltpu.make_async_remote_copy(
+            src_ref=gate_buf.at[d, slot],
+            dst_ref=gates_all.at[d, group, k],
+            send_sem=gate_send.at[d, slot, j],
+            recv_sem=row_recv.at[0, j],
+            device_id={"dp": other},
+            device_id_type=MESH,
+        )
+
+    def row(kind, source, target, j, other):
+        return pltpu.make_async_remote_copy(
+            src_ref=source,
+            dst_ref=target,
+            send_sem=row_send.at[kind, j],
+            recv_sem=row_recv.at[kind, j],
+            device_id={"dp": other},
+            device_id_type=MESH,
+        )
+
+    def from_peer(j, targets):
+        back = len(targets) - 1 - j
+        return targets[j] if relayed and len(targets) == 2 else targets[back]
+
+    def relay(kind, buffer, d):
+        source, target = (beside, across) if d == 0 else (across, beside)
+        return pltpu.make_async_remote_copy(
+            src_ref=buffer.at[d, source],
+            dst_ref=buffer.at[d, source],
+            send_sem=relay_send.at[kind, d],
+            recv_sem=relay_recv.at[kind, d],
+            device_id={"dp": target},
+            device_id_type=MESH,
         )
 
     @pl.when(section == 0)
@@ -239,6 +298,8 @@
         copy = pltpu.make_async_copy(base_ref, x_out, base_sem)
         copy.start()
         copy.wait()
+        for j, other in enumerate(others):
+            row(1, x_out, x_all.at[:, group], j, other).start()
 
     for d in range(2):
         state_out[d, 0] = jnp.zeros(state_out.shape[2:], BF16)
@@ -280,6 +341,8 @@
             hidden_out[d, k, :, own] = (out_gate * jnp.tanh(cell_new)).astype(BF16)
         part = jnp.dot(hidden_out[d, k], proj_ref[d], preferred_element_type=F32)
         exchange_start(parts, send_sem, recv_sem, d, lax.rem(k, 2), part)
+        for j, other in enumerate(others):
+            row(2, hidden_out.at[d, k], hidden_all.at[d, group, k], j, other).start()
 
     def forward_state(d, k):
         total = exchange_wait(parts, send_sem, recv_sem, d, lax.rem(k, 2))
@@ -296,6 +359,9 @@
 
             pass_up(d, k).start()
 
+        for j, other in enumerate(others):
+            row(3, state_out.at[d, k + 1], state_all.at[d, group, k + 1], j, other).start()
+
     for d in range(2):
         input_part(d, 0)
     for d in range(2):
@@ -329,16 +395,23 @@
         exchange_start(back_parts, back_send, back_recv, d, parity, value)
 
     def backward_cells(d, k, total):
-        parity = lax.rem(k, 2)
+        slot = lax.rem(k, SLOTS)
         live = live_ref[d, k]
         clip = clips[d, k]
         grad_out = wide(live, clip.shape[1]) * (total + top_ref[d, k].astype(F32))
         grad_projected = (grad_out * (1.0 - clip * clip)).astype(BF16)
         projected_out[d, k] = grad_projected
 
-        @pl.when(k < steps - 2)
-        def _():
-            gates_copy(d, k + 2, parity).wait()
+        for j, other in enumerate(near):
+            row(
+                4, projected_out.at[d, k], projected_all.at[d, group, k], j, other
+            ).start()
+
+        @pl.when(k < steps - SLOTS)
+        def _():
+            gates_copy(d, k + SLOTS, slot).wait()
+            for j, other in enumerate(near):
+                gates_row(d, k + SLOTS, slot, j, other).wait_send()
 
         for start in range(0, cell_count, chunk):
             own = slice(start, start + chunk)
@@ -360,14 +433,17 @@
             )
             for block, value in enumerate(grads):
                 cols = slice(block * cell_count + start, block * cell_count + start + chunk)
-                gate_buf[d, parity, :, cols] = value.astype(BF16)
-        gates_copy(d, k, parity).start()
+                gate_buf[d, slot, :, cols] = value.astype(BF16)
+        gates_copy(d, k, slot).start()
+
+    def gates_send(d, k):
+        for j, other in enumerate(near):
+            gates_row(d, k, lax.rem(k, SLOTS), j, other).start()
 
     def backward_state(d, k):
         @pl.when(k > 0)
         def _():
-            parity = lax.rem(k, 2)
-            back = jnp.dot(gate_buf[d, parity], w_state_t[d], preferred_element_type=F32)
+            back = jnp.dot(gate_buf[d, lax.rem(k, SLOTS)], w_state_t[d], preferred_element_type=F32)
             pre[d, :, : back.shape[1]] = back
 
             @pl.when(section == 0)
@@ -378,8 +454,8 @@
             back_start(d, lax.rem(k - 1, 2), pre[d, :, : back.shape[1]])
 
     def backward_input(d, k):
-        parity = lax.rem(k, 2)
-        part = jnp.dot(gate_buf[d, parity], w_in_t[d], preferred_element_type=F32)
+        gates_send(d, k)
+        part = jnp.dot(gate_buf[d, lax.rem(k, SLOTS)], w_in_t[d], preferred_element_type=F32)
 
         @pl.when(section == 1)
         def _():
@@ -428,13 +504,105 @@
             backward_input(d, k)
 
     for d in range(2):
-        for k in range(min(2, steps)):
-            gates_copy(d, k, k % 2).wait()
+        for k in range(min(SLOTS, steps)):
+            gates_copy(d, k, k % SLOTS).wait()
+            for j, other in enumerate(near):
+                gates_row(d, k, k % SLOTS, j, other).wait_send()
 
     @pl.when(section == 1)
     def _():
         for d in range(2):
             pass_down(d, 0).wait_send()
+
+    own = [
+        (hidden_out, hidden_all.at[:, group]),
+        (state_out, state_all.at[:, group]),
+        (projected_out, projected_all.at[:, group]),
+    ]
+    for other in others:
+        own.append((state_out.at[:, 0], state_all.at[:, other, 0]))
+    own = [
+        pltpu.make_async_copy(source, target, own_sem.at[i])
+        for i, (source, target) in enumerate(own)
+    ]
+    for copy in own:
+        copy.start()
+
+    rest = pl.ds(1, steps)
+    for j, other in enumerate(others):
+        source = from_peer(j, others)
+        hidden_row = row(2, hidden_out, hidden_all.at[:, source], j, other)
+        state_row = row(3, state_out.at[:, rest], state_all.at[:, source, rest], j, other)
+        for copy in (hidden_row, state_row):
+            copy.wait_send()
+            copy.wait_recv()
+
+    for copy in own:
+        copy.wait()
+
+    @pl.when(section == 0)
+    def _():
+        mine = pltpu.make_async_copy(x_out, x_all.at[:, group], base_sem)
+        mine.start()
+        for j, other in enumerate(others):
+            copy = row(1, x_out, x_all.at[:, from_peer(j, others)], j, other)
+            copy.wait_send()
+            copy.wait_recv()
+        mine.wait()
+
+    def lift():
+        return pltpu.make_async_remote_copy(
+            src_ref=state_all.at[:, :, rest],
+            dst_ref=x_all,
+            send_sem=lift_send,
+            recv_sem=lift_recv,
+            device_id={"section": 1 - section},
+            device_id_type=MESH,
+        )
+
+    @pl.when(section == 0)
+    def _():
+        lift().start()
+
+    for j, other in enumerate(near):
+        source = from_peer(j, near)
+        pltpu.make_async_remote_copy(
+            src_ref=gates_all.at[:, source],
+            dst_ref=gates_all.at[:, source],
+            send_sem=row_send.at[0, j],
+            recv_sem=row_recv.at[0, j],
+            device_id={"dp": other},
+            device_id_type=MESH,
+        ).wait_recv()
+        projected_row = row(4, projected_out, projected_all.at[:, source], j, other)
+        projected_row.wait_send()
+        projected_row.wait_recv()
+
+    if relayed:
+        for d in range(2):
+            relay(0, gates_all, d).start()
+            relay(1, projected_all, d).start()
+        for d in range(2):
+            for kind, buffer in ((0, gates_all), (1, projected_all)):
+                copy = relay(kind, buffer, d)
+                copy.wait_send()
+                far = 3 - group
+                pltpu.make_async_remote_copy(
+                    src_ref=buffer.at[d, far],
+                    dst_ref=buffer.at[d, far],
+                    send_sem=relay_send.at[kind, d],
+                    recv_sem=relay_recv.at[kind, d],
+                    device_id={"dp": across if d == 0 else beside},
+                    device_id_type=MESH,
+                ).wait_recv()
+
+    @pl.when(section == 0)
+    def _():
+        lift().wait_send()
+
+    @pl.when(section == 1)
+    def _():
+        lift().wait_recv()
 
 
 def recurrence(base_seq, live_seq, top_seq, layer_weights):
@@ -442,6 +610,7 @@
     _, steps, rows, width = base_seq.shape
     cell_count = proj.shape[1]
     count = lax.axis_size("mp")
+    groups = lax.axis_size("dp")
     weights = (
         w_in,
         w_state,
@@ -455,16 +624,20 @@
     return pl.pallas_call(
         recurrence_kernel,
         out_shape=(
-            jax.ShapeDtypeStruct((2, steps, rows, width), BF16),
-            jax.ShapeDtypeStruct((2, steps + 1, rows, width), BF16),
-            jax.ShapeDtypeStruct((2, steps, rows, cell_count), BF16),
-            jax.ShapeDtypeStruct((2, steps, rows, 4 * cell_count), BF16),
-            jax.ShapeDtypeStruct((2, steps, rows, width), BF16),
+            jax.ShapeDtypeStruct((2, groups, steps, rows, width), BF16),
+            jax.ShapeDtypeStruct((2, groups, steps + 1, rows, width), BF16),
+            jax.ShapeDtypeStruct((2, groups, steps, rows, cell_count), BF16),
+            jax.ShapeDtypeStruct((2, groups, steps, rows, 4 * cell_count), BF16),
+            jax.ShapeDtypeStruct((2, groups, steps, rows, width), BF16),
             jax.ShapeDtypeStruct((2, steps, rows, width), F32),
         ),
         in_specs=[ANY_SPEC] + [VMEM_SPEC] * 9,
-        out_specs=(VMEM_SPEC, VMEM_SPEC, VMEM_SPEC, ANY_SPEC, VMEM_SPEC, VMEM_SPEC),
+        out_specs=(*[ANY_SPEC] * 5, VMEM_SPEC),
         scratch_shapes=[
+            pltpu.VMEM((2, steps, rows, width), BF16),
+            pltpu.VMEM((2, steps + 1, rows, width), BF16),
+            pltpu.VMEM((2, steps, rows, cell_count), BF16),
+            pltpu.VMEM((2, steps, rows, width), BF16),
             pltpu.VMEM((2, steps, 4, rows, cell_count), F32),
             pltpu.VMEM((2, steps + 1, rows, cell_count), F32),
             pltpu.VMEM((2, steps, rows, width), F32),
@@ -473,7 +646,7 @@
             pltpu.VMEM((2, 2, count, rows, width), BF16),
             pltpu.VMEM((2, 2, count, rows, width), BF16),
             pltpu.VMEM((2, steps, rows, width), F32),
-            pltpu.VMEM((2, 2, rows, 4 * cell_count), BF16),
+            pltpu.VMEM((2, SLOTS, rows, 4 * cell_count), BF16),
             dma,
             dma((2, 2, count - 1)),
             dma((2, 2, count)),
@@ -483,13 +656,94 @@
             dma((2, steps)),
             dma((2,)),
             dma((2, steps)),
+            dma((2, SLOTS)),
+            dma((2, SLOTS, groups - 1)),
+            dma((groups + 2,)),
+            dma((5, groups - 1)),
+            dma((5, groups - 1)),
             dma((2, 2)),
+            dma((2, 2)),
+            dma,
+            dma,
         ],
         compiler_params=pltpu.CompilerParams(
             collective_id=0, has_side_effects=True, vmem_limit_bytes=VMEM_LIMIT
         ),
         name="recurrence",
     )(base_seq, live_seq, top_seq, *weights)
+
+
+def weight_grads(lefts, right, parts):
+    batch, tokens, _ = lefts[0].shape
+    sizes = [left.shape[2] for left in lefts]
+    columns = right.shape[2] // parts
+    block = min(256, columns)
+    blocks = columns // block
+    chunk = 256
+
+    def kernel(*refs):
+        left_refs = refs[: len(lefts)]
+        right_refs = refs[len(lefts) : len(lefts) + parts]
+        out_refs = refs[len(lefts) + parts : -3]
+        bias_out, turned, ones = refs[-3:]
+
+        @pl.when(pl.program_id(1) == 0)
+        def _():
+            start = 0
+            for left, size in zip(left_refs, sizes):
+                for offset in range(0, size, chunk):
+                    turned[start + offset : start + offset + chunk, :] = left[
+                        0, :, offset : offset + chunk
+                    ].T
+                start += size
+            ones[...] = jnp.ones_like(ones)
+
+        start = 0
+        for out, size in zip(out_refs, sizes):
+
+            @pl.loop(0, size // chunk)
+            def _(i):
+                at = pl.multiple_of(start + i * chunk, chunk)
+                own = pl.multiple_of(i * chunk, chunk)
+                left = turned[pl.ds(at, chunk), :]
+                for part in range(parts):
+                    out[0, pl.ds(own, chunk), part, :] = jnp.dot(
+                        left, right_refs[part][0], preferred_element_type=F32
+                    )
+
+            start += size
+        for part in range(parts):
+            bias_out[0, part : part + 1, :] = jnp.dot(
+                ones[...], right_refs[part][0], preferred_element_type=F32
+            )[:1]
+
+    return pl.pallas_call(
+        kernel,
+        out_shape=(
+            *[jax.ShapeDtypeStruct((batch, size, parts, columns), F32) for size in sizes],
+            jax.ShapeDtypeStruct((batch, parts, columns), F32),
+        ),
+        grid=(batch, blocks),
+        in_specs=[
+            *[pl.BlockSpec((1, tokens, size), lambda b, n: (b, 0, 0)) for size in sizes],
+            *[
+                pl.BlockSpec(
+                    (1, tokens, block), functools.partial(lambda g, b, n: (b, 0, g * blocks + n), g)
+                )
+                for g in range(parts)
+            ],
+        ],
+        out_specs=(
+            *[pl.BlockSpec((1, size, parts, block), lambda b, n: (b, 0, 0, n)) for size in sizes],
+            pl.BlockSpec((1, parts, block), lambda b, n: (b, 0, n)),
+        ),
+        scratch_shapes=[
+            pltpu.VMEM((sum(sizes), tokens), BF16),
+            pltpu.VMEM((16, tokens), BF16),
+        ],
+        compiler_params=pltpu.CompilerParams(vmem_limit_bytes=VMEM_LIMIT),
+        name="weight_grads",
+    )(*lefts, *[right] * parts)
 
 
 def on_device(
@@ -537,11 +791,9 @@
         lstm_bias[0].reshape(2, -1),
         lstm_proj[0],
     )
-    inputs_all, state_all, hidden_all, grad_gates, grad_projected, input_parts = recurrence(
+    all_inputs, all_states, all_hidden, all_gates, all_projected, input_parts = recurrence(
         base_seq, live_seq, top_seq, layer_weights
     )
-
-    state_all = state_all[:, :steps]
     both = input_parts[0] + jnp.flip(input_parts[1], axis=0)
     grad_base = lax.psum(both, "mp").astype(BF16)
     lower, upper = grad_base[:, :half], grad_base[:, half:]
@@ -550,51 +802,40 @@
     grad_half = jnp.transpose(grad_half, (1, 0, 2)).reshape(half * steps, proj_width)
     table_grad, conv_grad, conv_bias_grad, mixed_grads = cnn_backward(grad_half, saved, weights)
 
-    def all_rows(values):
-        return lax.all_gather(values, "dp", axis=0, tiled=False)
-
-    def weight_grad(left, right):
-        return lax.dot_general(
-            left, right, (((0, 2, 3), (0, 2, 3)), ((1,), (1,))), preferred_element_type=F32
-        )
-
-    all_inputs, all_states, all_hidden, all_gates, all_projected = [
-        all_rows(item) for item in (inputs_all, state_all, hidden_all, grad_gates, grad_projected)
-    ]
-    input_grad = weight_grad(all_inputs, all_gates)
-    state_grad = weight_grad(all_states, all_gates)
-    proj_grad = weight_grad(all_hidden, all_projected)
+    def flat(values):
+        return values.reshape(2, -1, values.shape[4])
+
+    input_grad, state_grad, bias_grad = weight_grads(
+        [flat(all_inputs), flat(all_states[:, :, :steps])], flat(all_gates), 4
+    )
+    proj_grad = lax.dot_general(
+        flat(all_hidden),
+        flat(all_projected),
+        (((1,), (1,)), ((0,), (0,))),
+        preferred_element_type=F32,
+    )
 
     def all_tokens(values):
-        return lax.all_gather(values, ("section", "dp"), axis=0, tiled=True)
+        return lax.all_gather(values, ("section", "dp"), axis=values.ndim - 2, tiled=True)
 
     layers, gathered_last = saved[7], saved[8]
-    high_grad = jnp.stack(
-        [
-            dot(all_tokens(layer[0]), all_tokens(grad_mixed), 0, 0)
-            for layer, grad_mixed in zip(layers, mixed_grads)
-        ]
-    )
-    proj_weight_grad = dot(all_tokens(gathered_last), all_tokens(grad_half), 0, 0)
-    small = lax.psum(
-        (
-            conv_grad,
-            conv_bias_grad,
-            jnp.stack([jnp.sum(item.astype(F32), axis=0) for item in mixed_grads]),
-            jnp.sum(grad_half.astype(F32), axis=0),
-        ),
-        ("section", "dp"),
-    )
-    bias_grad = lax.psum(jnp.sum(grad_gates.astype(F32), axis=(1, 2)), "dp")
+    high_grad, high_bias_grad = weight_grads(
+        [all_tokens(jnp.stack([layer[0] for layer in layers]))],
+        all_tokens(jnp.stack(mixed_grads)),
+        2,
+    )
+    all_base = all_tokens(grad_half)
+    proj_weight_grad = dot(all_tokens(gathered_last), all_base, 0, 0)
+    small = lax.psum((conv_grad, conv_bias_grad), ("section", "dp"))
     table_grad = lax.psum(table_grad, ("section", "mp", "dp"))
     return (
         table_grad,
         small[0],
         small[1],
-        high_grad.reshape(highway_weight.shape),
-        small[2].reshape(highway_bias.shape),
+        high_grad,
+        high_bias_grad,
         proj_weight_grad,
-        small[3],
+        jnp.sum(all_base.astype(F32), axis=0),
         input_grad.reshape(lstm_input.shape),
         state_grad.reshape(lstm_state.shape),
         bias_grad.reshape(lstm_bias.shape),

time: 1170 us -> 847 us (0.72)
  waiting for transfers between devices: 363 us -> 49 us
  Pallas kernels: 226 us -> 388 us
  local copies, waits for them, and re-layouts: 226 us -> 158 us
  matrix products: 109 us -> 48.5 us
  blocking collectives: 166 us -> 137 us
  other arithmetic: 63.2 us -> 43.5 us
    all_gather x11 -> x4, waiting for transfers between devices: 328 us -> 0.03 us  [all_tokens(): lax.all_gather(values, ('section', 'dp'), axis=values.ndim - 2, tiled=True)]
    pallas_call x1 -> x3, Pallas kernels: 226 us -> 388 us  [the longest x1 318 us: recurrence(): pl.pallas_call(recurrence_kernel, out_shape=(jax.ShapeDtypeStruct((2, gro...]
    reshape x4 -> x0, local copies, waits for them, and re-layouts: 41.7 us -> none  [the longest x1 20.5 us: on_device(): state_grad.reshape(lstm_state.shape)]
    dot_general x3 -> x1, matrix products: 47.7 us -> 8.27 us  [on_device(): lax.dot_general(flat(all_hidden), flat(all_projected), (((1,), (1,)), ((0...]
    psum x2 -> x1, blocking collectives: 46.3 us -> 15.7 us  [on_device(): small = lax.psum((conv_grad, conv_bias_grad), ('section', 'dp'))]
    another operation x2 -> x0, local copies, waits for them, and re-layouts: 26.5 us -> none  [on_device(): jnp.stack([dot(all_tokens(layer[0]), all_tokens(grad_mixed), 0, 0) for la...]
    dot_general x9 -> x7, matrix products: 50 us -> 31.3 us  [dot(): lax.dot_general(left, right, (((left_dim,), (right_dim,)), ((), ())), pre...]
    psum x1, waiting for transfers between devices: 0.01 us -> 18.1 us  [on_device(): small = lax.psum((conv_grad, conv_bias_grad), ('section', 'dp'))]
  transfers between devices with their start and end apart: 15 -> 8, of which waited for: 8 -> 3; matrix products, arithmetic and copies ran while one was open for 21% -> 13% of each run, Pallas kernels for 0% -> 8%
where the time goes in v2:
time: 847 us; the launch traced here: 842 us
  Pallas kernels  388 us (46%)
  local copies, waits for them, and re-layouts  158 us (19%)
  blocking collectives  137 us (16%)
  waiting for transfers between devices  49 us (6%)
  matrix products  48.5 us (6%)
  other arithmetic  43.5 us (5%)
  between operations  17.1 us (2%)
    pallas_call x1, Pallas kernels, recurrence(): pl.pallas_call(recurrence_kernel, out_shape=(jax.ShapeDtypeStruct((2, gro...  318 us
    pallas_call x2, Pallas kernels, weight_grads(): pl.pallas_call(kernel, out_shape=(*[jax.ShapeDtypeStruct((batch, size, pa...  69.8 us
    all_gather x3, blocking collectives, spread(): return lax.all_gather(values, 'mp', axis=1, tiled=True)  51.4 us
    unnamed x113, local copies, waits for them, and re-layouts  45.1 us
    psum x1, blocking collectives, on_device(): table_grad = lax.psum(table_grad, ('section', 'mp', 'dp'))  39.7 us
    dot_general x7, matrix products, dot(): lax.dot_general(left, right, (((left_dim,), (right_dim,)), ((), ())), pre...  31.3 us
    reduce_scatter x2, waiting for transfers between devices, cnn_backward(): lax.psum_scatter(dot(weight_here, grad_mixed, 1, 1), 'mp', scatter_dimens...  28.7 us
    psum x1, blocking collectives, on_device(): grad_base = lax.psum(both, 'mp').astype(BF16)  28.1 us
  transfers between devices with their start and end apart: 8, of which 3 were waited for; matrix products, arithmetic and copies ran while one was open for 13% of the time, Pallas kernels for 8%

profile of v2, /device:TPU:0, one launch (start us, length us, event | category | flops | bytes accessed | tf_op | source)
XLA Modules:
  0.0 842.4 jit_solution(9277960674711102874)
XLA Ops:
  9.8 2.2 convolution_convert_fusion
  12.1 15.1 %reshape.353 = bf16[160,50,112]{1,0,2:T(8,128)(2,1)} reshape(bf16[8000,112]{0,1:T(8,128)(2,1)S(1)} %convolution_convert_fusion) | data formatting | bytes 3584000 | tf_op jit(solution)/shard_map/reshape | solution.py:58
  27.2 8.3 copy.67
  45.2 5.5 select_select_fusion
  50.8 2.6 fusion
  53.5 4.6 fusion.1
  58.1 3.7 copy-done.3
  62.0 19.6 %all_gather.24 = bf16[160,2048]{1,0:T(8,128)(2,1)S(1)} all-gather(bf16[160,512]{1,0:T(8,128)(2,1)S(1)} %get-tuple-element.39), channel_id=1, replica_groups=mesh['section'=2,'mp'=4,'dp'=4] {'mp'}, dimensions={1}, use_global_device_ids=true | all-gather | bytes 819200 | tf_op jit(solution)/shard_map/all_gather | solution.py:47
  81.7 6.3 fusion.40
  91.4 16.1 %all_gather.25 = bf16[160,2048]{1,0:T(8,128)(2,1)S(1)} all-gather(bf16[160,512]{1,0:T(8,128)(2,1)S(1)} %get-tuple-element.37), channel_id=1, replica_groups=mesh['section'=2,'mp'=4,'dp'=4] {'mp'}, dimensions={1}, use_global_device_ids=true | all-gather | bytes 819200 | tf_op jit(solution)/shard_map/all_gather | solution.py:47
  111.8 15.7 %all_gather.26 = bf16[160,2048]{1,0:T(8,128)(2,1)S(1)} all-gather(bf16[160,512]{1,0:T(8,128)(2,1)S(1)} %add_convert_fusion), channel_id=1, replica_groups=mesh['section'=2,'mp'=4,'dp'=4] {'mp'}, dimensions={1}, use_global_device_ids=true | all-gather | bytes 819200 | tf_op jit(solution)/shard_map/all_gather | solution.py:47
  127.5 2.3 fusion.7
  129.9 2.0 all_gather.27
  133.4 13.7 %copy.76 = bf16[1,2,512,4,1024]{2,4,3,1,0:T(8,128)(2,1)} copy(bf16[1,2,512,4,1024]{4,3,2,1,0:T(4,128)(2,1)} %param.24) | data formatting | bytes 16777216 | tf_op args[10]
  147.0 11.9 %copy.79.w_in = bf16[2,512,4096]{2,1,0:T(8,128)(2,1)} copy(bf16[2,512,4096]{1,2,0:T(8,128)(2,1)} %bitcast.110) | data formatting | bytes 16777216 | tf_op jit(solution)/shard_map/reshape;squeeze | solution.py:789
  159.0 13.7 %copy.77 = bf16[1,2,512,4,1024]{2,4,3,1,0:T(8,128)(2,1)} copy(bf16[1,2,512,4,1024]{4,3,2,1,0:T(4,128)(2,1)} %param.25) | data formatting | bytes 16777216 | tf_op args[11]
  172.6 12.0 %copy.80.w_state = bf16[2,512,4096]{2,1,0:T(8,128)(2,1)} copy(bf16[2,512,4096]{1,2,0:T(8,128)(2,1)} %bitcast.112) | data formatting | bytes 16777216 | tf_op jit(solution)/shard_map/reshape;squeeze | solution.py:790
  184.6 4.0 copy.78
  192.0 317.7 %recurrence.1 = (bf16[2,4,20,16,512]{4,3,2,1,0:T(8,128)(2,1)}, bf16[2,4,21,16,512]{4,3,2,1,0:T(8,128)(2,1)}, bf16[2,4,20,16,1024]{4,3,2,1,0:T(8,128)(2,1)}, bf16...) custom-call(bf16[2,20,16,512]{3,2,1,0:T(8,128)(2,1)} %pad_maximum_fusion.1.base_r, ...), custom_call_target="tpu_custom_call" | custom-call | tf_op jit(solution)/shard_map/recurrence/pallas_call | solution.py:624
  510.9 2.1 bitcast_add_fusion
  513.0 28.1 %all-reduce.16 = bf16[20,16,512]{2,1,0:T(8,128)(2,1)S(1)} all-reduce(f32[20,16,512]{2,1,0:T(8,128)} %bitcast_add_fusion), channel_id=1, replica_groups=mesh['section'=2,'mp'=4,'dp'=4] {'mp'}, use_global_device_ids=true, to_apply=%region_2.3 | all-reduce | flops 163840 | bytes 983040 | tf_op jit(solution)/shard_map/psum | solution.py:798
  543.6 1.7 multiply_convert_fusion.4
  546.0 2.6 convolution_bitcast_fusion.1
  549.3 28.7 %reduce-scatter.3.cloned.1.call-done = f32[512,160]{0,1:T(8,128)} async-done(((f32[2048,160]{0,1:T(8,128)}), f32[512,160]{0,1:T(8,128)}) %reduce-scatter.3.cloned.1.call-update) | async-done | bytes 327696 | tf_op jit(solution)/shard_map/reduce_scatter | solution.py:110
  579.5 4.8 convolution_bitcast_fusion
  585.9 2.6 pad_maximum_fusion
  588.6 2.2 copy.85
  590.9 1.7 slice.109
  592.6 3.0 reshape.335
  595.6 2.7 copy.86
  598.3 41.9 %weight_grads.3 = (f32[2,512,4,1024]{3,2,1,0:T(4,128)}, f32[2,512,4,1024]{3,2,1,0:T(4,128)}, f32[2,4,1024]{2,1,0:T(4,128)}) custom-call(bf16[2,1280,512]{2,1,0:T(8,128)(2,1)} %bitcast.132, bf16[2,1280,512]{2,1,0:T(8,128)(2,1)} %bitcast.120, bf16[2,1280,4096]{2,1,0:T(8,128)(2,1)} %bitcast.106, bf16[2,1280,4096]{2,1,0:T(8,128)(2,1)} %bitcast.107, ...), custom_call_target="tpu_custom_call" | custom-call | tf_op jit(solution)/shard_map/weight_grads/pallas_call | solution.py:720
  640.2 8.3 convolution_bitcast_fusion.2
  648.5 2.1 convert_reduce_fusion.1
  652.0 11.7 %convert_reduce_fusion = (f32[512]{0:T(512)S(1)}, bf16[160,50,512]{2,0,1:T(8,128)(2,1)}) fusion(f32[160,512]{1,0:T(8,128)S(1)} %fusion.26, f32[160,512]{1,0:T(8,128)S(1)} %get-tuple-element.49, f32[160,50,512]{2,0,1:T(8,128)} %copy-done.3, f32[512]{0:T(512)S(1)} %copy-done.30, pred[50,512]{1,0:T(8,128)(4,1)S(1)} %iota_compare_fusion.2), kind=kLoop, calls=%fused_computation | loop fusion | flops 32767488 | bytes 25261056 | tf_op jit(solution)/shard_map/reduce_sum | solution.py:119
  663.6 11.8 %copy.87 = bf16[160,50,512]{2,1,0:T(8,128)(2,1)} copy(bf16[160,50,512]{2,0,1:T(8,128)(2,1)} %get-tuple-element.34) | data formatting | bytes 16384000 | tf_op jit(solution)/shard_map/convert_element_type | solution.py:115
  675.4 6.2 fusion.42
  688.8 12.0 %reshape.351 = bf16[8000,512,1]{1,0,2:T(8,128)(2,1)} reshape(bf16[160,50,512]{2,1,0:T(8,128)(2,1)} %copy.87) | data formatting | bytes 16384000 | tf_op jit(solution)/shard_map/reshape | solution.py:116
  700.8 7.3 select_convert_fusion
  709.0 2.2 reshape.334
  711.1 4.0 copy.84
  715.1 15.7 %psum.31 = f32[512]{0:T(512)} all-reduce(f32[512]{0:T(512)S(1)} %get-tuple-element.33), channel_id=1, replica_groups=mesh['section'=2,'mp'=4,'dp'=4] {'section','dp'}, use_global_device_ids=true, to_apply=%region_9.10 | all-reduce | flops 512 | bytes 4096 | tf_op jit(solution)/shard_map/psum | solution.py:829
  730.8 3.5 fusion.8
  734.3 39.7 %psum.29 = f32[262,16]{0,1:T(8,128)} all-reduce(f32[262,16]{0,1:T(8,128)S(1)} %fusion.8), channel_id=1, replica_groups=mesh['section'=2,'mp'=4,'dp'=4] {'section','mp','dp'}, use_global_device_ids=true, to_apply=%region_6.7 | all-reduce | flops 4192 | bytes 33536 | tf_op jit(solution)/shard_map/psum | solution.py:830
  774.1 5.5 convolution_select_fusion
  779.6 7.0 fusion.43
  786.6 27.9 %weight_grads.2 = (f32[2,2048,2,512]{3,2,1,0:T(2,128)}, f32[2,2,512]{2,1,0:T(2,128)}) custom-call(bf16[2,1280,2048]{2,1,0:T(8,128)(2,1)} %all-gather.5.cloned.1.call-done.refs_0_, bf16[2,1280,1024]{2,1,0:T(8,128)(2,1)} %all-gather.7.cloned.1.call-done.refs_1_.refs_2_, bf16[2,1280,1024]{2,1,0:T(8,128)(2,1)} %all-gather.7.cloned.1.call-done.refs_1_.refs_2_), custom_call_target="tpu_custom_call" | custom-call | tf_op jit(solution)/shard_map/weight_grads/pallas_call | solution.py:720
  814.6 18.1 %all-reduce.15.cloned.1.call-done = f32[7,16,512]{2,1,0:T(8,128)} async-done(((f32[7,16,512]{2,1,0:T(8,128)}), f32[7,16,512]{2,1,0:T(8,128)}) %all-reduce.15.cloned.1.call-update) | async-done | bytes 229392 | tf_op jit(solution)/shard_map/psum | solution.py:829
  832.7 1.6 copy.102
  (186 shorter events, 41.6 us)
Async XLA Ops:
  8.0 570.0 %reduce-scatter.3.cloned.1.call-start = ((), (), s32[]{:S(2)}) async-start(), calls=%async_computation.2 | async-start | bytes 1638400 | tf_op jit(solution)/shard_map/reduce_scatter | solution.py:110
  9.1 3.0 copy-start.27
  42.4 2.8 copy-start.24
  43.8 7.0 copy-start.35
  43.8 7.0 copy-start.37
  43.8 7.0 copy-start.39
  43.8 7.0 copy-start.41
  43.8 7.0 copy-start.43
  43.8 7.0 copy-start.45
  43.9 14.2 %copy-start.31 = (f32[512]{0:T(512)}, f32[512]{0:T(512)S(1)}, u32[]{:S(2)}) copy-start(f32[512]{0:T(512)S(1)} %convert_log_fusion) | copy-start | bytes 6148
  45.2 8.3 copy-start.29
  45.2 5.6 copy-start.21
  53.5 8.3 copy-start.3
  53.5 28.1 %slice-start.1 = ((s8[8388608]{0:T(1024)(128)(4,1)}), s8[4194304]{0:T(1024)(128)(4,1)S(1)}, s32[]{:S(2)}) async-start(s8[8388608]{0:T(1024)(128)(4,1)} %bitcast.124), calls=%async_computation.10 | async-start | bytes 8388608
  53.5 28.1 %slice-start.2 = ((s8[8388608]{0:T(1024)(128)(4,1)}), s8[4194304]{0:T(1024)(128)(4,1)S(1)}, s32[]{:S(2)}) async-start(s8[8388608]{0:T(1024)(128)(4,1)} %bitcast.124), calls=%async_computation.11 | async-start | bytes 8388608
  61.8 26.2 %copy-start.15 = (f32[160,512]{1,0:T(8,128)}, f32[160,512]{1,0:T(8,128)S(1)}, u32[]{:S(2)}) copy-start(f32[160,512]{1,0:T(8,128)S(1)} %fusion.1) | copy-start | bytes 983044
  81.7 7.6 copy-start.10
  91.4 19.3 %copy-start.19 = (f32[160,512]{1,0:T(8,128)}, f32[160,512]{1,0:T(8,128)S(1)}, u32[]{:S(2)}) copy-start(f32[160,512]{1,0:T(8,128)S(1)} %get-tuple-element.38) | copy-start | bytes 983044
  108.8 18.7 %copy-start.49 = (bf16[512]{0:T(512)(128)(2,1)S(1)}, bf16[512]{0:T(512)(128)(2,1)}, u32[]{:S(2)}) copy-start(bf16[512]{0:T(512)(128)(2,1)} %param.23) | copy-start | bytes 3076
  127.5 4.5 copy-start.12
  184.6 4.0 copy-start.25
  184.6 4.0 copy-start.33
  510.9 32.7 %copy-start.14 = (f32[160,1024]{1,0:T(8,128)S(1)}, f32[160,1024]{1,0:T(8,128)}, u32[]{:S(2)}) copy-start(f32[160,1024]{1,0:T(8,128)} %copy-done.13) | copy-start | bytes 1966084
  510.9 32.7 %copy-start.20 = (f32[160,512]{1,0:T(8,128)S(1)}, f32[160,512]{1,0:T(8,128)}, u32[]{:S(2)}) copy-start(f32[160,512]{1,0:T(8,128)} %copy-done.19) | copy-start | bytes 983044
  541.1 2.3 collective-permute-start
  548.6 99.8 %all-gather.11.cloned.1.call-start = ((), (), s32[]{:S(2)}) async-start(), calls=%async_computation.8 | async-start | bytes 1474560 | tf_op jit(solution)/shard_map/all_gather | solution.py:819
  549.2 101.4 %reduce-scatter.5.cloned.1.call-start = ((), (), s32[]{:S(2)}) async-start(), calls=%async_computation.3 | async-start | bytes 1638400 | tf_op jit(solution)/shard_map/reduce_scatter | solution.py:110
  584.2 195.4 %all-gather.9.cloned.1.call-start = ((), (), s32[]{:S(2)}) async-start(), calls=%async_computation.7 | async-start | bytes 5898240 | tf_op jit(solution)/shard_map/all_gather | solution.py:819
  584.8 201.8 %all-gather.7.cloned.1.call-start = ((), (), s32[]{:S(2)}) async-start(), calls=%async_computation.6 | async-start | bytes 5898240 | tf_op jit(solution)/shard_map/all_gather | solution.py:819
  585.8 2.8 copy-start.8
  585.9 200.8 %all-gather.5.cloned.1.call-start = ((), (), s32[]{:S(2)}) async-start(), calls=%async_computation.5 | async-start | bytes 11796480 | tf_op jit(solution)/shard_map/all_gather | solution.py:819
  588.6 244.1 %all-reduce.15.cloned.1.call-start = ((), (), s32[]{:S(2)}) async-start(), calls=%async_computation.4 | async-start | bytes 458752 | tf_op jit(solution)/shard_map/psum | solution.py:829
  640.2 10.4 %copy-start.16 = (f32[160,512]{1,0:T(8,128)S(1)}, f32[160,512]{1,0:T(8,128)}, u32[]{:S(2)}) copy-start(f32[160,512]{1,0:T(8,128)} %copy-done.15) | copy-start | bytes 983044
  640.2 10.4 %copy-start.32 = (f32[512]{0:T(512)S(1)}, f32[512]{0:T(512)}, u32[]{:S(2)}) copy-start(f32[512]{0:T(512)} %copy-done.31) | copy-start | bytes 6148
  648.5 3.5 copy-start.30
  663.6 11.8 %copy-start.22 = (bf16[7,16,512]{2,1,0:T(8,128)(2,1)S(1)}, bf16[7,16,512]{2,1,0:T(8,128)(2,1)}, u32[]{:S(2)}) copy-start(bf16[7,16,512]{2,1,0:T(8,128)(2,1)} %copy-done.21) | copy-start | bytes 344068
  681.7 5.7 copy-start.2
  688.8 12.0 %slice-start = ((bf16[160,50,112]{2,0,1:T(8,128)(2,1)}), bf16[160,49,112]{2,0,1:T(8,128)(2,1)S(1)}, s32[]{:S(2)}) async-start(bf16[160,50,112]{2,0,1:T(8,128)(2,1)} %copy-done.2), calls=%async_computation.9 | async-start | bytes 4014080 | tf_op jit(solution)/shard_map/slice | solution.py:43
  688.8 12.0 %copy-start.36 = (pred[112]{0:T(512)(128)(4,1)S(1)}, pred[112]{0:T(512)(128)(4,1)}, u32[]{:S(2)}) copy-start(pred[112]{0:T(512)(128)(4,1)} %copy-done.35) | copy-start | bytes 340
  688.8 12.0 %copy-start.38 = (pred[112]{0:T(512)(128)(4,1)S(1)}, pred[112]{0:T(512)(128)(4,1)}, u32[]{:S(2)}) copy-start(pred[112]{0:T(512)(128)(4,1)} %copy-done.37) | copy-start | bytes 340
  688.8 12.0 %copy-start.40 = (pred[112]{0:T(512)(128)(4,1)S(1)}, pred[112]{0:T(512)(128)(4,1)}, u32[]{:S(2)}) copy-start(pred[112]{0:T(512)(128)(4,1)} %copy-done.39) | copy-start | bytes 340
  688.8 12.0 %copy-start.42 = (pred[112]{0:T(512)(128)(4,1)S(1)}, pred[112]{0:T(512)(128)(4,1)}, u32[]{:S(2)}) copy-start(pred[112]{0:T(512)(128)(4,1)} %copy-done.41) | copy-start | bytes 340
  688.8 12.0 %copy-start.44 = (pred[112]{0:T(512)(128)(4,1)S(1)}, pred[112]{0:T(512)(128)(4,1)}, u32[]{:S(2)}) copy-start(pred[112]{0:T(512)(128)(4,1)} %copy-done.43) | copy-start | bytes 340
  688.8 12.0 %copy-start.46 = (pred[112]{0:T(512)(128)(4,1)S(1)}, pred[112]{0:T(512)(128)(4,1)}, u32[]{:S(2)}) copy-start(pred[112]{0:T(512)(128)(4,1)} %copy-done.45) | copy-start | bytes 340
  711.1 19.7 %copy-start.28 = (s32[8000]{0:T(1024)S(1)}, s32[8000]{0:T(1024)}, u32[]{:S(2)}) copy-start(s32[8000]{0:T(1024)} %copy-done.27) | copy-start | bytes 96004
  730.8 43.2 %copy-start.9 = (bf16[112,8000]{1,0:T(8,128)(2,1)S(1)}, bf16[112,8000]{1,0:T(8,128)(2,1)}, u32[]{:S(2)}) copy-start(bf16[112,8000]{1,0:T(8,128)(2,1)} %copy.86) | copy-start | bytes 5376004
  774.1 5.5 copy-start.18
  786.6 47.7 %copy-start.1 = (s32[16,20,50]{2,0,1:T(8,128)S(1)}, s32[16,20,50]{2,0,1:T(8,128)}, u32[]{:S(2)}) copy-start(s32[16,20,50]{2,0,1:T(8,128)} %param.14) | copy-start | bytes 192004
  (13 other events, 24.0 us)
Sparse Core Ops, SparseCore 0:
  548.8 29.1 reduce-scatter.2
  584.4 30.0 reduce-scatter.4
Sparse Core Ops, SparseCore 1:
  551.6 22.4 all-gather.10
  586.6 39.7 all-gather.8
  628.2 41.0 all-gather.6
  671.1 63.4 all-gather.4
  779.6 53.0 all-reduce.14

commit v3 on v2

v3 whole, which is shorter than its diff:
```python
import functools

import jax
import jax.numpy as jnp
from jax import lax
from jax.experimental import pallas as pl
from jax.experimental.pallas import tpu as pltpu
from jax.sharding import PartitionSpec as P

F32 = jnp.float32
BF16 = jnp.bfloat16
PERIODS = 32
TAPS = 7
VMEM_LIMIT = 62 * 1024 * 1024
SLOTS = 4
CHUNK = 16
TURN = 128
RELAY_SHARE = 4
PER_TOKEN = 50
CHARS = 262


def dot(left, right, left_dim, right_dim):
    return lax.dot_general(
        left, right, (((left_dim,), (right_dim,)), ((), ())), preferred_element_type=F32
    )


def soft_clip(values):
    return 3.0 * jnp.tanh(values / 3.0)


def filter_widths(offset, amount, total):
    period = total // PERIODS
    in_period = (offset + jnp.arange(amount, dtype=jnp.int32)) % period
    widths = jnp.ones((amount,), jnp.int32)
    for exponent in range(6):
        widths = widths + (in_period * 64 >= period * 2**exponent).astype(jnp.int32)
    return widths


MESH = pl.DeviceIdType.MESH
VMEM_SPEC = pl.BlockSpec(memory_space=pltpu.VMEM)
ANY_SPEC = pl.BlockSpec(memory_space=pl.ANY)


def column_peers():
    count = lax.axis_size("mp")
    me = lax.axis_index("mp")
    return [lax.rem(me + j, count) for j in range(1, count)]


def greet(devices):
    barrier = pltpu.get_barrier_semaphore()
    for device in devices:
        pl.semaphore_signal(barrier, inc=1, device_id=device, device_id_type=MESH)
    pl.semaphore_wait(barrier, len(devices))


def remote(source, target, send, recv, device):
    return pltpu.make_async_remote_copy(
        src_ref=source,
        dst_ref=target,
        send_sem=send,
        recv_sem=recv,
        device_id=device,
        device_id_type=MESH,
    )


def one_hot_columns(ids, vocabulary):
    symbols = lax.broadcasted_iota(jnp.int32, (vocabulary, ids.shape[1]), 0)
    return (symbols == ids).astype(F32).astype(BF16)


def cnn_forward_kernel(
    ids_ref,
    table_ref,
    flags_ref,
    masked_ref,
    log_positions,
    w_high,
    b_high,
    w_proj,
    b_proj,
    input_ref,
    state_ref,
    base_out,
    taps_out,
    peak_out,
    pooled_out,
    features,
    current_out,
    transform_out,
    gate_out,
    features_all,
    input_out,
    state_out,
    raw,
    turned,
    send_sem,
    recv_sem,
    base_send,
    base_recv,
    row_send,
    row_recv,
    own_sem,
    relay_send,
    relay_recv,
    raw_sem,
    turned_sem,
):
    count = lax.axis_size("mp")
    me = lax.axis_index("mp")
    section = lax.axis_index("section")
    peers = column_peers()
    depth_count, tokens, local = current_out.shape
    chunk_rows = ids_ref.shape[2]
    padded = chunk_rows // CHUNK
    half = tokens // 2
    emb = 16
    block = min(256, local)
    groups = lax.axis_size("dp")
    group = lax.axis_index("dp")
    others = [lax.rem(group + j, groups) for j in range(1, groups)]
    relayed = groups == 4
    beside = group + 1 - 2 * lax.rem(group, 2)
    across = lax.rem(group + 2, 4)
    far = 3 - group
    near = [beside, across] if relayed else others
    origin = near if relayed else others[::-1]
    greet(
        [{"mp": peer} for peer in peers]
        + [{"section": 1 - section}]
        + [{"dp": other} for other in others]
    )

    def relay_rows(depth, way, slot):
        pieces = pl.ds(way * (count // 2), count // 2)
        return remote(
            features_all.at[depth, section, slot, pieces],
            features_all.at[depth, section, slot, pieces],
            relay_send.at[depth, way],
            relay_recv.at[depth, way],
            {"dp": across if way == 0 else beside},
        )

    def pass_rows(depth):
        for j in range(len(near)):
            give_rows(depth, j, origin[j]).wait_recv()
        if relayed and depth + 1 < depth_count:
            for way in range(2):
                relay_rows(depth, way, beside if way == 0 else across).start()

    blocks = input_out.shape[2] // TURN
    units = 4 * blocks

    def fetch(unit, start):
        slot = lax.rem(unit, 2)
        d = lax.rem(unit, 2 * blocks) // blocks
        rows = pl.ds(pl.multiple_of(lax.rem(unit, blocks) * TURN, TURN), TURN)
        for which, source in enumerate((input_ref, state_ref)):

            @pl.when(unit // (2 * blocks) == which)
            def _():
                copy = pltpu.make_async_copy(source.at[d, rows], raw.at[slot], raw_sem.at[slot])
                copy.start() if start else copy.wait()

    def deliver(unit, start):
        slot = lax.rem(unit, 2)
        d = lax.rem(unit, 2 * blocks) // blocks
        rows = pl.ds(pl.multiple_of(lax.rem(unit, blocks) * TURN, TURN), TURN)
        for which, target in enumerate((input_out, state_out)):

            @pl.when(unit // (2 * blocks) == which)
            def _():
                copy = pltpu.make_async_copy(
                    turned.at[slot], target.at[d, :, rows], turned_sem.at[slot]
                )
                copy.start() if start else copy.wait()

    def turn_units(first, last):
        @pl.loop(first, last)
        def _(unit):
            slot = lax.rem(unit, 2)
            fetch(unit, False)

            @pl.when(unit + 1 < units)
            def _():
                fetch(unit + 1, True)

            @pl.when(unit >= 2)
            def _():
                deliver(unit - 2, False)

            for g in range(4):
                turned[slot, g] = raw[slot, :, g, :]
            deliver(unit, True)

    fetch(0, True)

    def own_rows(depth):
        return pltpu.make_async_copy(
            features.at[depth], features_all.at[depth, section, group], own_sem.at[depth]
        )

    def give_rows(depth, j, slot):
        return remote(
            features.at[depth],
            features_all.at[depth, section, slot],
            row_send.at[depth, j],
            row_recv.at[depth, j],
            {"dp": near[j]},
        )

    def send(depth, part, rows, start):
        for j, peer in enumerate(peers):
            copy = remote(
                features.at[depth, me, rows],
                features.at[depth, me, rows],
                send_sem.at[depth, part, j],
                recv_sem.at[depth, part, me],
                {"mp": peer},
            )
            if start:
                copy.start()
            else:
                copy.wait_send()

    def receive(depth, part):
        rows = pl.ds(part * half, half)
        for j, peer in enumerate(peers):
            remote(
                features.at[depth, peer, rows],
                features.at[depth, peer, rows],
                send_sem.at[depth, part, j],
                recv_sem.at[depth, part, peer],
                {"mp": peer},
            ).wait_recv()

    lane_group = lax.broadcasted_iota(jnp.int32, (chunk_rows, 128), 1) // emb

    def pool_chunk(c):
        hot = one_hot_columns(ids_ref[c], table_ref.shape[0])
        embedded = lax.dot_general(
            hot, table_ref[...], (((0,), (0,)), ((), ())), preferred_element_type=F32
        )
        taps = embedded + flags_ref[...]
        for offset in range(1, TAPS):
            rolled = pltpu.roll(embedded, chunk_rows - offset, 0)
            taps = jnp.where(lane_group == offset, rolled, taps)
        taps = taps.astype(BF16)
        taps_out[c] = taps
        rows = pl.ds(pl.multiple_of(c * CHUNK, CHUNK), CHUNK)
        for start in range(0, local, block):
            cols = slice(start, start + block)
            scores = jnp.dot(taps, masked_ref[:, cols], preferred_element_type=F32)
            scores = scores.reshape(CHUNK, padded, block)
            top = jnp.max(scores, axis=1, keepdims=True)
            total = jnp.sum(jnp.exp(scores - top), axis=1, keepdims=True)
            peak = top + jnp.log(total)
            peak_out[rows, :, cols] = peak
            pooled = jnp.sum(peak, axis=1) - log_positions[:, cols]
            pooled_out[rows, cols] = pooled
            current = jnp.maximum(pooled, 0.0) + jnp.log1p(jnp.exp(-jnp.abs(pooled)))
            current_out[0, rows, cols] = current
            features[0, me, rows, cols] = current.astype(BF16)
        return rows

    for part in range(2):

        @pl.loop(0, half // CHUNK)
        def _(i):
            rows = pool_chunk(part * (half // CHUNK) + i)
            send(0, part, rows, True)

    for depth in range(depth_count):
        for part in range(2):
            rows = pl.ds(part * half, half)
            receive(depth, part)
            if part == 1:
                own_rows(depth).start()
                for j in range(len(near)):
                    give_rows(depth, j, group).start()
            mixed = []
            for g in range(2):
                total = jnp.broadcast_to(b_high[depth, g : g + 1, :], (half, local))
                for p in range(count):
                    total = total + jnp.dot(
                        features[depth, p, rows, :],
                        w_high[depth, g, p * local : (p + 1) * local, :],
                        preferred_element_type=F32,
                    )
                mixed.append(total)
            transform = mixed[0]
            gate = jax.nn.sigmoid(mixed[1])
            transform_out[depth, rows, :] = transform
            gate_out[depth, rows, :] = gate
            current = gate * current_out[depth, rows, :] + (1.0 - gate) * (
                transform * jax.nn.sigmoid(transform)
            )
            if depth + 1 < depth_count:
                current_out[depth + 1, rows, :] = current
            features[depth + 1, me, rows, :] = current.astype(BF16)
            send(depth + 1, part, rows, True)
        if depth >= 1:
            pass_rows(depth - 1)
        turn_units(depth * units * 3 // (4 * depth_count), (depth + 1) * units * 3 // (4 * depth_count))

    def give():
        return remote(
            base_out.at[section],
            base_out.at[section],
            base_send,
            base_recv,
            {"section": 1 - section},
        )

    for part in range(2):
        rows = pl.ds(part * half, half)
        receive(depth_count, part)
        total = jnp.broadcast_to(b_proj[...], (half, w_proj.shape[1]))
        for p in range(count):
            total = total + jnp.dot(
                features[depth_count, p, rows, :],
                w_proj[p * local : (p + 1) * local, :],
                preferred_element_type=F32,
            )
        base_out[section, rows, :] = total
    give().start()
    turn_units(units * 3 // 4, units)
    pass_rows(depth_count - 1)
    for depth in range(depth_count + 1):
        for part in range(2):
            send(depth, part, pl.ds(part * half, half), False)
    give().wait_send()
    remote(
        base_out.at[1 - section],
        base_out.at[1 - section],
        base_send,
        base_recv,
        {"section": 1 - section},
    ).wait_recv()
    for depth in range(depth_count):
        own_rows(depth).wait()
        for j in range(len(near)):
            give_rows(depth, j, group).wait_send()
        if relayed and depth + 1 < depth_count:
            for way in range(2):
                relay_rows(depth, way, beside if way == 0 else across).wait_send()
                relay_rows(depth, way, far).wait_recv()
    for unit in range(units - 2, units):
        deliver(unit, False)


def cnn_forward(ids, weights, lstm_input, lstm_state):
    table, masked, log_positions, w_high, b_high, w_proj, b_proj = weights
    chunks, _, chunk_rows = ids.shape
    tokens = chunks * CHUNK
    depth_count, _, total, local = w_high.shape
    count = lax.axis_size("mp")
    groups = lax.axis_size("dp")
    directions, in_width, gate_blocks, cell_columns = lstm_input.shape
    padded = chunk_rows // CHUNK
    position = jnp.tile(jnp.arange(padded, dtype=jnp.int32), CHUNK)[:, None]
    lane = jnp.arange(128, dtype=jnp.int32)[None, :]
    width = lane - 16 * TAPS
    flags = (lane == 16 * TAPS) | ((width >= 1) & (width <= TAPS) & (position > PER_TOKEN - width))
    dma = pltpu.SemaphoreType.DMA
    return pl.pallas_call(
        cnn_forward_kernel,
        out_shape=(
            jax.ShapeDtypeStruct((2, tokens, w_proj.shape[1]), F32),
            jax.ShapeDtypeStruct((chunks, chunk_rows, 128), BF16),
            jax.ShapeDtypeStruct((tokens, 1, local), F32),
            jax.ShapeDtypeStruct((tokens, local), F32),
            jax.ShapeDtypeStruct((depth_count + 1, count, tokens, local), BF16),
            jax.ShapeDtypeStruct((depth_count, tokens, local), F32),
            jax.ShapeDtypeStruct((depth_count, tokens, local), F32),
            jax.ShapeDtypeStruct((depth_count, tokens, local), F32),
            jax.ShapeDtypeStruct((depth_count, 2, groups, count, tokens, local), BF16),
            jax.ShapeDtypeStruct((directions, gate_blocks, in_width, cell_columns), BF16),
            jax.ShapeDtypeStruct((directions, gate_blocks, in_width, cell_columns), BF16),
        ),
        in_specs=[VMEM_SPEC] * 9 + [ANY_SPEC] * 2,
        out_specs=(*[VMEM_SPEC] * 8, *[ANY_SPEC] * 3),
        scratch_shapes=[
            pltpu.VMEM((2, TURN, gate_blocks, cell_columns), BF16),
            pltpu.VMEM((2, gate_blocks, TURN, cell_columns), BF16),
            dma((depth_count + 1, 2, count - 1)),
            dma((depth_count + 1, 2, count)),
            dma,
            dma,
            dma((depth_count, groups - 1)),
            dma((depth_count, groups - 1)),
            dma((depth_count,)),
            dma((depth_count, 2)),
            dma((depth_count, 2)),
            dma((2,)),
            dma((2,)),
        ],
        compiler_params=pltpu.CompilerParams(
            collective_id=1, has_side_effects=True, vmem_limit_bytes=VMEM_LIMIT
        ),
        name="cnn_forward",
    )(
        ids,
        table,
        flags.astype(F32),
        masked,
        log_positions,
        w_high,
        b_high,
        w_proj,
        b_proj,
        lstm_input,
        lstm_state,
    )


def cnn_backward_kernel(
    base_ref,
    own_ref,
    w_high,
    current_ref,
    transform_ref,
    gate_ref,
    peak_ref,
    pooled_ref,
    taps_ref,
    masked_ref,
    masked_t,
    ids_ref,
    gates_in,
    projected_in,
    x_in,
    state_all,
    gates_all,
    projected_all,
    x_all,
    base_full,
    mixed_all,
    late_first,
    late_second,
    conv_out,
    table_out,
    mixed_out,
    late_buf,
    base_all,
    table_sum,
    table_all,
    grad_current,
    outgoing,
    incoming,
    base_send,
    base_recv,
    sum_send,
    sum_recv,
    own_sem,
    relay_send,
    relay_recv,
    lift_send,
    lift_recv,
    row_send,
    row_recv,
    full_sem,
    share_send,
    share_recv,
    table_send,
    table_recv,
    mixed_sem,
    mixed_send,
    mixed_recv,
    mixed_share,
    mixed_shared,
    late_sem,
):
    count = lax.axis_size("mp")
    me = lax.axis_index("mp")
    section = lax.axis_index("section")
    groups = lax.axis_size("dp")
    group = lax.axis_index("dp")
    peers = column_peers()
    depth_count, tokens, local = current_ref.shape
    steps = x_all.shape[2]
    chunks, chunk_rows, _ = taps_ref.shape
    padded = chunk_rows // CHUNK
    emb = 16
    vocabulary = -(-CHARS // 8) * 8
    relayed = groups == 4
    beside = group + 1 - 2 * lax.rem(group, 2)
    across = lax.rem(group + 2, 4)
    far = 3 - group
    greet(
        [{"mp": peer} for peer in peers]
        + [{"section": 1 - section, "mp": peer} for peer in [*peers, me]]
        + [{"dp": lax.rem(group + j, groups)} for j in range(1, groups)]
    )

    def lift():
        return remote(
            state_all.at[:, :, pl.ds(1, steps)],
            x_all,
            lift_send,
            lift_recv,
            {"section": 1 - section},
        )

    def relay(kind, buffer, d, slot):
        early = pl.ds(0, steps if kind == 0 else steps // RELAY_SHARE)
        return remote(
            buffer.at[d, slot, early],
            buffer.at[d, slot, early],
            relay_send.at[kind, d],
            relay_recv.at[kind, d],
            {"dp": across if d == 0 else beside},
        )

    buffers = ((0, projected_all), (1, gates_all))

    early = steps // RELAY_SHARE
    late = pl.ds(early, steps - early)
    late_loads = [
        pltpu.make_async_copy(gates_all.at[d, slot, late], late_buf.at[d], late_sem.at[d])
        for d, slot in ((0, beside), (1, across))
    ]
    late_stores = [
        pltpu.make_async_copy(late_buf.at[d], target, late_sem.at[d])
        for d, target in ((0, late_first), (1, late_second))
    ]
    if relayed:
        for copy in late_loads:
            copy.start()

    def spread_base(half, target_section, peer, j):
        return remote(
            base_ref.at[half],
            base_all.at[me],
            base_send.at[half, j],
            base_recv.at[me],
            {"section": target_section, "mp": peer},
        )

    everyone = [*peers, me]

    @pl.when(section == 0)
    def _():
        for j, peer in enumerate(peers):
            spread_base(0, 0, peer, j).start()
        for j, peer in enumerate(everyone):
            spread_base(1, 1, peer, j).start()
        lift().start()
        own = pltpu.make_async_copy(base_ref.at[0], base_all.at[me], own_sem)
        own.start()
        own.wait()

    def base_arrival(source):
        return remote(
            base_ref.at[0],
            base_all.at[source],
            base_send.at[0, 0],
            base_recv.at[source],
            {"section": 1 - section},
        )

    for peer in peers:
        base_arrival(peer).wait_recv()

    @pl.when(section == 1)
    def _():
        base_arrival(me).wait_recv()

    others = [lax.rem(group + j, groups) for j in range(1, groups)]
    keep = pltpu.make_async_copy(base_all, base_full.at[section, group], full_sem)
    keep.start()

    def base_row(j, slot):
        return remote(
            base_all,
            base_full.at[section, slot],
            row_send.at[j],
            row_recv.at[j],
            {"dp": others[j]},
        )

    def share_base(owner):
        return remote(
            base_full.at[owner],
            base_full.at[owner],
            share_send,
            share_recv,
            {"section": 1 - section},
        )

    for j in range(groups - 1):
        base_row(j, group).start()

    def keep_mixed(depth):
        return pltpu.make_async_copy(
            mixed_out.at[depth], mixed_all.at[depth, section, group], mixed_sem.at[depth]
        )

    def mixed_row(depth, j, slot):
        return remote(
            mixed_out.at[depth],
            mixed_all.at[depth, section, slot],
            mixed_send.at[depth, j],
            mixed_recv.at[depth, j],
            {"dp": others[j]},
        )

    def share_mixed(depth, owner):
        return remote(
            mixed_all.at[depth, owner],
            mixed_all.at[depth, owner],
            mixed_share.at[depth],
            mixed_shared.at[depth],
            {"section": 1 - section},
        )

    def collect_mixed(depth):
        keep_mixed(depth).wait()
        for j in range(groups - 1):
            mixed_row(depth, j, others[groups - 2 - j]).wait_recv()
        share_mixed(depth, section).start()

    wide = base_all.shape[2]
    total = jnp.zeros((tokens, local), F32)
    for p in range(count):
        total = total + jnp.dot(
            base_all[p], own_ref[p * wide : (p + 1) * wide, :], preferred_element_type=F32
        )
    grad_current[...] = total

    def send_sum(depth, peer, j):
        return remote(
            outgoing.at[depth, j],
            incoming.at[depth, me],
            sum_send.at[depth, j],
            sum_recv.at[depth, me],
            {"mp": peer},
        )

    def back(depth, owner):
        rows = pl.ds(pl.multiple_of(owner * local, local), local)
        parts = [
            lax.dot_general(
                mixed_out[depth, :, g * local : (g + 1) * local],
                w_high[depth, g, rows, :],
                (((1,), (1,)), ((), ())),
                preferred_element_type=F32,
            )
            for g in range(2)
        ]
        return parts[0] + parts[1]

    for depth in range(depth_count - 1, -1, -1):
        transform = transform_ref[depth]
        gate = gate_ref[depth]
        grad = grad_current[...]
        slope = jax.nn.sigmoid(transform)
        mixed_out[depth, :, :local] = (
            grad * (1.0 - gate) * slope * (1.0 + transform * (1.0 - slope))
        ).astype(BF16)
        mixed_out[depth, :, local:] = (
            grad * (current_ref[depth] - transform * slope) * gate * (1.0 - gate)
        ).astype(BF16)
        keep_mixed(depth).start()
        for j in range(groups - 1):
            mixed_row(depth, j, group).start()
        if relayed and depth == depth_count - 1:
            for kind, buffer in buffers:
                for d in range(2):
                    relay(kind, buffer, d, beside if d == 0 else across).start()
        for j, peer in enumerate(peers):
            outgoing[depth, j] = back(depth, peer).astype(BF16)
            send_sum(depth, peer, j).start()
        total = grad * gate + back(depth, me)
        for j, peer in enumerate(peers):
            remote(
                outgoing.at[depth, j],
                incoming.at[depth, peer],
                sum_send.at[depth, j],
                sum_recv.at[depth, peer],
                {"mp": peer},
            ).wait_recv()
            total = total + incoming[depth, peer].astype(F32)
        grad_current[...] = total

    if relayed:
        for load, store in zip(late_loads, late_stores):
            load.wait()
            store.start()
    for depth in range(depth_count - 1, 0, -1):
        collect_mixed(depth)
    grad_current[...] = grad_current[...] * jax.nn.sigmoid(pooled_ref[...])
    conv_out[...] = jnp.zeros_like(conv_out)
    table_sum[...] = jnp.zeros_like(table_sum)
    lane_group = lax.broadcasted_iota(jnp.int32, (chunk_rows, 128), 1) // emb

    @pl.loop(0, chunks)
    def _(c):
        rows = pl.ds(pl.multiple_of(c * CHUNK, CHUNK), CHUNK)
        taps = taps_ref[c]
        scores = jnp.dot(taps, masked_ref[...], preferred_element_type=F32)
        scores = scores.reshape(CHUNK, padded, local)
        share = jnp.exp(scores - peak_ref[rows])
        grads = share * grad_current[rows, :][:, None, :]
        grads = grads.reshape(chunk_rows, local).astype(BF16)
        conv_out[...] += lax.dot_general(
            taps, grads, (((0,), (0,)), ((), ())), preferred_element_type=F32
        )
        back_taps = jnp.dot(grads, masked_t[...], preferred_element_type=F32)
        moved = back_taps
        for offset in range(1, TAPS):
            moved = jnp.where(lane_group == offset, pltpu.roll(back_taps, offset, 0), moved)
        hot = one_hot_columns(ids_ref[c], vocabulary)
        table_sum[:vocabulary, :] += jnp.dot(
            hot, moved.astype(BF16), preferred_element_type=F32
        )

    columns = table_sum[...].T
    folded = columns[:emb]
    for offset in range(1, TAPS):
        folded = folded + columns[offset * emb : (offset + 1) * emb]
    table_all[me] = folded

    def table_copy(j, slot):
        return remote(
            table_all.at[slot],
            table_all.at[slot],
            table_send.at[j],
            table_recv.at[slot],
            {"mp": peers[j]},
        )

    for j in range(count - 1):
        table_copy(j, me).start()

    for j in range(count - 1):
        table_copy(j, peers[j]).wait_recv()
    folded = table_all[0]
    for p in range(1, count):
        folded = folded + table_all[p]
    table_out[...] = folded
    for j in range(count - 1):
        table_copy(j, me).wait_send()
    keep.wait()
    for j in range(groups - 1):
        base_row(j, others[groups - 2 - j]).wait_recv()
    share_base(section).start()
    collect_mixed(0)
    for j in range(groups - 1):
        base_row(j, group).wait_send()
        for depth in range(depth_count):
            mixed_row(depth, j, group).wait_send()
    for depth in range(depth_count):
        for j, peer in enumerate(peers):
            send_sum(depth, peer, j).wait_send()

    @pl.when(section == 0)
    def _():
        for j, peer in enumerate(peers):
            spread_base(0, 0, peer, j).wait_send()
        for j, peer in enumerate(everyone):
            spread_base(1, 1, peer, j).wait_send()
        lift().wait_send()

    @pl.when(section == 1)
    def _():
        lift().wait_recv()

    if relayed:
        for kind, buffer in buffers:
            for d in range(2):
                relay(kind, buffer, d, beside if d == 0 else across).wait_send()
                relay(kind, buffer, d, far).wait_recv()
        for copy in late_stores:
            copy.wait()

    share_base(section).wait_send()
    share_base(1 - section).wait_recv()
    for depth in range(depth_count):
        share_mixed(depth, section).wait_send()
        share_mixed(depth, 1 - section).wait_recv()


def cnn_backward(base_shards, saved, weights, rows_all):
    own_rows, w_high, masked, ids = weights
    taps, peak, pooled, current, transform, gate = saved
    gates_all, projected_all, x_all, state_all = rows_all
    depth_count, tokens, local = current.shape
    count = lax.axis_size("mp")
    groups = lax.axis_size("dp")
    vocabulary = -(-CHARS // 128) * 128
    steps = gates_all.shape[2]
    late = steps - steps // RELAY_SHARE
    dma = pltpu.SemaphoreType.DMA
    return pl.pallas_call(
        cnn_backward_kernel,
        out_shape=(
            jax.ShapeDtypeStruct(gates_all.shape, BF16),
            jax.ShapeDtypeStruct(projected_all.shape, BF16),
            jax.ShapeDtypeStruct(x_all.shape, BF16),
            jax.ShapeDtypeStruct((2, groups, count, tokens, base_shards.shape[2]), BF16),
            jax.ShapeDtypeStruct((depth_count, 2, groups, tokens, 2 * local), BF16),
            jax.ShapeDtypeStruct((late, *gates_all.shape[3:]), BF16),
            jax.ShapeDtypeStruct((late, *gates_all.shape[3:]), BF16),
            jax.ShapeDtypeStruct((128, local), F32),
            jax.ShapeDtypeStruct((16, vocabulary), F32),
        ),
        in_specs=[VMEM_SPEC] * 12 + [ANY_SPEC] * 4,
        out_specs=(*[ANY_SPEC] * 7, *[VMEM_SPEC] * 2),
        input_output_aliases={12: 0, 13: 1, 14: 2},
        scratch_shapes=[
            pltpu.VMEM((depth_count, tokens, 2 * local), BF16),
            pltpu.VMEM((2, late, *gates_all.shape[3:]), BF16),
            pltpu.VMEM((count, tokens, base_shards.shape[2]), BF16),
            pltpu.VMEM((vocabulary, 128), F32),
            pltpu.VMEM((count, 16, vocabulary), F32),
            pltpu.VMEM((tokens, local), F32),
            pltpu.VMEM((depth_count, count - 1, tokens, local), BF16),
            pltpu.VMEM((depth_count, count, tokens, local), BF16),
            dma((2, count)),
            dma((count,)),
            dma((depth_count, count - 1)),
            dma((depth_count, count)),
            dma,
            dma((2, 2)),
            dma((2, 2)),
            dma,
            dma,
            dma((groups - 1,)),
            dma((groups - 1,)),
            dma,
            dma,
            dma,
            dma((count - 1,)),
            dma((count,)),
            dma((depth_count,)),
            dma((depth_count, groups - 1)),
            dma((depth_count, groups - 1)),
            dma((depth_count,)),
            dma((depth_count,)),
            dma((2,)),
        ],
        compiler_params=pltpu.CompilerParams(
            collective_id=2, has_side_effects=True, vmem_limit_bytes=VMEM_LIMIT
        ),
        name="cnn_backward",
    )(
        base_shards,
        own_rows,
        w_high,
        current,
        transform,
        gate,
        peak,
        pooled,
        taps,
        masked,
        jnp.pad(masked[: 16 * TAPS], ((0, 128 - 16 * TAPS), (0, 0))).T,
        ids,
        gates_all,
        projected_all,
        x_all,
        state_all,
    )


def recurrence_kernel(
    base_ref,
    live_ref,
    top_ref,
    w_in,
    w_state,
    bias_ref,
    proj_ref,
    features_in,
    x_all,
    state_all,
    hidden_all,
    gates_all,
    projected_all,
    base_out,
    features_all,
    x_out,
    state_out,
    hidden_out,
    projected_out,
    acts,
    cells,
    clips,
    pre,
    grad_cell,
    parts,
    back_parts,
    above,
    gate_buf,
    base_sem,
    send_sem,
    recv_sem,
    back_send,
    back_recv,
    x_send,
    x_recv,
    above_send,
    above_recv,
    gate_sem,
    gate_send,
    own_sem,
    row_send,
    row_recv,
    w_in_t,
    w_state_t,
    proj_t,
    input_parts,
    input_sums,
    input_send,
    input_recv,
    base_sum,
    share_send,
    share_recv,
    relay_send,
    relay_recv,
):
    count = lax.axis_size("mp")
    me = lax.axis_index("mp")
    section = lax.axis_index("section")
    steps = x_out.shape[1]
    cell_count = proj_ref.shape[1]
    chunk = min(256, cell_count)
    peers = [lax.rem(me + j, count) for j in range(1, count)]
    groups = lax.axis_size("dp")
    group = lax.axis_index("dp")
    others = [lax.rem(group + j, groups) for j in range(1, groups)]
    relayed = groups == 4
    beside = group + 1 - 2 * lax.rem(group, 2)
    across = lax.rem(group + 2, 4)
    near = [beside, across] if relayed else others

    barrier = pltpu.get_barrier_semaphore()
    for peer in peers:
        pl.semaphore_signal(barrier, inc=1, device_id={"mp": peer}, device_id_type=MESH)
    pl.semaphore_signal(barrier, inc=1, device_id={"section": 1 - section}, device_id_type=MESH)
    for other in others:
        pl.semaphore_signal(barrier, inc=1, device_id={"dp": other}, device_id_type=MESH)
    pl.semaphore_wait(barrier, count + groups - 1)

    def share_features(owner):
        return remote(
            features_all.at[:, owner],
            features_all.at[:, owner],
            share_send,
            share_recv,
            {"section": 1 - section},
        )

    pieces = features_all.shape[3]

    def relay_features(way, slot):
        half = pl.ds(way * (pieces // 2), pieces // 2)
        depth = features_all.shape[0] - 1
        return remote(
            features_all.at[depth, section, slot, half],
            features_all.at[depth, section, slot, half],
            relay_send.at[way],
            relay_recv.at[way],
            {"dp": across if way == 0 else beside},
        )

    if relayed:
        for way in range(2):
            relay_features(way, beside if way == 0 else across).start()

    def wide(values, width):
        return jnp.concatenate([values] * (width // values.shape[1]), axis=1)

    def copy_part(buffer, send, recv, d, parity, source, j, target):
        return pltpu.make_async_remote_copy(
            src_ref=buffer.at[d, parity, source],
            dst_ref=buffer.at[d, parity, source],
            send_sem=send.at[d, parity, j],
            recv_sem=recv.at[d, parity, source],
            device_id={"mp": target},
            device_id_type=MESH,
        )

    ordered = peers
    if count == 4:
        ordered = [3 - me, lax.rem(me + 2, 4), me + 1 - 2 * lax.rem(me, 2)]

    def exchange_start(buffer, send, recv, d, parity, value):
        buffer[d, parity, me] = value.astype(BF16)
        for j, peer in enumerate(ordered):
            copy_part(buffer, send, recv, d, parity, me, j, peer).start()

    def exchange_wait(buffer, send, recv, d, parity):
        for j, peer in enumerate(ordered):
            copy_part(buffer, send, recv, d, parity, peer, j, peer).wait_recv()
        total = buffer[d, parity, 0].astype(F32)
        for source in range(1, count):
            total = total + buffer[d, parity, source].astype(F32)
        for j, peer in enumerate(ordered):
            copy_part(buffer, send, recv, d, parity, me, j, peer).wait_send()
        return total

    def pass_up(d, k):
        return pltpu.make_async_remote_copy(
            src_ref=state_out.at[d, k + 1],
            dst_ref=x_out.at[d, k],
            send_sem=x_send.at[d],
            recv_sem=x_recv.at[d, k],
            device_id={"section": 1 - section},
            device_id_type=MESH,
        )

    def pass_down(d, k):
        return pltpu.make_async_remote_copy(
            src_ref=above.at[d, k],
            dst_ref=above.at[d, k],
            send_sem=above_send.at[d],
            recv_sem=above_recv.at[d, k],
            device_id={"section": 1 - section},
            device_id_type=MESH,
        )

    def gates_copy(d, k, slot):
        return pltpu.make_async_copy(
            gate_buf.at[d, slot], gates_all.at[d, group, k], gate_sem.at[d, slot]
        )

    def gates_row(d, k, slot, j, other):
        return pltpu.make_async_remote_copy(
            src_ref=gate_buf.at[d, slot],
            dst_ref=gates_all.at[d, group, k],
            send_sem=gate_send.at[d, slot, j],
            recv_sem=row_recv.at[0, j],
            device_id={"dp": other},
            device_id_type=MESH,
        )

    def row(kind, source, target, j, other):
        return pltpu.make_async_remote_copy(
            src_ref=source,
            dst_ref=target,
            send_sem=row_send.at[kind, j],
            recv_sem=row_recv.at[kind, j],
            device_id={"dp": other},
            device_id_type=MESH,
        )

    def from_peer(j, targets):
        back = len(targets) - 1 - j
        return targets[j] if relayed and len(targets) == 2 else targets[back]

    def time_of(d, k):
        return k if d == 0 else steps - 1 - k

    @pl.when(section == 0)
    def _():
        part_rows = base_ref.shape[1] // steps

        @pl.loop(0, steps)
        def _(t):
            at = pl.ds(pl.multiple_of(t * part_rows, part_rows), part_rows)
            x = jnp.concatenate([base_ref[0, at, :], base_ref[1, at, :]], axis=0).astype(BF16)
            for d in range(2):
                x_out[d, time_of(d, t)] = x

        for j, other in enumerate(others):
            row(1, x_out, x_all.at[:, group], j, other).start()

    for d in range(2):
        state_out[d, 0] = jnp.zeros(state_out.shape[2:], BF16)
        cells[d, 0] = jnp.zeros(cells.shape[2:], F32)
        grad_cell[d] = jnp.zeros(grad_cell.shape[1:], F32)

    def input_part(d, k):
        @pl.when(section == 1)
        def _():
            pass_up(d, k).wait_recv()

        x = x_out[d, k]
        for block in range(4):
            for start in range(0, cell_count, chunk):
                cols = slice(block * cell_count + start, block * cell_count + start + chunk)
                pre[d, :, cols] = bias_ref[d, :, cols] + jnp.dot(
                    x, w_in[d, block, :, start : start + chunk], preferred_element_type=F32
                )

    def turn_weights(unit):
        per_block = cell_count // chunk
        block = unit // per_block
        cols = pl.ds(pl.multiple_of(lax.rem(unit, per_block) * chunk, chunk), chunk)
        rows_t = pl.ds(pl.multiple_of(unit * chunk, chunk), chunk)
        for d in range(2):
            w_in_t[d, rows_t, :] = w_in[d, block, :, cols].T
            w_state_t[d, rows_t, :] = w_state[d, block, :, cols].T

    def turn_proj(unit):
        cols = pl.ds(pl.multiple_of(unit * 128, 128), 128)
        for d in range(2):
            proj_t[d, :, cols] = proj_ref[d, cols, :].T

    def forward_cells(d, k):
        state = state_out[d, k]
        live = live_ref[time_of(d, k)]
        for start in range(0, cell_count, chunk):
            raw = []
            for block in range(4):
                cols = slice(block * cell_count + start, block * cell_count + start + chunk)
                raw.append(
                    pre[d, :, cols]
                    + jnp.dot(
                        state, w_state[d, block, :, start : start + chunk], preferred_element_type=F32
                    )
                )
            own = slice(start, start + chunk)
            in_gate = jax.nn.sigmoid(raw[0])
            forget = jax.nn.sigmoid(raw[1])
            memory = jnp.tanh(raw[2])
            out_gate = jax.nn.sigmoid(raw[3])
            for block, value in enumerate((in_gate, forget, memory, out_gate)):
                acts[d, k, block, :, own] = value
            cell_new = soft_clip(in_gate * memory + forget * cells[d, k, :, own])
            cells[d, k + 1, :, own] = wide(live, chunk) * cell_new
            hidden_out[d, k, :, own] = (out_gate * jnp.tanh(cell_new)).astype(BF16)
        part = jnp.dot(hidden_out[d, k], proj_ref[d], preferred_element_type=F32)
        exchange_start(parts, send_sem, recv_sem, d, lax.rem(k, 2), part)
        for j, other in enumerate(others):
            row(2, hidden_out.at[d, k], hidden_all.at[d, group, k], j, other).start()

    def forward_state(d, k):
        total = exchange_wait(parts, send_sem, recv_sem, d, lax.rem(k, 2))
        clip = jnp.tanh(total / 3.0)
        clips[d, k] = clip
        live = wide(live_ref[time_of(d, k)], clip.shape[1])
        state_out[d, k + 1] = (live * 3.0 * clip).astype(BF16)

        @pl.when(section == 0)
        def _():
            @pl.when(k > 0)
            def _():
                pass_up(d, k - 1).wait_send()

            pass_up(d, k).start()

        for j, other in enumerate(others):
            row(3, state_out.at[d, k + 1], state_all.at[d, group, k + 1], j, other).start()

    units = 4 * cell_count // chunk
    for d in range(2):
        input_part(d, 0)
    for d in range(2):
        forward_cells(d, 0)
    for d in range(2):
        input_part(d, 1)

    @pl.loop(1, steps)
    def _(k):
        for d in range(2):
            forward_state(d, k - 1)
            forward_cells(d, k)

        @pl.when(k + 1 < steps)
        def _():
            for d in range(2):
                input_part(d, k + 1)

        @pl.when(k <= units)
        def _():
            turn_weights(k - 1)

        @pl.when(k <= cell_count // 128)
        def _():
            turn_proj(k - 1)

    for unit in range(steps - 1, units):
        turn_weights(unit)
    for d in range(2):
        forward_state(d, steps - 1)
    if relayed:
        for way in range(2):
            relay_features(way, beside if way == 0 else across).wait_send()
            relay_features(way, 3 - group).wait_recv()
    share_features(section).start()

    @pl.when(section == 0)
    def _():
        for d in range(2):
            pass_up(d, steps - 1).wait_send()

    def back_wait(d, parity):
        return exchange_wait(back_parts, back_send, back_recv, d, parity)

    def back_start(d, parity, value):
        exchange_start(back_parts, back_send, back_recv, d, parity, value)

    def backward_cells(d, k, total):
        slot = lax.rem(k, SLOTS)
        live = live_ref[time_of(d, k)]
        clip = clips[d, k]
        grad_out = wide(live, clip.shape[1]) * (total + top_ref[d, time_of(d, k)].astype(F32))
        grad_projected = (grad_out * (1.0 - clip * clip)).astype(BF16)
        projected_out[d, k] = grad_projected

        for j, other in enumerate(near):
            row(
                4, projected_out.at[d, k], projected_all.at[d, group, k], j, other
            ).start()

        @pl.when(k < steps - SLOTS)
        def _():
            gates_copy(d, k + SLOTS, slot).wait()
            for j, other in enumerate(near):
                gates_row(d, k + SLOTS, slot, j, other).wait_send()

        for start in range(0, cell_count, chunk):
            own = slice(start, start + chunk)
            grad_hidden = jnp.dot(grad_projected, proj_t[d, :, own], preferred_element_type=F32)
            in_gate, forget, memory, out_gate = [acts[d, k, block, :, own] for block in range(4)]
            cell = cells[d, k, :, own]
            clip_raw = jnp.tanh((in_gate * memory + forget * cell) / 3.0)
            tanh_cell = jnp.tanh(3.0 * clip_raw)
            grad_new = wide(live, chunk) * grad_cell[d, :, own] + grad_hidden * out_gate * (
                1.0 - tanh_cell * tanh_cell
            )
            grad_raw = grad_new * (1.0 - clip_raw * clip_raw)
            grad_cell[d, :, own] = grad_raw * forget
            grads = (
                grad_raw * memory * in_gate * (1.0 - in_gate),
                grad_raw * cell * forget * (1.0 - forget),
                grad_raw * in_gate * (1.0 - memory * memory),
                grad_hidden * tanh_cell * out_gate * (1.0 - out_gate),
            )
            for block, value in enumerate(grads):
                cols = slice(block * cell_count + start, block * cell_count + start + chunk)
                gate_buf[d, slot, :, cols] = value.astype(BF16)
        gates_copy(d, k, slot).start()

    def gates_send(d, k):
        for j, other in enumerate(near):
            gates_row(d, k, lax.rem(k, SLOTS), j, other).start()

    def backward_state(d, k):
        @pl.when(k > 0)
        def _():
            back = jnp.dot(gate_buf[d, lax.rem(k, SLOTS)], w_state_t[d], preferred_element_type=F32)
            pre[d, :, : back.shape[1]] = back

            @pl.when(section == 0)
            def _():
                pass_down(d, k - 1).wait_recv()
                pre[d, :, : back.shape[1]] = back + above[d, k - 1]

            back_start(d, lax.rem(k - 1, 2), pre[d, :, : back.shape[1]])

    share = base_out.shape[2]

    def input_copy(source, target, j, peer):
        return remote(source, target, input_send.at[j], input_recv.at[j], {"mp": peer})

    def backward_input(d, k):
        gates_send(d, k)
        part = jnp.dot(gate_buf[d, lax.rem(k, SLOTS)], w_in_t[d], preferred_element_type=F32)

        @pl.when(section == 1)
        def _():
            above[d, k] = part

            @pl.when(k < steps - 1)
            def _():
                pass_down(d, k + 1).wait_send()

            pass_down(d, k).start()

        @pl.when(section == 0)
        def _():
            for p in range(count):
                input_parts[d, k, p] = part[:, p * share : (p + 1) * share].astype(BF16)
            for j, peer in enumerate(peers):
                input_copy(input_parts.at[d, k, peer], input_sums.at[d, k, me], j, peer).start()

    last = steps - 1

    @pl.when(section == 0)
    def _():
        for d in range(2):
            pass_down(d, last).wait_recv()
            back_start(d, lax.rem(last, 2), above[d, last])

    for d in range(2):

        @pl.when(section == 0)
        def _():
            pre[d, :, : clips.shape[3]] = back_wait(d, lax.rem(last, 2))

        @pl.when(section == 1)
        def _():
            pre[d, :, : clips.shape[3]] = jnp.zeros(clips.shape[2:], F32)

        backward_cells(d, last, pre[d, :, : clips.shape[3]])
        backward_state(d, last)
    for d in range(2):
        backward_input(d, last)

    @pl.loop(1, steps)
    def _(tick):
        k = last - tick
        for d in range(2):
            backward_cells(d, k, back_wait(d, lax.rem(k, 2)))
            backward_state(d, k)
        for d in range(2):
            backward_input(d, k)

    for d in range(2):
        for k in range(min(SLOTS, steps)):
            gates_copy(d, k, k % SLOTS).wait()
            for j, other in enumerate(near):
                gates_row(d, k, k % SLOTS, j, other).wait_send()

    @pl.when(section == 1)
    def _():
        for d in range(2):
            pass_down(d, 0).wait_send()

    own = [
        (hidden_out, hidden_all.at[:, group]),
        (state_out, state_all.at[:, group]),
        (projected_out, projected_all.at[:, group]),
    ]
    for other in others:
        own.append((state_out.at[:, 0], state_all.at[:, other, 0]))
    own = [
        pltpu.make_async_copy(source, target, own_sem.at[i])
        for i, (source, target) in enumerate(own)
    ]
    for copy in own:
        copy.start()

    rest = pl.ds(1, steps)
    for j, other in enumerate(others):
        source = from_peer(j, others)
        hidden_row = row(2, hidden_out, hidden_all.at[:, source], j, other)
        state_row = row(3, state_out.at[:, rest], state_all.at[:, source, rest], j, other)
        for copy in (hidden_row, state_row):
            copy.wait_send()
            copy.wait_recv()

    for copy in own:
        copy.wait()

    @pl.when(section == 0)
    def _():
        mine = pltpu.make_async_copy(x_out, x_all.at[:, group], base_sem)
        mine.start()
        for j, other in enumerate(others):
            copy = row(1, x_out, x_all.at[:, from_peer(j, others)], j, other)
            copy.wait_send()
            copy.wait_recv()
        mine.wait()

    @pl.when(section == 0)
    def _():
        for j, peer in enumerate(peers):
            source = peers[count - 2 - j]
            copy = input_copy(input_parts.at[:, :, peer], input_sums.at[:, :, source], j, peer)
            copy.wait_send()
            copy.wait_recv()
        rows_half = base_out.shape[1] // steps

        @pl.loop(0, steps)
        def _(t):
            total = input_parts[0, t, me].astype(F32) + input_parts[1, steps - 1 - t, me].astype(F32)
            for peer in peers:
                total = total + input_sums[0, t, peer].astype(F32)
                total = total + input_sums[1, steps - 1 - t, peer].astype(F32)
            at = pl.ds(pl.multiple_of(t * rows_half, rows_half), rows_half)
            for half in range(2):
                base_sum[half, at, :] = total[half * rows_half : (half + 1) * rows_half]

        base_out[...] = base_sum[...].astype(BF16)

    share_features(section).wait_send()
    share_features(1 - section).wait_recv()

    for j, other in enumerate(near):
        source = from_peer(j, near)
        pltpu.make_async_remote_copy(
            src_ref=gates_all.at[:, source],
            dst_ref=gates_all.at[:, source],
            send_sem=row_send.at[0, j],
            recv_sem=row_recv.at[0, j],
            device_id={"dp": other},
            device_id_type=MESH,
        ).wait_recv()
        projected_row = row(4, projected_out, projected_all.at[:, source], j, other)
        projected_row.wait_send()
        projected_row.wait_recv()


def recurrence(base_seq, live_seq, top_seq, layer_weights, features_all):
    w_in, w_state, bias, proj = layer_weights
    _, steps, rows, width = top_seq.shape
    cell_count = proj.shape[1]
    count = lax.axis_size("mp")
    groups = lax.axis_size("dp")
    weights = (
        w_in,
        w_state,
        bias.astype(F32)[:, None, :],
        proj,
    )
    dma = pltpu.SemaphoreType.DMA
    return pl.pallas_call(
        recurrence_kernel,
        out_shape=(
            jax.ShapeDtypeStruct((2, groups, steps, rows, width), BF16),
            jax.ShapeDtypeStruct((2, groups, steps + 1, rows, width), BF16),
            jax.ShapeDtypeStruct((2, groups, steps, rows, cell_count), BF16),
            jax.ShapeDtypeStruct((2, groups, steps, rows, 4 * cell_count), BF16),
            jax.ShapeDtypeStruct((2, groups, steps, rows, width), BF16),
            jax.ShapeDtypeStruct((2, steps * rows // 2, width // count), BF16),
            jax.ShapeDtypeStruct(features_all.shape, BF16),
        ),
        in_specs=[VMEM_SPEC] * 7 + [ANY_SPEC],
        out_specs=(*[ANY_SPEC] * 5, VMEM_SPEC, ANY_SPEC),
        input_output_aliases={7: 6},
        scratch_shapes=[
            pltpu.VMEM((2, steps, rows, width), BF16),
            pltpu.VMEM((2, steps + 1, rows, width), BF16),
            pltpu.VMEM((2, steps, rows, cell_count), BF16),
            pltpu.VMEM((2, steps, rows, width), BF16),
            pltpu.VMEM((2, steps, 4, rows, cell_count), F32),
            pltpu.VMEM((2, steps + 1, rows, cell_count), F32),
            pltpu.VMEM((2, steps, rows, width), F32),
            pltpu.VMEM((2, rows, 4 * cell_count), F32),
            pltpu.VMEM((2, rows, cell_count), F32),
            pltpu.VMEM((2, 2, count, rows, width), BF16),
            pltpu.VMEM((2, 2, count, rows, width), BF16),
            pltpu.VMEM((2, steps, rows, width), F32),
            pltpu.VMEM((2, SLOTS, rows, 4 * cell_count), BF16),
            dma,
            dma((2, 2, count - 1)),
            dma((2, 2, count)),
            dma((2, 2, count - 1)),
            dma((2, 2, count)),
            dma((2,)),
            dma((2, steps)),
            dma((2,)),
            dma((2, steps)),
            dma((2, SLOTS)),
            dma((2, SLOTS, groups - 1)),
            dma((groups + 2,)),
            dma((5, groups - 1)),
            dma((5, groups - 1)),
            pltpu.VMEM((2, 4 * cell_count, width), BF16),
            pltpu.VMEM((2, 4 * cell_count, width), BF16),
            pltpu.VMEM((2, width, cell_count), BF16),
            pltpu.VMEM((2, steps, count, rows, width // count), BF16),
            pltpu.VMEM((2, steps, count, rows, width // count), BF16),
            dma((count - 1,)),
            dma((count - 1,)),
            pltpu.VMEM((2, steps * rows // 2, width // count), F32),
            dma,
            dma,
            dma((2,)),
            dma((2,)),
        ],
        compiler_params=pltpu.CompilerParams(
            collective_id=0, has_side_effects=True, vmem_limit_bytes=VMEM_LIMIT
        ),
        name="recurrence",
    )(base_seq, live_seq, top_seq, *weights, features_all)


def weight_grads(lefts, right, parts):
    batch, outer, pieces, inner, size = lefts[0].shape
    tokens = right.shape[1]
    inner = tokens // outer
    columns = right.shape[2] // parts
    block = min(512, columns)
    blocks = columns // block
    chunk = min(512, size)
    total = size * len(lefts)
    single = parts == 1

    def kernel(*refs):
        left_refs = refs[: len(lefts)]
        right_refs = refs[len(lefts) : len(lefts) + parts]
        out_refs = refs[len(lefts) + parts : -3]
        bias_out, turned, ones = refs[-3:]

        @pl.when(pl.program_id(2) == 0)
        def _():
            for i, left in enumerate(left_refs):
                for offset in range(0, size, chunk):
                    at = i * size + offset
                    turned[at : at + chunk, :] = (
                        left[0, :, 0, :, offset : offset + chunk].reshape(tokens, chunk).T
                    )
            ones[...] = jnp.ones_like(ones)

        for i, out in enumerate(out_refs):

            @pl.loop(0, size // chunk)
            def _(step):
                at = pl.multiple_of(i * size + step * chunk, chunk)
                own = pl.multiple_of(step * chunk, chunk)
                left = turned[pl.ds(at, chunk), :]
                for part in range(parts):
                    value = jnp.dot(left, right_refs[part][0], preferred_element_type=F32)
                    if single:
                        out[0, pl.ds(own, chunk), :] = value
                    else:
                        out[0, pl.ds(own, chunk), part, :] = value

        for part in range(parts):
            bias_out[0, part : part + 1, :] = jnp.dot(
                ones[...], right_refs[part][0], preferred_element_type=F32
            )[:1]

    outputs = 4 * batch * pieces * total * parts * columns
    return pl.pallas_call(
        kernel,
        out_shape=(
            *[
                jax.ShapeDtypeStruct(
                    (batch, pieces * size, *((parts,) * (not single)), columns), F32
                )
                for _ in lefts
            ],
            jax.ShapeDtypeStruct((batch, parts, columns), F32),
        ),
        grid=(batch, pieces, blocks),
        in_specs=[
            *[
                pl.BlockSpec((1, outer, 1, inner, size), lambda b, p, n: (b, 0, p, 0, 0))
                for _ in lefts
            ],
            *[
                pl.BlockSpec(
                    (1, tokens, block),
                    functools.partial(lambda g, b, p, n: (b, 0, g * blocks + n), g),
                )
                for g in range(parts)
            ],
        ],
        out_specs=(
            *[
                pl.BlockSpec((1, size, block), lambda b, p, n: (b, p, n))
                if single
                else pl.BlockSpec((1, size, parts, block), lambda b, p, n: (b, p, 0, n))
                for _ in lefts
            ],
            pl.BlockSpec((1, parts, block), lambda b, p, n: (b, 0, n)),
        ),
        scratch_shapes=[
            pltpu.VMEM((total, tokens), BF16),
            pltpu.VMEM((16, tokens), BF16),
        ],
        compiler_params=pltpu.CompilerParams(vmem_limit_bytes=VMEM_LIMIT),
        cost_estimate=pl.CostEstimate(
            flops=2 * batch * pieces * total * tokens * parts * columns,
            bytes_accessed=outputs + 2 * right.size + 2 * batch * pieces * total * tokens,
            transcendentals=0,
        ),
        name="weight_grads",
    )(*lefts, *[right] * parts)


def merge_kernel(first_ref, second_ref, gates_in, gates_all, staged, sems):
    far = 3 - lax.axis_index("dp")
    late = first_ref.shape[0]
    half = late // 2
    pieces = [pl.ds(0, half), pl.ds(half, late - half)]
    start = gates_all.shape[2] - late
    loads, stores = [], []
    for d, source in enumerate((first_ref, second_ref)):
        for i, piece in enumerate(pieces):
            target = gates_all.at[d, far, pl.ds(start + i * half, piece.size)]
            buffer = staged.at[d, piece]
            loads.append(pltpu.make_async_copy(source.at[piece], buffer, sems.at[d, i]))
            stores.append(pltpu.make_async_copy(buffer, target, sems.at[d, i]))
    for load in loads:
        load.start()
    for load, store in zip(loads, stores):
        load.wait()
        store.start()
    for store in stores:
        store.wait()


def send_late(late):
    beside = [(i, i + 1 - 2 * (i % 2)) for i in range(4)]
    across = [(i, (i + 2) % 4) for i in range(4)]
    return lax.ppermute(late[0], "dp", across), lax.ppermute(late[1], "dp", beside)


def merge_late(gates_all, moved):
    return pl.pallas_call(
        merge_kernel,
        out_shape=jax.ShapeDtypeStruct(gates_all.shape, BF16),
        in_specs=[ANY_SPEC] * 3,
        out_specs=ANY_SPEC,
        input_output_aliases={2: 0},
        scratch_shapes=[pltpu.VMEM((2, *moved[0].shape), BF16), pltpu.SemaphoreType.DMA((2, 2))],
        compiler_params=pltpu.CompilerParams(vmem_limit_bytes=VMEM_LIMIT),
        name="merge_late",
    )(*moved, gates_all)


def on_device(
    char_ids,
    row_lengths,
    top_grad,
    char_table,
    conv_weight,
    conv_bias,
    highway_weight,
    highway_bias,
    proj_weight,
    proj_bias,
    lstm_input,
    lstm_state,
    lstm_bias,
    lstm_proj,
):
    section = lax.axis_index("section")
    rows, steps, per_token = char_ids.shape
    proj_width = proj_weight.shape[1]
    half = rows // 2
    tokens = half * steps
    local = conv_weight.shape[2]
    emb = char_table.shape[1]
    padded = -(-(per_token + TAPS - 1) // 8) * 8
    vocabulary = -(-char_table.shape[0] // 8) * 8
    chars = lax.dynamic_slice_in_dim(char_ids, section * half, half, 0)
    chars = jnp.transpose(chars, (1, 0, 2)).reshape(tokens, per_token)
    ids = jnp.pad(chars, ((0, 0), (0, padded - per_token)), constant_values=-1)
    ids = ids.reshape(tokens // CHUNK, 1, CHUNK * padded)
    table = jnp.pad(
        jnp.tile(char_table, (1, TAPS)),
        ((0, vocabulary - char_table.shape[0]), (0, 128 - TAPS * emb)),
    )
    widths = filter_widths(lax.axis_index("mp") * local, local, local * lax.axis_size("mp"))
    tap_keep = jnp.arange(TAPS, dtype=jnp.int32)[:, None] < widths[None, :]
    masked = jnp.where(tap_keep[:, None, :], conv_weight, jnp.zeros_like(conv_weight))
    excluded = jnp.arange(1, TAPS + 1, dtype=jnp.int32)[:, None] == widths[None, :]
    masked = jnp.concatenate(
        [
            masked.reshape(TAPS * emb, local),
            conv_bias[None, :],
            jnp.where(excluded, -1e30, 0.0).astype(BF16),
            jnp.zeros((128 - TAPS * emb - 1 - TAPS, local), BF16),
        ]
    )
    log_positions = jnp.log((per_token - widths + 1).astype(F32))[None, :]
    w_high = jnp.transpose(highway_weight, (0, 2, 1, 3))
    b_high = highway_bias.astype(F32)
    (
        base_pair,
        taps,
        peak,
        pooled,
        features,
        current,
        transform,
        gate,
        features_all,
        w_input,
        w_state,
    ) = cnn_forward(
        ids,
        (table, masked, log_positions, w_high, b_high, proj_weight, proj_bias.astype(F32)[None]),
        lstm_input[0],
        lstm_state[0],
    )
    depth_count = highway_weight.shape[0]

    def all_tokens(values):
        return lax.all_gather(values, ("section", "dp"), axis=values.ndim - 2, tiled=True)

    last_features = all_tokens(
        lax.dynamic_index_in_dim(features[depth_count], lax.axis_index("mp"), 0, False)
    )
    top_seq = jnp.transpose(top_grad, (2, 1, 0, 3))
    live = (jnp.arange(steps, dtype=jnp.int32)[:, None] < row_lengths[None, :]).astype(F32)
    live_seq = jnp.broadcast_to(live[..., None], (steps, rows, 128))
    layer_weights = (
        w_input,
        w_state,
        lstm_bias[0].reshape(2, -1),
        lstm_proj[0],
    )
    (
        x_all,
        all_states,
        all_hidden,
        gates_all,
        projected_all,
        base_shards,
        high_features,
    ) = recurrence(base_pair, live_seq, top_seq, layer_weights, features_all)
    own_rows = lax.dynamic_slice_in_dim(proj_weight, lax.axis_index("mp") * local, local, 0).T
    (
        all_gates,
        all_projected,
        all_inputs,
        base_full,
        all_mixed,
        late_first,
        late_second,
        conv_grad,
        table_grad,
    ) = (
        cnn_backward(
            base_shards,
            (taps, peak, pooled, current, transform, gate),
            (own_rows, w_high, masked, ids),
            (gates_all, projected_all, x_all, all_states),
        )
    )
    relayed = lax.axis_size("dp") == 4
    moved = send_late((late_first, late_second)) if relayed else None
    table_flat = table_grad.reshape(-1)
    table_rows = -(-(-(-table_flat.shape[0] // local)) // 16) * 16
    table_flat = jnp.pad(table_flat, (0, table_rows * local - table_flat.shape[0]))
    small = jnp.concatenate([conv_grad, table_flat.reshape(table_rows, local)]).astype(BF16)
    small = lax.all_gather(small, ("section", "dp"), axis=0)
    small = jnp.sum(small.astype(F32), axis=0)
    conv_weight_grad = jnp.where(
        tap_keep[:, None, :], small[: TAPS * emb].reshape(conv_weight.shape), 0.0
    )
    table_grad = small[128:].reshape(-1)[: table_grad.size].reshape(table_grad.shape)
    table_grad = table_grad[:, : char_table.shape[0]].T
    all_base = jnp.transpose(base_full, (0, 1, 3, 2, 4)).reshape(-1, proj_width)

    def flat(values):
        return values.reshape(2, -1, values.shape[4])

    def one_piece(values):
        batch, groups, _, _, width = values.shape
        return values.reshape(batch, groups, 1, -1, width)

    proj_weight_grad = lax.all_gather(
        dot(last_features, all_base, 0, 0).astype(BF16), "mp", axis=0, tiled=True
    ).astype(F32)
    proj_grad = weight_grads([one_piece(all_hidden)], flat(all_projected), 1)[0]
    batch, _, groups, count, _, _ = high_features.shape
    high_grad, high_bias_grad = weight_grads(
        [high_features.reshape(batch, 2 * groups, count, tokens, local)],
        all_mixed.reshape(batch, -1, 2 * local),
        2,
    )
    if relayed:
        moved, high_grad, proj_grad = lax.optimization_barrier((moved, high_grad, proj_grad))
        all_gates = merge_late(all_gates, moved)
    input_grad, state_grad, bias_grad = weight_grads(
        [one_piece(all_inputs), one_piece(all_states)], flat(all_gates), 4
    )
    return (
        table_grad,
        conv_weight_grad,
        small[TAPS * emb],
        high_grad,
        high_bias_grad,
        proj_weight_grad,
        jnp.sum(all_base.astype(F32), axis=0),
        input_grad.reshape(lstm_input.shape),
        state_grad.reshape(lstm_state.shape),
        bias_grad.reshape(lstm_bias.shape),
        proj_grad.reshape(lstm_proj.shape),
    )


def solution(mesh):
    return jax.shard_map(
        on_device,
        mesh=mesh,
        in_specs=(
            P("dp", None, None),
            P("dp"),
            P("dp", None, None, None),
            P(),
            P(None, None, "mp"),
            P("mp"),
            P(None, None, None, "mp"),
            P(None, None, "mp"),
            P(),
            P(),
            P("section", None, None, None, "mp"),
            P("section", None, None, None, "mp"),
            P("section", None, None, "mp"),
            P("section", None, "mp", None),
        ),
        out_specs=(
            P(),
            P(None, None, "mp"),
            P("mp"),
            P(None, None, None, "mp"),
            P(None, None, "mp"),
            P(),
            P(),
            P("section", None, None, None, "mp"),
            P("section", None, None, None, "mp"),
            P("section", None, None, "mp"),
            P("section", None, "mp", None),
        ),
        check_vma=False,
    )
```

time: 847 us -> 535 us (0.63)
  blocking collectives: 137 us -> 0 us
  local copies, waits for them, and re-layouts: 158 us -> 21.8 us
  Pallas kernels: 388 us -> 460 us
  matrix products: 48.5 us -> 2.98 us
  waiting for transfers between devices: 49 us -> 15.5 us
  other arithmetic: 43.5 us -> 14.5 us
    pallas_call x2 -> x6, Pallas kernels: 69.8 us -> 210 us  [the longest x1 73.8 us: cnn_backward(): pl.pallas_call(cnn_backward_kernel, out_shape=(jax.ShapeDtypeStruct(gates...]
    psum x3 -> x0, blocking collectives: 83.5 us -> none  [the longest x1 39.7 us: on_device(): table_grad = lax.psum(table_grad, ('section', 'mp', 'dp'))]
    pallas_call x1, Pallas kernels: 318 us -> 250 us  [recurrence(): pl.pallas_call(recurrence_kernel, out_shape=(jax.ShapeDtypeStruct((2, gro...]
    all_gather x4 -> x0, blocking collectives: 53.4 us -> none  [the longest x3 51.4 us: spread(): return lax.all_gather(values, 'mp', axis=1, tiled=True)]
    reshape x8 -> x5, local copies, waits for them, and re-layouts: 40.6 us -> 0.91 us  [the longest x1 0.75 us: on_device(): ids = ids.reshape(tokens // CHUNK, 1, CHUNK * padded)]
    unnamed x113 -> x17, local copies, waits for them, and re-layouts: 45.1 us -> 10.3 us
    reduce_scatter x2 -> x0, waiting for transfers between devices: 28.7 us -> none  [cnn_backward(): lax.psum_scatter(dot(weight_here, grad_mixed, 1, 1), 'mp', scatter_dimens...]
    dot_general x7 -> x1, matrix products: 31.3 us -> 2.98 us  [dot(): lax.dot_general(left, right, (((left_dim,), (right_dim,)), ((), ())), pre...]
  transfers between devices with their start and end apart: 8 -> 5, of which waited for: 3 -> 2; matrix products, arithmetic and copies ran while one was open for 13% -> 3% of each run, Pallas kernels for 8% -> 73%
where the time goes in v3:
time: 535 us; the launch traced here: 532 us
  Pallas kernels  460 us (86%)
  local copies, waits for them, and re-layouts  21.8 us (4%)
  waiting for transfers between devices  15.5 us (3%)
  other arithmetic  14.5 us (3%)
  between operations  14.2 us (3%)
    pallas_call x1, Pallas kernels, recurrence(): pl.pallas_call(recurrence_kernel, out_shape=(jax.ShapeDtypeStruct((2, gro...  250 us
    pallas_call x1, Pallas kernels, cnn_backward(): pl.pallas_call(cnn_backward_kernel, out_shape=(jax.ShapeDtypeStruct(gates...  73.8 us
    pallas_call x1, Pallas kernels, cnn_forward(): pl.pallas_call(cnn_forward_kernel, out_shape=(jax.ShapeDtypeStruct((2, to...  71.3 us
    pallas_call x3, Pallas kernels, weight_grads(): pl.pallas_call(kernel, out_shape=(*[jax.ShapeDtypeStruct((batch, pieces *...  62.1 us
    ppermute x1, waiting for transfers between devices, send_late(): lax.ppermute(late[0], 'dp', across)  13.9 us
  transfers between devices with their start and end apart: 5, of which 2 were waited for; matrix products, arithmetic and copies ran while one was open for 3% of the time, Pallas kernels for 73%

profile of v3, /device:TPU:0, one launch (start us, length us, event | category | flops | bytes accessed | tf_op | source)
XLA Modules:
  0.0 532.4 jit_solution(2786502755536123564)
XLA Ops:
  7.2 0.0 all-gather.9.cloned.1.call-start
  7.3 0.6 fusion.21.log_positions
  7.9 0.7 broadcast_in_dim.59
  8.6 1.3 broadcast_in_dim.67
  9.9 0.1 select_convert_fusion
  9.9 1.3 convert_element_type.172.b_high
  11.2 0.1 gt.15
  11.4 0.7 reshape.321.ids_ref
  12.1 0.7 tile.6
  12.8 0.1 copy.46
  13.0 8.2 %copy.64 = bf16[2,2048,2,512]{3,1,2,0:T(8,128)(2,1)} copy(bf16[2,2048,2,512]{3,2,1,0:T(2,128)(2,1)} %param.20) | data formatting | bytes 16777216 | tf_op args[6]
  21.2 0.6 pad.18.table_ref
  21.8 0.1 pad.26.clone
  21.9 0.7 maximum_maximum_fusion.masked_ref
  22.7 1.0 or_convert_fusion.flags_ref
  23.7 71.3 %cnn_forward.1 = (f32[2,160,512]{2,1,0:T(8,128)}, bf16[10,896,128]{2,1,0:T(8,128)(2,1)}, f32[160,1,512]{2,1,0:T(1,128)}, f32[160,512]{1,0:T(8,128)}, bf16[3,4,16...) custom-call(s32[10,1,896]{2,1,0:T(1,128)} %reshape.321.ids_ref, ...), custom_call_target="tpu_custom_call" | custom-call | tf_op jit(solution)/shard_map/cnn_forward/pallas_call | solution.py:370
  95.0 1.2 slice.22
  96.2 0.7 constant_dynamic-slice_fusion
  96.9 0.0 all-gather.5.cloned.1.call-start
  96.9 0.1 copy.51
  97.1 0.7 reshape.319.bias_ref
  97.7 1.1 constant_dynamic-slice_fusion.1
  98.8 1.0 copy.54
  99.8 1.0 copy.65
  100.9 0.8 broadcast_in_dim.65.live_ref
  101.6 250.1 %recurrence.1 = (bf16[2,4,20,16,512]{4,3,2,1,0:T(8,128)(2,1)}, bf16[2,4,21,16,512]{4,3,2,1,0:T(8,128)(2,1)}, bf16[2,4,20,16,1024]{4,3,2,1,0:T(8,128)(2,1)}, bf16...) custom-call(f32[2,160,512]{2,1,0:T(8,128)} %get-tuple-element.48.bas, ...), custom_call_target="tpu_custom_call", output_to_operand_aliasing={{6}: (7, {})} | custom-call | tf_op jit(solution)/shard_map/recurrence/pallas_call | solution.py:1416
  351.7 0.7 pad_bitcast_fusion.masked_t
  352.4 73.8 %cnn_backward.1 = (bf16[2,4,20,16,4096]{4,3,2,1,0:T(8,128)(2,1)}, bf16[2,4,20,16,512]{4,3,2,1,0:T(8,128)(2,1)}, bf16[2,4,20,16,512]{4,3,2,1,0:T(8,128)(2,1)}, bf...) custom-call(bf16[2,160,128]{2,1,0:T(8,128)(2,1)} %get-tuple-element., ...), custom_call_target="tpu_custom_call", output_to_operand_aliasing={{0}: (12, {}), {1}: (13, {}), {2}: (14, {})} | custom-call | tf_op jit(solution)/shard_map/cnn_backward/pallas_call | solution.py:799
  426.2 0.7 convert.14
  427.0 1.0 convert_bitcast_fusion
  428.0 0.7 pad_maximum_fusion
  428.7 0.0 all-gather.7.cloned.1.call-start
  428.7 2.2 collective-permute-start
  430.9 0.6 collective-permute-start.1
  431.5 2.0 copy.53
  433.5 3.0 fusion.4
  436.6 19.5 %weight_grads.3 = (f32[2,2048,2,512]{3,2,1,0:T(2,128)}, f32[2,2,512]{2,1,0:T(2,128)}) custom-call(bf16[2,8,4,160,512]{4,3,2,1,0:T(8,128)(2,1)} %bitcast.59, bf16[2,1280,1024]{2,1,0:T(8,128)(2,1)} %bitcast.78, bf16[2,1280,1024]{2,1,0:T(8,128)(2,1)} %bitcast.79), custom_call_target="tpu_custom_call" | custom-call | flops 10737418240 | bytes 32505856 | tf_op jit(solution)/shard_map/weight_grads/pallas_call | solution.py:1525
  456.1 0.8 convert_reduce_fusion
  456.9 8.5 %weight_grads.4 = (f32[2,1024,512]{2,1,0:T(8,128)}, f32[2,1,512]{2,1,0:T(1,128)}) custom-call(bf16[2,4,1,320,1024]{4,3,2,1,0:T(8,128)(2,1)} %bitcast.77, bf16[2,1280,512]{2,1,0:T(8,128)(2,1)} %bitcast.63), custom_call_target="tpu_custom_call" | custom-call | flops 2684354560 | bytes 12058624 | tf_op jit(solution)/shard_map/weight_grads/pallas_call | solution.py:1525
  465.4 13.9 %collective-permute-done.first_ref = bf16[15,16,4096]{2,1,0:T(8,128)(2,1)} collective-permute-done((bf16[15,16,4096]{2,1,0:T(8,128)(2,1)}, bf16[15,16,4096]{2,1,0:T(8,128)(2,1)}, u32[]{:S(2)}, u32[]{:S(2)}) %collective-permute-start) | collective-permute-done | bytes 1966112 | tf_op jit(solution)/shard_map/ppermute | solution.py:1598
  479.3 1.5 collective-permute-done.1.second_ref
  480.8 3.2 merge_late.1
  484.0 34.0 %weight_grads.5 = (f32[2,512,4,1024]{3,2,1,0:T(4,128)}, f32[2,512,4,1024]{3,2,1,0:T(4,128)}, f32[2,4,1024]{2,1,0:T(4,128)}) custom-call(bf16[2,4,1,320,512]{4,3,2,1,0:T(8,128)(2,1)} %bitcast.58, bf16[2,4,1,336,512]{4,3,2,1,0:T(8,128)(2,1)} %bitcast.57, bf16[2,1280,4096]{2,1,0:T(8,128)(2,1)} %bitcast.51, bf16[2,1280,4096]{2,1,0:T(8,128)(2,1)} %bitcast.52, ...), custom_call_target="tpu_custom_call" | custom-call | flops 21474836480 | bytes 59768832 | tf_op jit(solution)/shard_map/weight_grads/pallas_call | solution.py:1525
  518.0 1.5 convert_reduce_fusion.1
  519.5 0.6 slice.26
  520.1 0.6 slice_bitcast_fusion
  520.7 0.7 broadcast_select_fusion
  521.4 4.2 convert_element_type.178
  (37 shorter events, 0.3 us)
Async XLA Ops:
  7.2 4.1 copy-start
  7.2 426.3 %all-gather.9.cloned.1.call-start = ((), (), s32[]{:S(2)}) async-start(), calls=%async_computation.2 | async-start | bytes 1474560 | tf_op jit(solution)/shard_map/all_gather | solution.py:1683
  13.0 9.0 %copy-start.4 = (bf16[7,16,512]{2,1,0:T(8,128)(2,1)S(1)}, bf16[7,16,512]{2,1,0:T(8,128)(2,1)}, u32[]{:S(2)}) copy-start(bf16[7,16,512]{2,1,0:T(8,128)(2,1)} %param.18) | copy-start | bytes 344068
  23.7 73.4 %copy-start.5 = (bf16[1,2,4,1024]{3,2,1,0:T(4,128)(2,1)S(1)}, bf16[1,2,4,1024]{3,2,1,0:T(4,128)(2,1)}, u32[]{:S(2)}) copy-start(bf16[1,2,4,1024]{3,2,1,0:T(4,128)(2,1)} %param.26) | copy-start | bytes 49156
  95.0 4.9 copy-start.3
  95.0 5.9 %copy-start.6 = (s32[16]{0:T(128)S(1)}, s32[16]{0:T(128)}, u32[]{:S(2)}) copy-start(s32[16]{0:T(128)} %param.15) | copy-start | bytes 196
  96.9 421.1 %all-gather.5.cloned.1.call-start = ((), (), s32[]{:S(2)}) async-start(), calls=%async_computation | async-start | bytes 1327104 | tf_op jit(solution)/shard_map/all_gather | solution.py:1731
  428.7 92.8 %all-gather.7.cloned.1.call-start = ((), (), s32[]{:S(2)}) async-start(), calls=%async_computation.1 | async-start | bytes 2621440 | tf_op jit(solution)/shard_map/all_gather | solution.py:1747
  428.7 50.6 %collective-permute-start = (bf16[15,16,4096]{2,1,0:T(8,128)(2,1)}, bf16[15,16,4096]{2,1,0:T(8,128)(2,1)}, u32[]{:S(2)}, u32[]{:S(2)}) collective-permute-start(bf16[15,16,4096]{2,1,0:T(8,128)(2,1)} %get-tuple-element.65), channel_id=1, source_target_pairs={{0,2},{1,3},{2,0},{3,1},{4,6},{5,7},{6,4},{7,5},{8,10},{9,11},{10,... | collective-permute-start | bytes 5898248 | tf_op jit(solution)/shard_map/ppermute | solution.py:1598
  430.9 49.9 %collective-permute-start.1 = (bf16[15,16,4096]{2,1,0:T(8,128)(2,1)}, bf16[15,16,4096]{2,1,0:T(8,128)(2,1)}, u32[]{:S(2)}, u32[]{:S(2)}) collective-permute-start(bf16[15,16,4096]{2,1,0:T(8,128)(2,1)} %get-tuple-element.66), channel_id=1, source_target_pairs={{0,1},{1,0},{2,3},{3,2},{4,5},{5,4},{6,7},{7,6},{8,9},{9,8},{10,11... | collective-permute-start | bytes 5898248 | tf_op jit(solution)/shard_map/ppermute | solution.py:1598
  436.5 19.5 %copy-start.2 = (bf16[2,4,4,160,128]{4,3,2,1,0:T(8,128)(2,1)S(1)}, bf16[2,4,4,160,128]{4,3,2,1,0:T(8,128)(2,1)}, u32[]{:S(2)}) copy-start(bf16[2,4,4,160,128]{4,3,2,1,0:T(8,128)(2,1)} %get-tuple-element.76) | copy-start | bytes 3932164
  520.7 4.9 copy-start.1
Sparse Core Ops, SparseCore 0:
  97.0 26.2 all-gather.8
  428.8 29.6 all-gather.4
  460.7 46.0 all-gather.6

commit v4 on v3

--- a/solution.py
+++ b/solution.py
@@ -2,6 +2,7 @@
 
 import jax
 import jax.numpy as jnp
+import numpy as np
 from jax import lax
 from jax.experimental import pallas as pl
 from jax.experimental.pallas import tpu as pltpu
@@ -13,9 +14,9 @@
 TAPS = 7
 VMEM_LIMIT = 62 * 1024 * 1024
 SLOTS = 4
+DEFER = 3
 CHUNK = 16
 TURN = 128
-RELAY_SHARE = 4
 PER_TOKEN = 50
 CHARS = 262
 
@@ -89,13 +90,14 @@
     taps_out,
     peak_out,
     pooled_out,
-    features,
     current_out,
     transform_out,
     gate_out,
     features_all,
+    last_out,
     input_out,
     state_out,
+    features,
     raw,
     turned,
     send_sem,
@@ -284,7 +286,7 @@
                     give_rows(depth, j, group).start()
             mixed = []
             for g in range(2):
-                total = jnp.broadcast_to(b_high[depth, g : g + 1, :], (half, local))
+                total = jnp.broadcast_to(b_high[depth, g : g + 1, :].astype(F32), (half, local))
                 for p in range(count):
                     total = total + jnp.dot(
                         features[depth, p, rows, :],
@@ -301,6 +303,8 @@
             )
             if depth + 1 < depth_count:
                 current_out[depth + 1, rows, :] = current
+            else:
+                last_out[rows, :] = current.astype(BF16)
             features[depth + 1, me, rows, :] = current.astype(BF16)
             send(depth + 1, part, rows, True)
         if depth >= 1:
@@ -319,7 +323,7 @@
     for part in range(2):
         rows = pl.ds(part * half, half)
         receive(depth_count, part)
-        total = jnp.broadcast_to(b_proj[...], (half, w_proj.shape[1]))
+        total = jnp.broadcast_to(b_proj[...].astype(F32), (half, w_proj.shape[1]))
         for p in range(count):
             total = total + jnp.dot(
                 features[depth_count, p, rows, :],
@@ -362,10 +366,12 @@
     groups = lax.axis_size("dp")
     directions, in_width, gate_blocks, cell_columns = lstm_input.shape
     padded = chunk_rows // CHUNK
-    position = jnp.tile(jnp.arange(padded, dtype=jnp.int32), CHUNK)[:, None]
-    lane = jnp.arange(128, dtype=jnp.int32)[None, :]
-    width = lane - 16 * TAPS
-    flags = (lane == 16 * TAPS) | ((width >= 1) & (width <= TAPS) & (position > PER_TOKEN - width))
+    position = np.tile(np.arange(padded), CHUNK)[:, None]
+    lane = np.arange(128)[None, :]
+    excluded = lane - 16 * TAPS
+    flags = (lane == 16 * TAPS) | (
+        (excluded >= 1) & (excluded <= TAPS) & (position > PER_TOKEN - excluded)
+    )
     dma = pltpu.SemaphoreType.DMA
     return pl.pallas_call(
         cnn_forward_kernel,
@@ -374,17 +380,18 @@
             jax.ShapeDtypeStruct((chunks, chunk_rows, 128), BF16),
             jax.ShapeDtypeStruct((tokens, 1, local), F32),
             jax.ShapeDtypeStruct((tokens, local), F32),
-            jax.ShapeDtypeStruct((depth_count + 1, count, tokens, local), BF16),
             jax.ShapeDtypeStruct((depth_count, tokens, local), F32),
             jax.ShapeDtypeStruct((depth_count, tokens, local), F32),
             jax.ShapeDtypeStruct((depth_count, tokens, local), F32),
             jax.ShapeDtypeStruct((depth_count, 2, groups, count, tokens, local), BF16),
+            jax.ShapeDtypeStruct((tokens, local), BF16),
             jax.ShapeDtypeStruct((directions, gate_blocks, in_width, cell_columns), BF16),
             jax.ShapeDtypeStruct((directions, gate_blocks, in_width, cell_columns), BF16),
         ),
         in_specs=[VMEM_SPEC] * 9 + [ANY_SPEC] * 2,
-        out_specs=(*[VMEM_SPEC] * 8, *[ANY_SPEC] * 3),
+        out_specs=(*[VMEM_SPEC] * 7, ANY_SPEC, VMEM_SPEC, *[ANY_SPEC] * 2),
         scratch_shapes=[
+            pltpu.VMEM((depth_count + 1, count, tokens, local), BF16),
             pltpu.VMEM((2, TURN, gate_blocks, cell_columns), BF16),
             pltpu.VMEM((2, gate_blocks, TURN, cell_columns), BF16),
             dma((depth_count + 1, 2, count - 1)),
@@ -406,7 +413,7 @@
     )(
         ids,
         table,
-        flags.astype(F32),
+        jnp.asarray(flags.astype(np.float32)),
         masked,
         log_positions,
         w_high,
@@ -440,10 +447,12 @@
     x_all,
     base_full,
     mixed_all,
-    late_first,
-    late_second,
+    late_a,
+    late_b,
+    late_c,
+    late_d,
+    small_out,
     conv_out,
-    table_out,
     mixed_out,
     late_buf,
     base_all,
@@ -474,6 +483,8 @@
     mixed_share,
     mixed_shared,
     late_sem,
+    defer_send,
+    defer_recv,
 ):
     count = lax.axis_size("mp")
     me = lax.axis_index("mp")
@@ -506,31 +517,40 @@
             {"section": 1 - section},
         )
 
-    def relay(kind, buffer, d, slot):
-        early = pl.ds(0, steps if kind == 0 else steps // RELAY_SHARE)
+    half_steps = steps // 2
+    others = [lax.rem(group + j, groups) for j in range(1, groups)]
+    near = [beside, across] if relayed else others
+    origin = near if relayed else others[::-1]
+
+    def relay(way, slot):
         return remote(
-            buffer.at[d, slot, early],
-            buffer.at[d, slot, early],
-            relay_send.at[kind, d],
-            relay_recv.at[kind, d],
-            {"dp": across if d == 0 else beside},
-        )
-
-    buffers = ((0, projected_all), (1, gates_all))
-
-    early = steps // RELAY_SHARE
-    late = pl.ds(early, steps - early)
-    late_loads = [
-        pltpu.make_async_copy(gates_all.at[d, slot, late], late_buf.at[d], late_sem.at[d])
-        for d, slot in ((0, beside), (1, across))
-    ]
-    late_stores = [
-        pltpu.make_async_copy(late_buf.at[d], target, late_sem.at[d])
-        for d, target in ((0, late_first), (1, late_second))
-    ]
-    if relayed:
-        for copy in late_loads:
-            copy.start()
+            projected_all.at[way, slot],
+            projected_all.at[way, slot],
+            relay_send.at[way],
+            relay_recv.at[way],
+            {"dp": across if way == 0 else beside},
+        )
+
+    def deferred(j, slot):
+        return remote(
+            gates_all.at[:, slot, pl.ds(0, DEFER)],
+            gates_all.at[:, slot, pl.ds(0, DEFER)],
+            defer_send.at[j],
+            defer_recv.at[j],
+            {"dp": near[j]},
+        )
+
+    for j in range(len(near)):
+        deferred(j, group).start()
+
+
+    late_loads, late_stores = [], []
+    for i, target in enumerate((late_a, late_b, late_c, late_d)):
+        d, way = i // 2, i % 2
+        rows = pl.ds(way * half_steps, half_steps)
+        source = gates_all.at[d, (beside, across)[way], rows]
+        late_loads.append(pltpu.make_async_copy(source, late_buf.at[i], late_sem.at[i]))
+        late_stores.append(pltpu.make_async_copy(late_buf.at[i], target, late_sem.at[i]))
 
     def spread_base(half, target_section, peer, j):
         return remote(
@@ -570,7 +590,6 @@
     def _():
         base_arrival(me).wait_recv()
 
-    others = [lax.rem(group + j, groups) for j in range(1, groups)]
     keep = pltpu.make_async_copy(base_all, base_full.at[section, group], full_sem)
     keep.start()
 
@@ -625,10 +644,14 @@
         share_mixed(depth, section).start()
 
     wide = base_all.shape[2]
+    own_rows = pl.ds(pl.multiple_of(me * local, local), local)
     total = jnp.zeros((tokens, local), F32)
     for p in range(count):
-        total = total + jnp.dot(
-            base_all[p], own_ref[p * wide : (p + 1) * wide, :], preferred_element_type=F32
+        total = total + lax.dot_general(
+            base_all[p],
+            own_ref[own_rows, p * wide : (p + 1) * wide],
+            (((1,), (1,)), ((), ())),
+            preferred_element_type=F32,
         )
     grad_current[...] = total
 
@@ -669,9 +692,8 @@
         for j in range(groups - 1):
             mixed_row(depth, j, group).start()
         if relayed and depth == depth_count - 1:
-            for kind, buffer in buffers:
-                for d in range(2):
-                    relay(kind, buffer, d, beside if d == 0 else across).start()
+            for way in range(2):
+                relay(way, beside if way == 0 else across).start()
         for j, peer in enumerate(peers):
             outgoing[depth, j] = back(depth, peer).astype(BF16)
             send_sum(depth, peer, j).start()
@@ -687,14 +709,21 @@
             total = total + incoming[depth, peer].astype(F32)
         grad_current[...] = total
 
+    for j in range(len(near)):
+        deferred(j, group).wait_send()
+        deferred(j, origin[j]).wait_recv()
+    if relayed:
+        for load in late_loads:
+            load.start()
+    for depth in range(depth_count - 1, 0, -1):
+        collect_mixed(depth)
     if relayed:
         for load, store in zip(late_loads, late_stores):
             load.wait()
             store.start()
-    for depth in range(depth_count - 1, 0, -1):
-        collect_mixed(depth)
     grad_current[...] = grad_current[...] * jax.nn.sigmoid(pooled_ref[...])
     conv_out[...] = jnp.zeros_like(conv_out)
+    small_out[...] = jnp.zeros_like(small_out)
     table_sum[...] = jnp.zeros_like(table_sum)
     lane_group = lax.broadcasted_iota(jnp.int32, (chunk_rows, 128), 1) // emb
 
@@ -742,7 +771,11 @@
     folded = table_all[0]
     for p in range(1, count):
         folded = folded + table_all[p]
-    table_out[...] = folded
+    small_out[:128, :] = conv_out[...].astype(BF16)
+    span = min(local, folded.shape[1])
+    for i in range(folded.shape[1] // span):
+        at = 128 + i * emb
+        small_out[at : at + emb, :span] = folded[:, i * span : (i + 1) * span].astype(BF16)
     for j in range(count - 1):
         table_copy(j, me).wait_send()
     keep.wait()
@@ -771,10 +804,9 @@
         lift().wait_recv()
 
     if relayed:
-        for kind, buffer in buffers:
-            for d in range(2):
-                relay(kind, buffer, d, beside if d == 0 else across).wait_send()
-                relay(kind, buffer, d, far).wait_recv()
+        for way in range(2):
+            relay(way, beside if way == 0 else across).wait_send()
+            relay(way, far).wait_recv()
         for copy in late_stores:
             copy.wait()
 
@@ -786,15 +818,15 @@
 
 
 def cnn_backward(base_shards, saved, weights, rows_all):
-    own_rows, w_high, masked, ids = weights
+    w_proj, w_high, masked, ids = weights
     taps, peak, pooled, current, transform, gate = saved
     gates_all, projected_all, x_all, state_all = rows_all
     depth_count, tokens, local = current.shape
     count = lax.axis_size("mp")
     groups = lax.axis_size("dp")
     vocabulary = -(-CHARS // 128) * 128
-    steps = gates_all.shape[2]
-    late = steps - steps // RELAY_SHARE
+    half_steps = gates_all.shape[2] // 2
+    late = (half_steps, *gates_all.shape[3:])
     dma = pltpu.SemaphoreType.DMA
     return pl.pallas_call(
         cnn_backward_kernel,
@@ -804,17 +836,16 @@
             jax.ShapeDtypeStruct(x_all.shape, BF16),
             jax.ShapeDtypeStruct((2, groups, count, tokens, base_shards.shape[2]), BF16),
             jax.ShapeDtypeStruct((depth_count, 2, groups, tokens, 2 * local), BF16),
-            jax.ShapeDtypeStruct((late, *gates_all.shape[3:]), BF16),
-            jax.ShapeDtypeStruct((late, *gates_all.shape[3:]), BF16),
-            jax.ShapeDtypeStruct((128, local), F32),
-            jax.ShapeDtypeStruct((16, vocabulary), F32),
+            *[jax.ShapeDtypeStruct(late, BF16)] * 4,
+            jax.ShapeDtypeStruct((128 + 16 * max(1, vocabulary // local), local), BF16),
         ),
         in_specs=[VMEM_SPEC] * 12 + [ANY_SPEC] * 4,
-        out_specs=(*[ANY_SPEC] * 7, *[VMEM_SPEC] * 2),
+        out_specs=(*[ANY_SPEC] * 9, VMEM_SPEC),
         input_output_aliases={12: 0, 13: 1, 14: 2},
         scratch_shapes=[
+            pltpu.VMEM((128, local), F32),
             pltpu.VMEM((depth_count, tokens, 2 * local), BF16),
-            pltpu.VMEM((2, late, *gates_all.shape[3:]), BF16),
+            pltpu.VMEM((4, *late), BF16),
             pltpu.VMEM((count, tokens, base_shards.shape[2]), BF16),
             pltpu.VMEM((vocabulary, 128), F32),
             pltpu.VMEM((count, 16, vocabulary), F32),
@@ -826,8 +857,8 @@
             dma((depth_count, count - 1)),
             dma((depth_count, count)),
             dma,
-            dma((2, 2)),
-            dma((2, 2)),
+            dma((2,)),
+            dma((2,)),
             dma,
             dma,
             dma((groups - 1,)),
@@ -842,7 +873,9 @@
             dma((depth_count, groups - 1)),
             dma((depth_count,)),
             dma((depth_count,)),
-            dma((2,)),
+            dma((4,)),
+            dma((groups - 1,)),
+            dma((groups - 1,)),
         ],
         compiler_params=pltpu.CompilerParams(
             collective_id=2, has_side_effects=True, vmem_limit_bytes=VMEM_LIMIT
@@ -850,7 +883,7 @@
         name="cnn_backward",
     )(
         base_shards,
-        own_rows,
+        w_proj,
         w_high,
         current,
         transform,
@@ -1085,7 +1118,8 @@
         for block in range(4):
             for start in range(0, cell_count, chunk):
                 cols = slice(block * cell_count + start, block * cell_count + start + chunk)
-                pre[d, :, cols] = bias_ref[d, :, cols] + jnp.dot(
+                bias = bias_ref[d, block : block + 1, start : start + chunk].astype(F32)
+                pre[d, :, cols] = bias + jnp.dot(
                     x, w_in[d, block, :, start : start + chunk], preferred_element_type=F32
                 )
 
@@ -1240,8 +1274,10 @@
         gates_copy(d, k, slot).start()
 
     def gates_send(d, k):
-        for j, other in enumerate(near):
-            gates_row(d, k, lax.rem(k, SLOTS), j, other).start()
+        @pl.when(k >= DEFER)
+        def _():
+            for j, other in enumerate(near):
+                gates_row(d, k, lax.rem(k, SLOTS), j, other).start()
 
     def backward_state(d, k):
         @pl.when(k > 0)
@@ -1318,7 +1354,8 @@
         for k in range(min(SLOTS, steps)):
             gates_copy(d, k, k % SLOTS).wait()
             for j, other in enumerate(near):
-                gates_row(d, k, k % SLOTS, j, other).wait_send()
+                if k >= DEFER:
+                    gates_row(d, k, k % SLOTS, j, other).wait_send()
 
     @pl.when(section == 1)
     def _():
@@ -1388,8 +1425,8 @@
     for j, other in enumerate(near):
         source = from_peer(j, near)
         pltpu.make_async_remote_copy(
-            src_ref=gates_all.at[:, source],
-            dst_ref=gates_all.at[:, source],
+            src_ref=gates_all.at[:, source, pl.ds(DEFER, steps - DEFER)],
+            dst_ref=gates_all.at[:, source, pl.ds(DEFER, steps - DEFER)],
             send_sem=row_send.at[0, j],
             recv_sem=row_recv.at[0, j],
             device_id={"dp": other},
@@ -1409,7 +1446,7 @@
     weights = (
         w_in,
         w_state,
-        bias.astype(F32)[:, None, :],
+        bias,
         proj,
     )
     dma = pltpu.SemaphoreType.DMA
@@ -1475,7 +1512,7 @@
     )(base_seq, live_seq, top_seq, *weights, features_all)
 
 
-def weight_grads(lefts, right, parts):
+def weight_grads(lefts, right, parts, only=None, done=()):
     batch, outer, pieces, inner, size = lefts[0].shape
     tokens = right.shape[1]
     inner = tokens // outer
@@ -1485,11 +1522,16 @@
     chunk = min(512, size)
     total = size * len(lefts)
     single = parts == 1
+    chosen = 1 if only is not None else batch
+
+    def entry(b):
+        return b if only is None else only
+
 
     def kernel(*refs):
         left_refs = refs[: len(lefts)]
         right_refs = refs[len(lefts) : len(lefts) + parts]
-        out_refs = refs[len(lefts) + parts : -3]
+        out_refs = refs[len(lefts) + parts + len(done) : -3]
         bias_out, turned, ones = refs[-3:]
 
         @pl.when(pl.program_id(2) == 0)
@@ -1521,7 +1563,7 @@
                 ones[...], right_refs[part][0], preferred_element_type=F32
             )[:1]
 
-    outputs = 4 * batch * pieces * total * parts * columns
+    outputs = 4 * chosen * pieces * total * parts * columns
     return pl.pallas_call(
         kernel,
         out_shape=(
@@ -1533,28 +1575,30 @@
             ],
             jax.ShapeDtypeStruct((batch, parts, columns), F32),
         ),
-        grid=(batch, pieces, blocks),
+        grid=(chosen, pieces, blocks),
         in_specs=[
             *[
-                pl.BlockSpec((1, outer, 1, inner, size), lambda b, p, n: (b, 0, p, 0, 0))
+                pl.BlockSpec((1, outer, 1, inner, size), lambda b, p, n: (entry(b), 0, p, 0, 0))
                 for _ in lefts
             ],
             *[
                 pl.BlockSpec(
                     (1, tokens, block),
-                    functools.partial(lambda g, b, p, n: (b, 0, g * blocks + n), g),
+                    functools.partial(lambda g, b, p, n: (entry(b), 0, g * blocks + n), g),
                 )
                 for g in range(parts)
             ],
+            *[ANY_SPEC] * len(done),
         ],
+        input_output_aliases={len(lefts) + parts + i: i for i in range(len(done))},
         out_specs=(
             *[
-                pl.BlockSpec((1, size, block), lambda b, p, n: (b, p, n))
+                pl.BlockSpec((1, size, block), lambda b, p, n: (entry(b), p, n))
                 if single
-                else pl.BlockSpec((1, size, parts, block), lambda b, p, n: (b, p, 0, n))
+                else pl.BlockSpec((1, size, parts, block), lambda b, p, n: (entry(b), p, 0, n))
                 for _ in lefts
             ],
-            pl.BlockSpec((1, parts, block), lambda b, p, n: (b, 0, n)),
+            pl.BlockSpec((1, parts, block), lambda b, p, n: (entry(b), 0, n)),
         ),
         scratch_shapes=[
             pltpu.VMEM((total, tokens), BF16),
@@ -1562,27 +1606,24 @@
         ],
         compiler_params=pltpu.CompilerParams(vmem_limit_bytes=VMEM_LIMIT),
         cost_estimate=pl.CostEstimate(
-            flops=2 * batch * pieces * total * tokens * parts * columns,
+            flops=2 * chosen * pieces * total * tokens * parts * columns,
             bytes_accessed=outputs + 2 * right.size + 2 * batch * pieces * total * tokens,
             transcendentals=0,
         ),
         name="weight_grads",
-    )(*lefts, *[right] * parts)
-
-
-def merge_kernel(first_ref, second_ref, gates_in, gates_all, staged, sems):
+    )(*lefts, *[right] * parts, *done)
+
+
+def merge_kernel(d, first_ref, second_ref, gates_in, gates_all, staged, sems):
     far = 3 - lax.axis_index("dp")
     late = first_ref.shape[0]
-    half = late // 2
-    pieces = [pl.ds(0, half), pl.ds(half, late - half)]
-    start = gates_all.shape[2] - late
+    half_steps = gates_all.shape[2] // 2
     loads, stores = [], []
-    for d, source in enumerate((first_ref, second_ref)):
-        for i, piece in enumerate(pieces):
-            target = gates_all.at[d, far, pl.ds(start + i * half, piece.size)]
-            buffer = staged.at[d, piece]
-            loads.append(pltpu.make_async_copy(source.at[piece], buffer, sems.at[d, i]))
-            stores.append(pltpu.make_async_copy(buffer, target, sems.at[d, i]))
+    for way, source in enumerate((first_ref, second_ref)):
+        rows = pl.ds((way + 1) * half_steps - late, late)
+        buffer = staged.at[way]
+        loads.append(pltpu.make_async_copy(source, buffer, sems.at[way]))
+        stores.append(pltpu.make_async_copy(buffer, gates_all.at[d, far, rows], sems.at[way]))
     for load in loads:
         load.start()
     for load, store in zip(loads, stores):
@@ -1598,14 +1639,14 @@
     return lax.ppermute(late[0], "dp", across), lax.ppermute(late[1], "dp", beside)
 
 
-def merge_late(gates_all, moved):
+def merge_late(d, gates_all, moved):
     return pl.pallas_call(
-        merge_kernel,
+        functools.partial(merge_kernel, d),
         out_shape=jax.ShapeDtypeStruct(gates_all.shape, BF16),
         in_specs=[ANY_SPEC] * 3,
         out_specs=ANY_SPEC,
         input_output_aliases={2: 0},
-        scratch_shapes=[pltpu.VMEM((2, *moved[0].shape), BF16), pltpu.SemaphoreType.DMA((2, 2))],
+        scratch_shapes=[pltpu.VMEM((2, *moved[0].shape), BF16), pltpu.SemaphoreType.DMA((2,))],
         compiler_params=pltpu.CompilerParams(vmem_limit_bytes=VMEM_LIMIT),
         name="merge_late",
     )(*moved, gates_all)
@@ -1646,34 +1687,36 @@
     )
     widths = filter_widths(lax.axis_index("mp") * local, local, local * lax.axis_size("mp"))
     tap_keep = jnp.arange(TAPS, dtype=jnp.int32)[:, None] < widths[None, :]
-    masked = jnp.where(tap_keep[:, None, :], conv_weight, jnp.zeros_like(conv_weight))
-    excluded = jnp.arange(1, TAPS + 1, dtype=jnp.int32)[:, None] == widths[None, :]
-    masked = jnp.concatenate(
-        [
-            masked.reshape(TAPS * emb, local),
+    row = jnp.arange(128, dtype=jnp.int32)[:, None]
+    taps_padded = jnp.pad(
+        conv_weight.reshape(TAPS * emb, local), ((0, 128 - TAPS * emb), (0, 0))
+    )
+    masked = jnp.where(
+        row < emb * widths[None, :],
+        taps_padded,
+        jnp.where(
+            row == TAPS * emb,
             conv_bias[None, :],
-            jnp.where(excluded, -1e30, 0.0).astype(BF16),
-            jnp.zeros((128 - TAPS * emb - 1 - TAPS, local), BF16),
-        ]
+            jnp.where(row == TAPS * emb + widths[None, :], -1e30, 0.0).astype(BF16),
+        ),
     )
     log_positions = jnp.log((per_token - widths + 1).astype(F32))[None, :]
     w_high = jnp.transpose(highway_weight, (0, 2, 1, 3))
-    b_high = highway_bias.astype(F32)
     (
         base_pair,
         taps,
         peak,
         pooled,
-        features,
         current,
         transform,
         gate,
         features_all,
+        last_own,
         w_input,
         w_state,
     ) = cnn_forward(
         ids,
-        (table, masked, log_positions, w_high, b_high, proj_weight, proj_bias.astype(F32)[None]),
+        (table, masked, log_positions, w_high, highway_bias, proj_weight, proj_bias[None]),
         lstm_input[0],
         lstm_state[0],
     )
@@ -1682,16 +1725,14 @@
     def all_tokens(values):
         return lax.all_gather(values, ("section", "dp"), axis=values.ndim - 2, tiled=True)
 
-    last_features = all_tokens(
-        lax.dynamic_index_in_dim(features[depth_count], lax.axis_index("mp"), 0, False)
-    )
+    last_features = all_tokens(last_own)
     top_seq = jnp.transpose(top_grad, (2, 1, 0, 3))
     live = (jnp.arange(steps, dtype=jnp.int32)[:, None] < row_lengths[None, :]).astype(F32)
     live_seq = jnp.broadcast_to(live[..., None], (steps, rows, 128))
     layer_weights = (
         w_input,
         w_state,
-        lstm_bias[0].reshape(2, -1),
+        lstm_bias[0],
         lstm_proj[0],
     )
     (
@@ -1703,38 +1744,33 @@
         base_shards,
         high_features,
     ) = recurrence(base_pair, live_seq, top_seq, layer_weights, features_all)
-    own_rows = lax.dynamic_slice_in_dim(proj_weight, lax.axis_index("mp") * local, local, 0).T
     (
         all_gates,
         all_projected,
         all_inputs,
         base_full,
         all_mixed,
-        late_first,
-        late_second,
-        conv_grad,
-        table_grad,
+        *late,
+        small,
     ) = (
         cnn_backward(
             base_shards,
             (taps, peak, pooled, current, transform, gate),
-            (own_rows, w_high, masked, ids),
+            (proj_weight, w_high, masked, ids),
             (gates_all, projected_all, x_all, all_states),
         )
     )
     relayed = lax.axis_size("dp") == 4
-    moved = send_late((late_first, late_second)) if relayed else None
-    table_flat = table_grad.reshape(-1)
-    table_rows = -(-(-(-table_flat.shape[0] // local)) // 16) * 16
-    table_flat = jnp.pad(table_flat, (0, table_rows * local - table_flat.shape[0]))
-    small = jnp.concatenate([conv_grad, table_flat.reshape(table_rows, local)]).astype(BF16)
+    if relayed:
+        moved_first = send_late(late[:2])
+        moved_second = send_late(late[2:])
     small = lax.all_gather(small, ("section", "dp"), axis=0)
     small = jnp.sum(small.astype(F32), axis=0)
     conv_weight_grad = jnp.where(
         tap_keep[:, None, :], small[: TAPS * emb].reshape(conv_weight.shape), 0.0
     )
-    table_grad = small[128:].reshape(-1)[: table_grad.size].reshape(table_grad.shape)
-    table_grad = table_grad[:, : char_table.shape[0]].T
+    table_grad = small[128:].reshape(-1, emb, local)
+    table_grad = jnp.transpose(table_grad, (0, 2, 1)).reshape(-1, emb)[: char_table.shape[0]]
     all_base = jnp.transpose(base_full, (0, 1, 3, 2, 4)).reshape(-1, proj_width)
 
     def flat(values):
@@ -1754,12 +1790,20 @@
         all_mixed.reshape(batch, -1, 2 * local),
         2,
     )
+    lefts = [one_piece(all_inputs), one_piece(all_states)]
     if relayed:
-        moved, high_grad, proj_grad = lax.optimization_barrier((moved, high_grad, proj_grad))
-        all_gates = merge_late(all_gates, moved)
-    input_grad, state_grad, bias_grad = weight_grads(
-        [one_piece(all_inputs), one_piece(all_states)], flat(all_gates), 4
-    )
+        moved_first, high_grad, proj_grad, conv_weight_grad, table_grad = lax.optimization_barrier(
+            (moved_first, high_grad, proj_grad, conv_weight_grad, table_grad)
+        )
+        all_gates = merge_late(0, all_gates, moved_first)
+        done = weight_grads(lefts, flat(all_gates), 4, only=0)
+        done, moved_second, all_gates = lax.optimization_barrier((done, moved_second, all_gates))
+        all_gates = merge_late(1, all_gates, moved_second)
+        input_grad, state_grad, bias_grad = weight_grads(
+            lefts, flat(all_gates), 4, only=1, done=done
+        )
+    else:
+        input_grad, state_grad, bias_grad = weight_grads(lefts, flat(all_gates), 4)
     return (
         table_grad,
         conv_weight_grad,

time: 535 us -> 507 us (0.948)
  waiting for transfers between devices: 15.5 us -> 0.08 us
  Pallas kernels: 460 us -> 453 us
    pallas_call x1, Pallas kernels: 250 us -> 233 us  [recurrence(): pl.pallas_call(recurrence_kernel, out_shape=(jax.ShapeDtypeStruct((2, gro...]
    ppermute x1 -> x2, waiting for transfers between devices: 13.9 us -> 0.01 us  [send_late(): lax.ppermute(late[0], 'dp', across)]
    pallas_call x3 -> x4, Pallas kernels: 62.1 us -> 69 us  [weight_grads(): pl.pallas_call(kernel, out_shape=(*[jax.ShapeDtypeStruct((batch, pieces *...]
  transfers between devices with their start and end apart: 5 -> 7, of which waited for: 2 -> 0; matrix products, arithmetic and copies ran while one was open for 3% -> 2% of each run, Pallas kernels for 73% -> 76%
where the time goes in v4:
time: 507 us; the launch traced here: 504 us
  Pallas kernels  453 us (89%)
  local copies, waits for them, and re-layouts  19.5 us (4%)
  between operations  14.2 us (3%)
  other arithmetic  9.44 us (2%)
    pallas_call x1, Pallas kernels, recurrence(): pl.pallas_call(recurrence_kernel, out_shape=(jax.ShapeDtypeStruct((2, gro...  233 us
    pallas_call x1, Pallas kernels, cnn_backward(): pl.pallas_call(cnn_backward_kernel, out_shape=(jax.ShapeDtypeStruct(gates...  75.4 us
    pallas_call x1, Pallas kernels, cnn_forward(): pl.pallas_call(cnn_forward_kernel, out_shape=(jax.ShapeDtypeStruct((2, to...  70.8 us
    pallas_call x4, Pallas kernels, weight_grads(): pl.pallas_call(kernel, out_shape=(*[jax.ShapeDtypeStruct((batch, pieces *...  69 us
    unnamed x18, local copies, waits for them, and re-layouts  10.5 us
  transfers between devices with their start and end apart: 7, of which 0 were waited for; matrix products, arithmetic and copies ran while one was open for 2% of the time, Pallas kernels for 76%

profile of v4, /device:TPU:0, one launch (start us, length us, event | category | flops | bytes accessed | tf_op | source)
XLA Modules:
  0.0 504.3 jit_solution(8418075974880046321)
XLA Ops:
  7.2 0.0 copy-start
  7.2 0.0 all-gather.5.cloned.1.call-start
  7.3 0.6 fusion.20.log_positions
  7.9 0.2 copy-done
  8.1 0.8 reshape.261.ids_ref
  8.9 1.0 copy.42
  9.9 1.6 select_bitcast_fusion
  11.5 0.8 copy.45.masked_ref
  12.3 8.2 %copy.59 = bf16[2,2048,2,512]{3,1,2,0:T(8,128)(2,1)} copy(bf16[2,2048,2,512]{3,2,1,0:T(2,128)(2,1)} %param.21) | data formatting | bytes 16777216 | tf_op args[6]
  20.5 0.1 copy.41
  20.7 0.6 broadcast_in_dim.59.b_proj
  21.2 0.6 pad.16.table_ref
  21.9 70.8 %cnn_forward.1 = (f32[2,160,512]{2,1,0:T(8,128)}, bf16[10,896,128]{2,1,0:T(8,128)(2,1)}, f32[160,1,512]{2,1,0:T(1,128)}, f32[160,512]{1,0:T(8,128)}, f32[2,160,5...) custom-call(s32[10,1,896]{2,1,0:T(1,128)} %reshape.261.ids_ref, ...), custom_call_target="tpu_custom_call" | custom-call | tf_op jit(solution)/shard_map/cnn_forward/pallas_call | solution.py:376
  92.7 0.0 all-gather.5.cloned.1.call-update
  92.7 0.0 all-gather.9.cloned.1.call-start
  92.8 1.0 copy.60
  93.8 0.8 broadcast_in_dim.60.live_ref
  94.6 232.6 %recurrence.1 = (bf16[2,4,20,16,512]{4,3,2,1,0:T(8,128)(2,1)}, bf16[2,4,21,16,512]{4,3,2,1,0:T(8,128)(2,1)}, bf16[2,4,20,16,1024]{4,3,2,1,0:T(8,128)(2,1)}, bf16...) custom-call(f32[2,160,512]{2,1,0:T(8,128)} %get-tuple-element.60.bas, ...), custom_call_target="tpu_custom_call", output_to_operand_aliasing={{6}: (7, {})} | custom-call | tf_op jit(solution)/shard_map/recurrence/pallas_call | solution.py:1453
  327.2 75.4 %cnn_backward.1 = (bf16[2,4,20,16,4096]{4,3,2,1,0:T(8,128)(2,1)}, bf16[2,4,20,16,512]{4,3,2,1,0:T(8,128)(2,1)}, bf16[2,4,20,16,512]{4,3,2,1,0:T(8,128)(2,1)}, bf...) custom-call(bf16[2,160,128]{2,1,0:T(8,128)(2,1)} %get-tuple-element., ...), custom_call_target="tpu_custom_call", output_to_operand_aliasing={{0}: (12, {}), {1}: (13, {}), {2}: (14, {})} | custom-call | tf_op jit(solution)/shard_map/cnn_backward/pallas_call | solution.py:831
  402.6 0.0 all-gather.9.cloned.1.call-update
  402.6 0.0 all-gather.7.cloned.1.call-start
  402.6 0.6 collective-permute-start
  403.2 1.0 collective-permute-start.1
  404.2 1.2 collective-permute-start.2
  405.4 1.4 collective-permute-start.3
  406.8 3.1 copy.49
  409.9 20.0 %weight_grads.4 = (f32[2,2048,2,512]{3,2,1,0:T(2,128)}, f32[2,2,512]{2,1,0:T(2,128)}) custom-call(bf16[2,8,4,160,512]{4,3,2,1,0:T(8,128)(2,1)} %bitcast.67, bf16[2,1280,1024]{2,1,0:T(8,128)(2,1)} %bitcast.84, bf16[2,1280,1024]{2,1,0:T(8,128)(2,1)} %bitcast.85), custom_call_target="tpu_custom_call" | custom-call | flops 10737418240 | bytes 32505856 | tf_op jit(solution)/shard_map/weight_grads/pallas_call | solution.py:1567
  429.8 3.5 fusion.3
  433.3 0.0 all-gather.7.cloned.1.call-update
  433.4 0.8 convert_reduce_fusion
  434.1 8.5 %weight_grads.5 = (f32[2,1024,512]{2,1,0:T(8,128)}, f32[2,1,512]{2,1,0:T(1,128)}) custom-call(bf16[2,4,1,320,1024]{4,3,2,1,0:T(8,128)(2,1)} %bitcast.83, bf16[2,1280,512]{2,1,0:T(8,128)(2,1)} %bitcast.71), custom_call_target="tpu_custom_call" | custom-call | flops 2684354560 | bytes 12058624 | tf_op jit(solution)/shard_map/weight_grads/pallas_call | solution.py:1567
  442.6 1.5 convert_reduce_fusion.1
  444.1 0.6 slice_bitcast_fusion.1
  444.7 0.6 slice.25
  445.3 0.7 broadcast_select_fusion
  446.0 0.0 collective-permute-done.first_ref
  446.0 0.0 collective-permute-done.1.second_ref
  446.1 2.9 merge_late.2.gates_in
  449.0 20.1 %weight_grads.6 = (f32[2,512,4,1024]{3,2,1,0:T(4,128)}, f32[2,512,4,1024]{3,2,1,0:T(4,128)}, f32[2,4,1024]{2,1,0:T(4,128)}) custom-call(bf16[2,4,1,320,512]{4,3,2,1,0:T(8,128)(2,1)} %bitcast.63, bf16[2,4,1,336,512]{4,3,2,1,0:T(8,128)(2,1)} %bitcast.61, bf16[2,1280,4096]{2,1,0:T(8,128)(2,1)} %bitcast.51, bf16[2,1280,4096]{2,1,0:T(8,128)(2,1)} %bitcast.52, ...), custom_call_target="tpu_custom_call" | custom-call | flops 10737418240 | bytes 42991616 | tf_op jit(solution)/shard_map/weight_grads/pallas_call | solution.py:1567
  469.1 0.0 collective-permute-done.2.first_ref
  469.1 0.0 copy-start.3
  469.1 0.0 collective-permute-done.3.second_ref
  469.1 1.0 copy-done.3
  470.1 2.8 merge_late.3
  472.9 0.0 copy-start.1
  473.0 20.4 %weight_grads.7 = (f32[2,512,4,1024]{3,2,1,0:T(4,128)}, f32[2,512,4,1024]{3,2,1,0:T(4,128)}, f32[2,4,1024]{2,1,0:T(4,128)}) custom-call(bf16[2,4,1,320,512]{4,3,2,1,0:T(8,128)(2,1)} %bitcast.64, bf16[2,4,1,336,512]{4,3,2,1,0:T(8,128)(2,1)} %bitcast.62, bf16[2,1280,4096]{2,1,0:T(8,128)(2,1)} %bitcast.55, ...), custom_call_target="tpu_custom_call", output_to_operand_aliasing={{0}: (6, {}), {1}: (7, {}), {2}: (8, {})} | custom-call | flops 10737418240 | bytes 42991616 | tf_op jit(solution)/shard_map/weight_grads/pallas_call | solution.py:1567
  493.4 0.0 all-gather.7.cloned.1.call-done
  493.4 4.2 convert_element_type.181
  (23 shorter events, 0.1 us)
Async XLA Ops:
  7.2 0.9 copy-start
  7.2 422.6 %all-gather.5.cloned.1.call-start = ((), (), s32[]{:S(2)}) async-start(), calls=%async_computation | async-start | bytes 1474560 | tf_op jit(solution)/shard_map/all_gather | solution.py:1726
  12.3 8.2 %copy-start.5 = (bf16[262,16]{0,1:T(8,128)(2,1)S(1)}, bf16[262,16]{0,1:T(8,128)(2,1)}, u32[]{:S(2)}) copy-start(bf16[262,16]{0,1:T(8,128)(2,1)} %param.18) | copy-start | bytes 25156
  12.3 8.4 %copy-start.6 = (bf16[512]{0:T(512)(128)(2,1)S(1)}, bf16[512]{0:T(512)(128)(2,1)}, u32[]{:S(2)}) copy-start(bf16[512]{0:T(512)(128)(2,1)} %param.24) | copy-start | bytes 3076
  21.9 70.9 %copy-start.4 = (bf16[16,20,2,512]{3,2,1,0:T(2,128)(2,1)S(1)}, bf16[16,20,2,512]{3,2,1,0:T(2,128)(2,1)}, u32[]{:S(2)}) copy-start(bf16[16,20,2,512]{3,2,1,0:T(2,128)(2,1)} %param.17) | copy-start | bytes 1966084
  21.9 71.9 %copy-start.7 = (s32[16]{0:T(128)S(1)}, s32[16]{0:T(128)}, u32[]{:S(2)}) copy-start(s32[16]{0:T(128)} %param.16) | copy-start | bytes 196
  92.7 349.9 %all-gather.9.cloned.1.call-start = ((), (), s32[]{:S(2)}) async-start(), calls=%async_computation.2 | async-start | bytes 1327104 | tf_op jit(solution)/shard_map/all_gather | solution.py:1767
  402.6 90.8 %all-gather.7.cloned.1.call-start = ((), (), s32[]{:S(2)}) async-start(), calls=%async_computation.1 | async-start | bytes 2621440 | tf_op jit(solution)/shard_map/all_gather | solution.py:1783
  402.6 43.4 %collective-permute-start = (bf16[10,16,4096]{2,1,0:T(8,128)(2,1)}, bf16[10,16,4096]{2,1,0:T(8,128)(2,1)}, u32[]{:S(2)}, u32[]{:S(2)}) collective-permute-start(bf16[10,16,4096]{2,1,0:T(8,128)(2,1)} %get-tuple-element.75), channel_id=1, source_target_pairs={{0,2},{1,3},{2,0},{3,1},{4,6},{5,7},{6,4},{7,5},{8,10},{9,11},{10,... | collective-permute-start | bytes 3932168 | tf_op jit(solution)/shard_map/ppermute | solution.py:1639
  403.2 42.8 %collective-permute-start.1 = (bf16[10,16,4096]{2,1,0:T(8,128)(2,1)}, bf16[10,16,4096]{2,1,0:T(8,128)(2,1)}, u32[]{:S(2)}, u32[]{:S(2)}) collective-permute-start(bf16[10,16,4096]{2,1,0:T(8,128)(2,1)} %get-tuple-element.76), channel_id=1, source_target_pairs={{0,1},{1,0},{2,3},{3,2},{4,5},{5,4},{6,7},{7,6},{8,9},{9,8},{10,11... | collective-permute-start | bytes 3932168 | tf_op jit(solution)/shard_map/ppermute | solution.py:1639
  404.2 64.9 %collective-permute-start.2 = (bf16[10,16,4096]{2,1,0:T(8,128)(2,1)}, bf16[10,16,4096]{2,1,0:T(8,128)(2,1)S(1)}, u32[]{:S(2)}, u32[]{:S(2)}) collective-permute-start(bf16[10,16,4096]{2,1,0:T(8,128)(2,1)} %get-tuple-element.97), channel_id=1, source_target_pairs={{0,2},{1,3},{2,0},{3,1},{4,6},{5,7},{6,4},{7,5},{8,10},{9,11},{10,... | collective-permute-start | bytes 3932168 | tf_op jit(solution)/shard_map/ppermute | solution.py:1639
  405.4 63.7 %collective-permute-start.3 = (bf16[10,16,4096]{2,1,0:T(8,128)(2,1)}, bf16[10,16,4096]{2,1,0:T(8,128)(2,1)}, u32[]{:S(2)}, u32[]{:S(2)}) collective-permute-start(bf16[10,16,4096]{2,1,0:T(8,128)(2,1)} %get-tuple-element.98), channel_id=1, source_target_pairs={{0,1},{1,0},{2,3},{3,2},{4,5},{5,4},{6,7},{7,6},{8,9},{9,8},{10,11... | collective-permute-start | bytes 3932168 | tf_op jit(solution)/shard_map/ppermute | solution.py:1639
  429.8 3.5 copy-start.2
  469.1 1.1 copy-start.3
  472.9 24.6 %copy-start.1 = (s32[16,20,50]{2,0,1:T(8,128)S(1)}, s32[16,20,50]{2,0,1:T(8,128)}, u32[]{:S(2)}) copy-start(s32[16,20,50]{2,0,1:T(8,128)} %param.15) | copy-start | bytes 192004
Sparse Core Ops, SparseCore 0:
  92.8 36.1 all-gather.4
  402.7 26.6 all-gather.8
  433.5 43.4 all-gather.6

commit v5 on v4

--- a/solution.py
+++ b/solution.py
@@ -80,10 +80,10 @@
     flags_ref,
     masked_ref,
     log_positions,
-    w_high,
     b_high,
-    w_proj,
     b_proj,
+    high_ref,
+    proj_ref,
     input_ref,
     state_ref,
     base_out,
@@ -98,6 +98,8 @@
     input_out,
     state_out,
     features,
+    w_high,
+    w_proj,
     raw,
     turned,
     send_sem,
@@ -107,10 +109,11 @@
     row_send,
     row_recv,
     own_sem,
+    raw_sem,
+    turned_sem,
+    load_sem,
     relay_send,
     relay_recv,
-    raw_sem,
-    turned_sem,
 ):
     count = lax.axis_size("mp")
     me = lax.axis_index("mp")
@@ -122,6 +125,12 @@
     half = tokens // 2
     emb = 16
     block = min(256, local)
+    loads = [
+        pltpu.make_async_copy(high_ref, w_high, load_sem.at[0]),
+        pltpu.make_async_copy(proj_ref, w_proj, load_sem.at[1]),
+    ]
+    for load in loads:
+        load.start()
     groups = lax.axis_size("dp")
     group = lax.axis_index("dp")
     others = [lax.rem(group + j, groups) for j in range(1, groups)]
@@ -150,7 +159,7 @@
     def pass_rows(depth):
         for j in range(len(near)):
             give_rows(depth, j, origin[j]).wait_recv()
-        if relayed and depth + 1 < depth_count:
+        if relayed:
             for way in range(2):
                 relay_rows(depth, way, beside if way == 0 else across).start()
 
@@ -276,14 +285,29 @@
             rows = pool_chunk(part * (half // CHUNK) + i)
             send(0, part, rows, True)
 
+    for load in loads:
+        load.wait()
+    stops = [2, 2, 6, 9, 13, 16]
+    turned_to = [0]
+
+    def turn_some():
+        stop = units * stops[min(turn_count[0], len(stops) - 1)] // 16
+        turn_count[0] += 1
+        if stop > turned_to[0]:
+            turn_units(turned_to[0], stop)
+            turned_to[0] = stop
+
+    turn_count = [0]
     for depth in range(depth_count):
         for part in range(2):
             rows = pl.ds(part * half, half)
+            turn_some()
             receive(depth, part)
             if part == 1:
                 own_rows(depth).start()
-                for j in range(len(near)):
-                    give_rows(depth, j, group).start()
+                if depth + 1 < depth_count:
+                    for j in range(len(near)):
+                        give_rows(depth, j, group).start()
             mixed = []
             for g in range(2):
                 total = jnp.broadcast_to(b_high[depth, g : g + 1, :].astype(F32), (half, local))
@@ -309,7 +333,6 @@
             send(depth + 1, part, rows, True)
         if depth >= 1:
             pass_rows(depth - 1)
-        turn_units(depth * units * 3 // (4 * depth_count), (depth + 1) * units * 3 // (4 * depth_count))
 
     def give():
         return remote(
@@ -322,6 +345,7 @@
 
     for part in range(2):
         rows = pl.ds(part * half, half)
+        turn_some()
         receive(depth_count, part)
         total = jnp.broadcast_to(b_proj[...].astype(F32), (half, w_proj.shape[1]))
         for p in range(count):
@@ -332,8 +356,7 @@
             )
         base_out[section, rows, :] = total
     give().start()
-    turn_units(units * 3 // 4, units)
-    pass_rows(depth_count - 1)
+    turn_units(turned_to[0], units)
     for depth in range(depth_count + 1):
         for part in range(2):
             send(depth, part, pl.ds(part * half, half), False)
@@ -347,12 +370,13 @@
     ).wait_recv()
     for depth in range(depth_count):
         own_rows(depth).wait()
-        for j in range(len(near)):
-            give_rows(depth, j, group).wait_send()
-        if relayed and depth + 1 < depth_count:
-            for way in range(2):
-                relay_rows(depth, way, beside if way == 0 else across).wait_send()
-                relay_rows(depth, way, far).wait_recv()
+        if depth + 1 < depth_count:
+            for j in range(len(near)):
+                give_rows(depth, j, group).wait_send()
+            if relayed:
+                for way in range(2):
+                    relay_rows(depth, way, beside if way == 0 else across).wait_send()
+                    relay_rows(depth, way, far).wait_recv()
     for unit in range(units - 2, units):
         deliver(unit, False)
 
@@ -388,10 +412,12 @@
             jax.ShapeDtypeStruct((directions, gate_blocks, in_width, cell_columns), BF16),
             jax.ShapeDtypeStruct((directions, gate_blocks, in_width, cell_columns), BF16),
         ),
-        in_specs=[VMEM_SPEC] * 9 + [ANY_SPEC] * 2,
+        in_specs=[VMEM_SPEC] * 7 + [ANY_SPEC] * 4,
         out_specs=(*[VMEM_SPEC] * 7, ANY_SPEC, VMEM_SPEC, *[ANY_SPEC] * 2),
         scratch_shapes=[
             pltpu.VMEM((depth_count + 1, count, tokens, local), BF16),
+            pltpu.VMEM(w_high.shape, BF16),
+            pltpu.VMEM(w_proj.shape, BF16),
             pltpu.VMEM((2, TURN, gate_blocks, cell_columns), BF16),
             pltpu.VMEM((2, gate_blocks, TURN, cell_columns), BF16),
             dma((depth_count + 1, 2, count - 1)),
@@ -401,10 +427,11 @@
             dma((depth_count, groups - 1)),
             dma((depth_count, groups - 1)),
             dma((depth_count,)),
+            dma((2,)),
+            dma((2,)),
+            dma((2,)),
             dma((depth_count, 2)),
             dma((depth_count, 2)),
-            dma((2,)),
-            dma((2,)),
         ],
         compiler_params=pltpu.CompilerParams(
             collective_id=1, has_side_effects=True, vmem_limit_bytes=VMEM_LIMIT
@@ -416,10 +443,10 @@
         jnp.asarray(flags.astype(np.float32)),
         masked,
         log_positions,
+        b_high,
+        b_proj,
         w_high,
-        b_high,
         w_proj,
-        b_proj,
         lstm_input,
         lstm_state,
     )
@@ -428,23 +455,25 @@
 def cnn_backward_kernel(
     base_ref,
     own_ref,
-    w_high,
     current_ref,
     transform_ref,
     gate_ref,
     peak_ref,
     pooled_ref,
-    taps_ref,
     masked_ref,
     masked_t,
     ids_ref,
+    high_ref,
+    taps_hbm,
     gates_in,
     projected_in,
     x_in,
+    hidden_in,
     state_all,
     gates_all,
     projected_all,
     x_all,
+    hidden_all,
     base_full,
     mixed_all,
     late_a,
@@ -452,10 +481,14 @@
     late_c,
     late_d,
     small_out,
+    w_high,
+    taps_ref,
+    load_sem,
     conv_out,
     mixed_out,
     late_buf,
     base_all,
+    base_rows,
     table_sum,
     table_all,
     grad_current,
@@ -495,6 +528,12 @@
     depth_count, tokens, local = current_ref.shape
     steps = x_all.shape[2]
     chunks, chunk_rows, _ = taps_ref.shape
+    loads = [
+        pltpu.make_async_copy(high_ref, w_high, load_sem.at[0]),
+        pltpu.make_async_copy(taps_hbm, taps_ref, load_sem.at[1]),
+    ]
+    for load in loads:
+        load.start()
     padded = chunk_rows // CHUNK
     emb = 16
     vocabulary = -(-CHARS // 8) * 8
@@ -522,12 +561,17 @@
     near = [beside, across] if relayed else others
     origin = near if relayed else others[::-1]
 
-    def relay(way, slot):
+    def relay(kind, way, slot):
+        head = steps * 7 // 10
+        if kind == 0:
+            block = projected_all.at[way, slot]
+        else:
+            block = hidden_all.at[way, slot, pl.ds(head, steps - head)]
         return remote(
-            projected_all.at[way, slot],
-            projected_all.at[way, slot],
-            relay_send.at[way],
-            relay_recv.at[way],
+            block,
+            block,
+            relay_send.at[kind, way],
+            relay_recv.at[kind, way],
             {"dp": across if way == 0 else beside},
         )
 
@@ -590,12 +634,15 @@
     def _():
         base_arrival(me).wait_recv()
 
-    keep = pltpu.make_async_copy(base_all, base_full.at[section, group], full_sem)
+    wide = base_all.shape[2]
+    for p in range(count):
+        base_rows[:, p * wide : (p + 1) * wide] = base_all[p]
+    keep = pltpu.make_async_copy(base_rows, base_full.at[section, group], full_sem)
     keep.start()
 
     def base_row(j, slot):
         return remote(
-            base_all,
+            base_rows,
             base_full.at[section, slot],
             row_send.at[j],
             row_recv.at[j],
@@ -643,7 +690,6 @@
             mixed_row(depth, j, others[groups - 2 - j]).wait_recv()
         share_mixed(depth, section).start()
 
-    wide = base_all.shape[2]
     own_rows = pl.ds(pl.multiple_of(me * local, local), local)
     total = jnp.zeros((tokens, local), F32)
     for p in range(count):
@@ -677,6 +723,8 @@
         ]
         return parts[0] + parts[1]
 
+    for load in loads:
+        load.wait()
     for depth in range(depth_count - 1, -1, -1):
         transform = transform_ref[depth]
         gate = gate_ref[depth]
@@ -692,8 +740,9 @@
         for j in range(groups - 1):
             mixed_row(depth, j, group).start()
         if relayed and depth == depth_count - 1:
-            for way in range(2):
-                relay(way, beside if way == 0 else across).start()
+            for kind in range(2):
+                for way in range(2):
+                    relay(kind, way, beside if way == 0 else across).start()
         for j, peer in enumerate(peers):
             outgoing[depth, j] = back(depth, peer).astype(BF16)
             send_sum(depth, peer, j).start()
@@ -804,9 +853,10 @@
         lift().wait_recv()
 
     if relayed:
-        for way in range(2):
-            relay(way, beside if way == 0 else across).wait_send()
-            relay(way, far).wait_recv()
+        for kind in range(2):
+            for way in range(2):
+                relay(kind, way, beside if way == 0 else across).wait_send()
+                relay(kind, way, far).wait_recv()
         for copy in late_stores:
             copy.wait()
 
@@ -820,7 +870,7 @@
 def cnn_backward(base_shards, saved, weights, rows_all):
     w_proj, w_high, masked, ids = weights
     taps, peak, pooled, current, transform, gate = saved
-    gates_all, projected_all, x_all, state_all = rows_all
+    gates_all, projected_all, x_all, hidden_all, state_all = rows_all
     depth_count, tokens, local = current.shape
     count = lax.axis_size("mp")
     groups = lax.axis_size("dp")
@@ -834,19 +884,24 @@
             jax.ShapeDtypeStruct(gates_all.shape, BF16),
             jax.ShapeDtypeStruct(projected_all.shape, BF16),
             jax.ShapeDtypeStruct(x_all.shape, BF16),
-            jax.ShapeDtypeStruct((2, groups, count, tokens, base_shards.shape[2]), BF16),
+            jax.ShapeDtypeStruct(hidden_all.shape, BF16),
+            jax.ShapeDtypeStruct((2, groups, tokens, count * base_shards.shape[2]), BF16),
             jax.ShapeDtypeStruct((depth_count, 2, groups, tokens, 2 * local), BF16),
             *[jax.ShapeDtypeStruct(late, BF16)] * 4,
             jax.ShapeDtypeStruct((128 + 16 * max(1, vocabulary // local), local), BF16),
         ),
-        in_specs=[VMEM_SPEC] * 12 + [ANY_SPEC] * 4,
-        out_specs=(*[ANY_SPEC] * 9, VMEM_SPEC),
-        input_output_aliases={12: 0, 13: 1, 14: 2},
+        in_specs=[VMEM_SPEC] * 10 + [ANY_SPEC] * 7,
+        out_specs=(*[ANY_SPEC] * 10, VMEM_SPEC),
+        input_output_aliases={12: 0, 13: 1, 14: 2, 15: 3},
         scratch_shapes=[
+            pltpu.VMEM(w_high.shape, BF16),
+            pltpu.VMEM(taps.shape, BF16),
+            dma((2,)),
             pltpu.VMEM((128, local), F32),
             pltpu.VMEM((depth_count, tokens, 2 * local), BF16),
             pltpu.VMEM((4, *late), BF16),
             pltpu.VMEM((count, tokens, base_shards.shape[2]), BF16),
+            pltpu.VMEM((tokens, count * base_shards.shape[2]), BF16),
             pltpu.VMEM((vocabulary, 128), F32),
             pltpu.VMEM((count, 16, vocabulary), F32),
             pltpu.VMEM((tokens, local), F32),
@@ -857,8 +912,8 @@
             dma((depth_count, count - 1)),
             dma((depth_count, count)),
             dma,
-            dma((2,)),
-            dma((2,)),
+            dma((2, 2)),
+            dma((2, 2)),
             dma,
             dma,
             dma((groups - 1,)),
@@ -884,19 +939,20 @@
     )(
         base_shards,
         w_proj,
-        w_high,
         current,
         transform,
         gate,
         peak,
         pooled,
-        taps,
         masked,
         jnp.pad(masked[: 16 * TAPS], ((0, 128 - 16 * TAPS), (0, 0))).T,
         ids,
+        w_high,
+        taps,
         gates_all,
         projected_all,
         x_all,
+        hidden_all,
         state_all,
     )
 
@@ -905,10 +961,10 @@
     base_ref,
     live_ref,
     top_ref,
-    w_in,
-    w_state,
     bias_ref,
     proj_ref,
+    in_ref,
+    state_ref,
     features_in,
     x_all,
     state_all,
@@ -944,6 +1000,9 @@
     own_sem,
     row_send,
     row_recv,
+    w_in,
+    w_state,
+    load_sem,
     w_in_t,
     w_state_t,
     proj_t,
@@ -956,6 +1015,10 @@
     share_recv,
     relay_send,
     relay_recv,
+    feature_send,
+    feature_recv,
+    hidden_send,
+    hidden_recv,
 ):
     count = lax.axis_size("mp")
     me = lax.axis_index("mp")
@@ -971,6 +1034,14 @@
     beside = group + 1 - 2 * lax.rem(group, 2)
     across = lax.rem(group + 2, 4)
     near = [beside, across] if relayed else others
+    loads = [
+        [pltpu.make_async_copy(source.at[d], target.at[d], load_sem.at[i, d]) for d in range(2)]
+        for i, (source, target) in enumerate(((in_ref, w_in), (state_ref, w_state)))
+    ]
+    for d in range(2):
+        loads[0][d].start()
+    for d in range(2):
+        loads[1][d].start()
 
     barrier = pltpu.get_barrier_semaphore()
     for peer in peers:
@@ -991,20 +1062,41 @@
 
     pieces = features_all.shape[3]
 
+    last_depth = features_all.shape[0] - 1
+
+    def give_features(j, slot):
+        return remote(
+            features_all.at[last_depth, section, slot],
+            features_all.at[last_depth, section, slot],
+            feature_send.at[j],
+            feature_recv.at[j],
+            {"dp": near[j]},
+        )
+
     def relay_features(way, slot):
         half = pl.ds(way * (pieces // 2), pieces // 2)
-        depth = features_all.shape[0] - 1
+        block = features_all.at[last_depth, section, slot, half]
         return remote(
-            features_all.at[depth, section, slot, half],
-            features_all.at[depth, section, slot, half],
+            block,
+            block,
             relay_send.at[way],
             relay_recv.at[way],
             {"dp": across if way == 0 else beside},
         )
 
-    if relayed:
-        for way in range(2):
-            relay_features(way, beside if way == 0 else across).start()
+    def start_relays():
+        if relayed:
+            for way in range(2):
+                relay_features(way, beside if way == 0 else across).start()
+
+    def finish_relays():
+        if relayed:
+            for way in range(2):
+                relay_features(way, beside if way == 0 else across).wait_send()
+                relay_features(way, 3 - group).wait_recv()
+
+    for j in range(len(near)):
+        give_features(j, group).start()
 
     def wide(values, width):
         return jnp.concatenate([values] * (width // values.shape[1]), axis=1)
@@ -1087,6 +1179,25 @@
         back = len(targets) - 1 - j
         return targets[j] if relayed and len(targets) == 2 else targets[back]
 
+    head = steps * 7 // 10
+
+    def relay_hidden(way, slot):
+        block = hidden_all.at[way, slot, pl.ds(0, head)]
+        return remote(
+            block,
+            block,
+            hidden_send.at[way],
+            hidden_recv.at[way],
+            {"dp": across if way == 0 else beside},
+        )
+
+    def finish_hidden(kind, some):
+        for j, other in enumerate(near):
+            target = hidden_all.at[:, from_peer(j, near), some]
+            copy = row(kind, hidden_out.at[:, some], target, j, other)
+            copy.wait_send()
+            copy.wait_recv()
+
     def time_of(d, k):
         return k if d == 0 else steps - 1 - k
 
@@ -1102,7 +1213,7 @@
                 x_out[d, time_of(d, t)] = x
 
         for j, other in enumerate(others):
-            row(1, x_out, x_all.at[:, group], j, other).start()
+            row(1, x_out.at[0], x_all.at[0, group], j, other).start()
 
     for d in range(2):
         state_out[d, 0] = jnp.zeros(state_out.shape[2:], BF16)
@@ -1162,8 +1273,9 @@
             hidden_out[d, k, :, own] = (out_gate * jnp.tanh(cell_new)).astype(BF16)
         part = jnp.dot(hidden_out[d, k], proj_ref[d], preferred_element_type=F32)
         exchange_start(parts, send_sem, recv_sem, d, lax.rem(k, 2), part)
-        for j, other in enumerate(others):
-            row(2, hidden_out.at[d, k], hidden_all.at[d, group, k], j, other).start()
+        for j, other in enumerate(near):
+            kind = 2 + 3 * (k // head)
+            row(kind, hidden_out.at[d, k], hidden_all.at[d, group, k], j, other).start()
 
     def forward_state(d, k):
         total = exchange_wait(parts, send_sem, recv_sem, d, lax.rem(k, 2))
@@ -1185,8 +1297,10 @@
 
     units = 4 * cell_count // chunk
     for d in range(2):
+        loads[0][d].wait()
         input_part(d, 0)
     for d in range(2):
+        loads[1][d].wait()
         forward_cells(d, 0)
     for d in range(2):
         input_part(d, 1)
@@ -1206,6 +1320,20 @@
         def _():
             turn_weights(k - 1)
 
+        @pl.when(k == steps - 3)
+        def _():
+            finish_hidden(2, pl.ds(0, head))
+            if relayed:
+                for way in range(2):
+                    relay_hidden(way, beside if way == 0 else across).start()
+
+        @pl.when(k == steps - 5)
+        def _():
+            for j in range(len(near)):
+                give_features(j, group).wait_send()
+                give_features(j, from_peer(j, near)).wait_recv()
+            start_relays()
+
         @pl.when(k <= cell_count // 128)
         def _():
             turn_proj(k - 1)
@@ -1214,11 +1342,6 @@
         turn_weights(unit)
     for d in range(2):
         forward_state(d, steps - 1)
-    if relayed:
-        for way in range(2):
-            relay_features(way, beside if way == 0 else across).wait_send()
-            relay_features(way, 3 - group).wait_recv()
-    share_features(section).start()
 
     @pl.when(section == 0)
     def _():
@@ -1350,6 +1473,15 @@
         for d in range(2):
             backward_input(d, k)
 
+        @pl.when(tick == 5)
+        def _():
+            finish_relays()
+            share_features(section).start()
+            if relayed:
+                for way in range(2):
+                    relay_hidden(way, beside if way == 0 else across).wait_send()
+                    relay_hidden(way, 3 - group).wait_recv()
+
     for d in range(2):
         for k in range(min(SLOTS, steps)):
             gates_copy(d, k, k % SLOTS).wait()
@@ -1379,21 +1511,21 @@
     rest = pl.ds(1, steps)
     for j, other in enumerate(others):
         source = from_peer(j, others)
-        hidden_row = row(2, hidden_out, hidden_all.at[:, source], j, other)
         state_row = row(3, state_out.at[:, rest], state_all.at[:, source, rest], j, other)
-        for copy in (hidden_row, state_row):
-            copy.wait_send()
-            copy.wait_recv()
+        state_row.wait_send()
+        state_row.wait_recv()
+
+    finish_hidden(5, pl.ds(head, steps - head))
 
     for copy in own:
         copy.wait()
 
     @pl.when(section == 0)
     def _():
-        mine = pltpu.make_async_copy(x_out, x_all.at[:, group], base_sem)
+        mine = pltpu.make_async_copy(x_out.at[0], x_all.at[0, group], base_sem)
         mine.start()
         for j, other in enumerate(others):
-            copy = row(1, x_out, x_all.at[:, from_peer(j, others)], j, other)
+            copy = row(1, x_out.at[0], x_all.at[0, from_peer(j, others)], j, other)
             copy.wait_send()
             copy.wait_recv()
         mine.wait()
@@ -1443,12 +1575,7 @@
     cell_count = proj.shape[1]
     count = lax.axis_size("mp")
     groups = lax.axis_size("dp")
-    weights = (
-        w_in,
-        w_state,
-        bias,
-        proj,
-    )
+    weights = (bias, proj, w_in, w_state)
     dma = pltpu.SemaphoreType.DMA
     return pl.pallas_call(
         recurrence_kernel,
@@ -1461,7 +1588,7 @@
             jax.ShapeDtypeStruct((2, steps * rows // 2, width // count), BF16),
             jax.ShapeDtypeStruct(features_all.shape, BF16),
         ),
-        in_specs=[VMEM_SPEC] * 7 + [ANY_SPEC],
+        in_specs=[VMEM_SPEC] * 5 + [ANY_SPEC] * 3,
         out_specs=(*[ANY_SPEC] * 5, VMEM_SPEC, ANY_SPEC),
         input_output_aliases={7: 6},
         scratch_shapes=[
@@ -1490,8 +1617,11 @@
             dma((2, SLOTS)),
             dma((2, SLOTS, groups - 1)),
             dma((groups + 2,)),
-            dma((5, groups - 1)),
-            dma((5, groups - 1)),
+            dma((6, groups - 1)),
+            dma((6, groups - 1)),
+            pltpu.VMEM(w_in.shape, BF16),
+            pltpu.VMEM(w_state.shape, BF16),
+            dma((2, 2)),
             pltpu.VMEM((2, 4 * cell_count, width), BF16),
             pltpu.VMEM((2, 4 * cell_count, width), BF16),
             pltpu.VMEM((2, width, cell_count), BF16),
@@ -1504,6 +1634,10 @@
             dma,
             dma((2,)),
             dma((2,)),
+            dma((groups - 1,)),
+            dma((groups - 1,)),
+            dma((2,)),
+            dma((2,)),
         ],
         compiler_params=pltpu.CompilerParams(
             collective_id=0, has_side_effects=True, vmem_limit_bytes=VMEM_LIMIT
@@ -1513,7 +1647,8 @@
 
 
 def weight_grads(lefts, right, parts, only=None, done=()):
-    batch, outer, pieces, inner, size = lefts[0].shape
+    _, outer, pieces, inner, size = lefts[0].shape
+    batch = right.shape[0]
     tokens = right.shape[1]
     inner = tokens // outer
     columns = right.shape[2] // parts
@@ -1526,6 +1661,9 @@
 
     def entry(b):
         return b if only is None else only
+
+    def left_entry(left, b):
+        return entry(b) if left.shape[0] == batch else 0
 
 
     def kernel(*refs):
@@ -1578,8 +1716,13 @@
         grid=(chosen, pieces, blocks),
         in_specs=[
             *[
-                pl.BlockSpec((1, outer, 1, inner, size), lambda b, p, n: (entry(b), 0, p, 0, 0))
-                for _ in lefts
+                pl.BlockSpec(
+                    (1, outer, 1, inner, size),
+                    functools.partial(
+                        lambda left, b, p, n: (left_entry(left, b), 0, p, 0, 0), left
+                    ),
+                )
+                for left in lefts
             ],
             *[
                 pl.BlockSpec(
@@ -1738,7 +1881,7 @@
     (
         x_all,
         all_states,
-        all_hidden,
+        hidden_all,
         gates_all,
         projected_all,
         base_shards,
@@ -1748,6 +1891,7 @@
         all_gates,
         all_projected,
         all_inputs,
+        all_hidden,
         base_full,
         all_mixed,
         *late,
@@ -1757,7 +1901,7 @@
             base_shards,
             (taps, peak, pooled, current, transform, gate),
             (proj_weight, w_high, masked, ids),
-            (gates_all, projected_all, x_all, all_states),
+            (gates_all, projected_all, x_all, hidden_all, all_states),
         )
     )
     relayed = lax.axis_size("dp") == 4
@@ -1771,7 +1915,7 @@
     )
     table_grad = small[128:].reshape(-1, emb, local)
     table_grad = jnp.transpose(table_grad, (0, 2, 1)).reshape(-1, emb)[: char_table.shape[0]]
-    all_base = jnp.transpose(base_full, (0, 1, 3, 2, 4)).reshape(-1, proj_width)
+    all_base = base_full.reshape(-1, proj_width)
 
     def flat(values):
         return values.reshape(2, -1, values.shape[4])
@@ -1790,20 +1934,26 @@
         all_mixed.reshape(batch, -1, 2 * local),
         2,
     )
-    lefts = [one_piece(all_inputs), one_piece(all_states)]
+    states = one_piece(all_states)
+    turned_inputs = jnp.where(section == 0, jnp.flip(all_inputs[0], axis=1), all_inputs[1])[None]
     if relayed:
-        moved_first, high_grad, proj_grad, conv_weight_grad, table_grad = lax.optimization_barrier(
-            (moved_first, high_grad, proj_grad, conv_weight_grad, table_grad)
+        moved_first, high_grad, proj_grad, conv_weight_grad, table_grad, turned_inputs = (
+            lax.optimization_barrier(
+                (moved_first, high_grad, proj_grad, conv_weight_grad, table_grad, turned_inputs)
+            )
         )
         all_gates = merge_late(0, all_gates, moved_first)
-        done = weight_grads(lefts, flat(all_gates), 4, only=0)
+        done = weight_grads([one_piece(all_inputs), states], flat(all_gates), 4, only=0)
         done, moved_second, all_gates = lax.optimization_barrier((done, moved_second, all_gates))
         all_gates = merge_late(1, all_gates, moved_second)
         input_grad, state_grad, bias_grad = weight_grads(
-            lefts, flat(all_gates), 4, only=1, done=done
+            [one_piece(turned_inputs), states], flat(all_gates), 4, only=1, done=done
         )
     else:
-        input_grad, state_grad, bias_grad = weight_grads(lefts, flat(all_gates), 4)
+        both = jnp.concatenate([all_inputs[:1], turned_inputs])
+        input_grad, state_grad, bias_grad = weight_grads(
+            [one_piece(both), states], flat(all_gates), 4
+        )
     return (
         table_grad,
         conv_weight_grad,

time: 507 us -> 494 us (0.974)
  Pallas kernels: 453 us -> 437 us
    pallas_call x1, Pallas kernels: 70.8 us -> 60.6 us  [cnn_forward(): pl.pallas_call(cnn_forward_kernel, out_shape=(jax.ShapeDtypeStruct((2, to...]
    unnamed x18 -> x16, local copies, waits for them, and re-layouts: 10.5 us -> 9.46 us
  transfers between devices with their start and end apart: 7 -> 7, of which waited for: 0 -> 0; matrix products, arithmetic and copies ran while one was open for 2% -> 3% of each run, Pallas kernels for 76% -> 77%
where the time goes in v5:
time: 494 us; the launch traced here: 491 us
  Pallas kernels  437 us (88%)
  local copies, waits for them, and re-layouts  17.8 us (4%)
  between operations  14.2 us (3%)
  other arithmetic  13.8 us (3%)
    pallas_call x1, Pallas kernels, recurrence(): pl.pallas_call(recurrence_kernel, out_shape=(jax.ShapeDtypeStruct((2, gro...  228 us
    pallas_call x1, Pallas kernels, cnn_backward(): pl.pallas_call(cnn_backward_kernel, out_shape=(jax.ShapeDtypeStruct(gates...  74.3 us
    pallas_call x4, Pallas kernels, weight_grads(): pl.pallas_call(kernel, out_shape=(*[jax.ShapeDtypeStruct((batch, pieces *...  68.3 us
    pallas_call x1, Pallas kernels, cnn_forward(): pl.pallas_call(cnn_forward_kernel, out_shape=(jax.ShapeDtypeStruct((2, to...  60.6 us
  transfers between devices with their start and end apart: 7, of which 0 were waited for; matrix products, arithmetic and copies ran while one was open for 3% of the time, Pallas kernels for 77%

profile of v5, /device:TPU:0, one launch (start us, length us, event | category | flops | bytes accessed | tf_op | source)
XLA Modules:
  0.0 490.6 jit_solution(3076116316376831195)
XLA Ops:
  7.2 0.0 copy-start
  7.2 0.0 all-gather.5.cloned.1.call-start
  7.3 0.6 fusion.15.log_positions
  7.9 0.2 copy-done
  8.1 0.8 reshape.264.ids_ref
  8.9 1.0 copy.43
  9.9 1.6 select_bitcast_fusion
  11.5 0.8 copy.46.masked_ref
  12.3 8.2 %copy.52 = bf16[2,2048,2,512]{3,1,2,0:T(8,128)(2,1)} copy(bf16[2,2048,2,512]{3,2,1,0:T(2,128)(2,1)} %param.21) | data formatting | bytes 16777216 | tf_op args[6]
  20.5 0.1 copy.42
  20.7 0.6 broadcast_in_dim.62.b_proj
  21.2 0.6 pad.16.table_ref
  21.9 60.6 %cnn_forward.1 = (f32[2,160,512]{2,1,0:T(8,128)}, bf16[10,896,128]{2,1,0:T(8,128)(2,1)}, f32[160,1,512]{2,1,0:T(1,128)}, f32[160,512]{1,0:T(8,128)}, f32[2,160,5...) custom-call(s32[10,1,896]{2,1,0:T(1,128)} %reshape.264.ids_ref, ...), custom_call_target="tpu_custom_call" | custom-call | tf_op jit(solution)/shard_map/cnn_forward/pallas_call | solution.py:400
  82.5 0.0 all-gather.5.cloned.1.call-update
  82.6 0.0 all-gather.9.cloned.1.call-start
  82.6 1.0 copy.53
  83.6 0.0 copy-done.6
  83.7 0.8 broadcast_in_dim.63.live_ref
  84.4 227.8 %recurrence.1 = (bf16[2,4,20,16,512]{4,3,2,1,0:T(8,128)(2,1)}, bf16[2,4,21,16,512]{4,3,2,1,0:T(8,128)(2,1)}, bf16[2,4,20,16,1024]{4,3,2,1,0:T(8,128)(2,1)}, bf16...) custom-call(f32[2,160,512]{2,1,0:T(8,128)} %get-tuple-element.62.bas, ...), custom_call_target="tpu_custom_call", output_to_operand_aliasing={{6}: (7, {})} | custom-call | tf_op jit(solution)/shard_map/recurrence/pallas_call | solution.py:1580
  312.3 74.3 %cnn_backward.1 = (bf16[2,4,20,16,4096]{4,3,2,1,0:T(8,128)(2,1)}, bf16[2,4,20,16,512]{4,3,2,1,0:T(8,128)(2,1)}, bf16[2,4,20,16,512]{4,3,2,1,0:T(8,128)(2,1)}, bf...) custom-call(bf16[2,160,128]{2,1,0:T(8,128)(2,1)} %get-tuple-element., ...), custom_call_target="tpu_custom_call", output_to_operand_aliasing={{0}: (12, {}), {1}: (13, {}), {2}: (14, {}), {3}: (15, {})} | custom-call | tf_op jit(solution)/shard_map/cnn_backward/pallas_call | solution.py:881
  386.6 1.1 collective-permute-start
  387.6 1.1 collective-permute-start.1
  388.7 1.4 collective-permute-start.2
  390.1 0.6 collective-permute-start.3
  390.7 0.0 all-gather.9.cloned.1.call-update
  390.7 0.3 all-gather.7.cloned.1.call-start
  391.0 2.1 convert_reduce_fusion
  393.1 8.5 %weight_grads.5 = (f32[2,1024,512]{2,1,0:T(8,128)}, f32[2,1,512]{2,1,0:T(1,128)}) custom-call(bf16[2,4,1,320,1024]{4,3,2,1,0:T(8,128)(2,1)} %bitcast.71, bf16[2,1280,512]{2,1,0:T(8,128)(2,1)} %bitcast.72), custom_call_target="tpu_custom_call" | custom-call | flops 2684354560 | bytes 12058624 | tf_op jit(solution)/shard_map/weight_grads/pallas_call | solution.py:1705
  401.6 2.5 slice_bitcast_fusion
  404.1 19.4 %weight_grads.4 = (f32[2,2048,2,512]{3,2,1,0:T(2,128)}, f32[2,2,512]{2,1,0:T(2,128)}) custom-call(bf16[2,8,4,160,512]{4,3,2,1,0:T(8,128)(2,1)} %bitcast.67, bf16[2,1280,1024]{2,1,0:T(8,128)(2,1)} %bitcast.83, bf16[2,1280,1024]{2,1,0:T(8,128)(2,1)} %bitcast.84), custom_call_target="tpu_custom_call" | custom-call | flops 10737418240 | bytes 32505856 | tf_op jit(solution)/shard_map/weight_grads/pallas_call | solution.py:1705
  423.5 3.5 convolution_convert_fusion
  427.0 0.0 all-gather.7.cloned.1.call-update
  427.1 3.0 fusion
  430.0 1.5 convert_reduce_fusion.1
  431.5 0.6 slice_bitcast_fusion.2
  432.1 0.6 slice.33
  432.7 0.7 broadcast_select_fusion
  433.4 0.0 collective-permute-done.first_ref
  433.4 0.0 collective-permute-done.1.second_ref
  433.4 3.0 merge_late.2.gates_in
  436.4 20.0 %weight_grads.6 = (f32[2,512,4,1024]{3,2,1,0:T(4,128)}, f32[2,512,4,1024]{3,2,1,0:T(4,128)}, f32[2,4,1024]{2,1,0:T(4,128)}) custom-call(bf16[2,4,1,320,512]{4,3,2,1,0:T(8,128)(2,1)} %bitcast.64, bf16[2,4,1,336,512]{4,3,2,1,0:T(8,128)(2,1)} %bitcast.62, bf16[2,1280,4096]{2,1,0:T(8,128)(2,1)} %bitcast.52, bf16[2,1280,4096]{2,1,0:T(8,128)(2,1)} %bitcast.53, ...), custom_call_target="tpu_custom_call" | custom-call | flops 10737418240 | bytes 42991616 | tf_op jit(solution)/shard_map/weight_grads/pallas_call | solution.py:1705
  456.5 0.0 collective-permute-done.2.first_ref
  456.5 0.0 collective-permute-done.3.second_ref
  456.5 2.8 merge_late.3
  459.3 0.0 copy-start.1
  459.3 20.3 %weight_grads.7 = (f32[2,512,4,1024]{3,2,1,0:T(4,128)}, f32[2,512,4,1024]{3,2,1,0:T(4,128)}, f32[2,4,1024]{2,1,0:T(4,128)}) custom-call(bf16[1,4,1,320,512]{4,3,2,1,0:T(8,128)(2,1)} %bitcast.70, bf16[2,4,1,336,512]{4,3,2,1,0:T(8,128)(2,1)} %bitcast.63, bf16[2,1280,4096]{2,1,0:T(8,128)(2,1)} %bitcast.56, ...), custom_call_target="tpu_custom_call", output_to_operand_aliasing={{0}: (6, {}), {1}: (7, {}), {2}: (8, {})} | custom-call | flops 10737418240 | bytes 42991616 | tf_op jit(solution)/shard_map/weight_grads/pallas_call | solution.py:1705
  479.6 0.0 all-gather.7.cloned.1.call-done
  479.6 4.2 convert_element_type.181
  (22 shorter events, 0.1 us)
Async XLA Ops:
  7.2 0.9 copy-start
  7.2 416.3 %all-gather.5.cloned.1.call-start = ((), (), s32[]{:S(2)}) async-start(), calls=%async_computation | async-start | bytes 1474560 | tf_op jit(solution)/shard_map/all_gather | solution.py:1869
  12.3 8.2 %copy-start.4 = (bf16[262,16]{0,1:T(8,128)(2,1)S(1)}, bf16[262,16]{0,1:T(8,128)(2,1)}, u32[]{:S(2)}) copy-start(bf16[262,16]{0,1:T(8,128)(2,1)} %param.18) | copy-start | bytes 25156
  12.3 8.4 %copy-start.5 = (bf16[512]{0:T(512)(128)(2,1)S(1)}, bf16[512]{0:T(512)(128)(2,1)}, u32[]{:S(2)}) copy-start(bf16[512]{0:T(512)(128)(2,1)} %param.24) | copy-start | bytes 3076
  21.9 60.7 %copy-start.3 = (bf16[16,20,2,512]{3,2,1,0:T(2,128)(2,1)S(1)}, bf16[16,20,2,512]{3,2,1,0:T(2,128)(2,1)}, u32[]{:S(2)}) copy-start(bf16[16,20,2,512]{3,2,1,0:T(2,128)(2,1)} %param.17) | copy-start | bytes 1966084
  21.9 61.8 %copy-start.6 = (s32[16]{0:T(128)S(1)}, s32[16]{0:T(128)}, u32[]{:S(2)}) copy-start(s32[16]{0:T(128)} %param.16) | copy-start | bytes 196
  82.6 347.5 %all-gather.9.cloned.1.call-start = ((), (), s32[]{:S(2)}) async-start(), calls=%async_computation.2 | async-start | bytes 1327104 | tf_op jit(solution)/shard_map/all_gather | solution.py:1911
  386.6 46.9 %collective-permute-start = (bf16[10,16,4096]{2,1,0:T(8,128)(2,1)}, bf16[10,16,4096]{2,1,0:T(8,128)(2,1)}, u32[]{:S(2)}, u32[]{:S(2)}) collective-permute-start(bf16[10,16,4096]{2,1,0:T(8,128)(2,1)} %get-tuple-element.78), channel_id=1, source_target_pairs={{0,2},{1,3},{2,0},{3,1},{4,6},{5,7},{6,4},{7,5},{8,10},{9,11},{10,... | collective-permute-start | bytes 3932168 | tf_op jit(solution)/shard_map/ppermute | solution.py:1782
  387.6 45.8 %collective-permute-start.1 = (bf16[10,16,4096]{2,1,0:T(8,128)(2,1)}, bf16[10,16,4096]{2,1,0:T(8,128)(2,1)}, u32[]{:S(2)}, u32[]{:S(2)}) collective-permute-start(bf16[10,16,4096]{2,1,0:T(8,128)(2,1)} %get-tuple-element.79), channel_id=1, source_target_pairs={{0,1},{1,0},{2,3},{3,2},{4,5},{5,4},{6,7},{7,6},{8,9},{9,8},{10,11... | collective-permute-start | bytes 3932168 | tf_op jit(solution)/shard_map/ppermute | solution.py:1782
  388.7 67.8 %collective-permute-start.2 = (bf16[10,16,4096]{2,1,0:T(8,128)(2,1)}, bf16[10,16,4096]{2,1,0:T(8,128)(2,1)}, u32[]{:S(2)}, u32[]{:S(2)}) collective-permute-start(bf16[10,16,4096]{2,1,0:T(8,128)(2,1)} %get-tuple-element.101), channel_id=1, source_target_pairs={{0,2},{1,3},{2,0},{3,1},{4,6},{5,7},{6,4},{7,5},{8,10},{9,11},{10,... | collective-permute-start | bytes 3932168 | tf_op jit(solution)/shard_map/ppermute | solution.py:1782
  390.1 66.4 %collective-permute-start.3 = (bf16[10,16,4096]{2,1,0:T(8,128)(2,1)}, bf16[10,16,4096]{2,1,0:T(8,128)(2,1)}, u32[]{:S(2)}, u32[]{:S(2)}) collective-permute-start(bf16[10,16,4096]{2,1,0:T(8,128)(2,1)} %get-tuple-element.102), channel_id=1, source_target_pairs={{0,1},{1,0},{2,3},{3,2},{4,5},{5,4},{6,7},{7,6},{8,9},{9,8},{10,11... | collective-permute-start | bytes 3932168 | tf_op jit(solution)/shard_map/ppermute | solution.py:1782
  390.7 88.9 %all-gather.7.cloned.1.call-start = ((), (), s32[]{:S(2)}) async-start(), calls=%async_computation.1 | async-start | bytes 2621440 | tf_op jit(solution)/shard_map/all_gather | solution.py:1927
  423.5 3.6 copy-start.2
  459.3 24.5 %copy-start.1 = (s32[16,20,50]{2,0,1:T(8,128)S(1)}, s32[16,20,50]{2,0,1:T(8,128)}, u32[]{:S(2)}) copy-start(s32[16,20,50]{2,0,1:T(8,128)} %param.15) | copy-start | bytes 192004
Sparse Core Ops, SparseCore 0:
  82.7 31.9 all-gather.4
  390.8 28.1 all-gather.8
  427.2 45.0 all-gather.6

commit v6 on v5

--- a/solution.py
+++ b/solution.py
@@ -518,6 +518,8 @@
     late_sem,
     defer_send,
     defer_recv,
+    x_buf,
+    flip_sem,
 ):
     count = lax.axis_size("mp")
     me = lax.axis_index("mp")
@@ -607,8 +609,11 @@
 
     everyone = [*peers, me]
 
+    x_load = pltpu.make_async_copy(x_all.at[0], x_buf, flip_sem.at[0])
+
     @pl.when(section == 0)
     def _():
+        x_load.start()
         for j, peer in enumerate(peers):
             spread_base(0, 0, peer, j).start()
         for j, peer in enumerate(everyone):
@@ -770,6 +775,17 @@
         for load, store in zip(late_loads, late_stores):
             load.wait()
             store.start()
+    @pl.when(section == 0)
+    def _():
+        x_load.wait()
+
+        @pl.loop(0, steps)
+        def _(t):
+            for q in range(groups):
+                pltpu.make_async_copy(
+                    x_buf.at[q, t], x_all.at[1, q, steps - 1 - t], flip_sem.at[1]
+                ).start()
+
     grad_current[...] = grad_current[...] * jax.nn.sigmoid(pooled_ref[...])
     conv_out[...] = jnp.zeros_like(conv_out)
     small_out[...] = jnp.zeros_like(small_out)
@@ -847,6 +863,7 @@
         for j, peer in enumerate(everyone):
             spread_base(1, 1, peer, j).wait_send()
         lift().wait_send()
+        pltpu.make_async_copy(x_buf, x_all.at[1], flip_sem.at[1]).wait()
 
     @pl.when(section == 1)
     def _():
@@ -931,6 +948,8 @@
             dma((4,)),
             dma((groups - 1,)),
             dma((groups - 1,)),
+            pltpu.VMEM(x_all.shape[1:], BF16),
+            dma((2,)),
         ],
         compiler_params=pltpu.CompilerParams(
             collective_id=2, has_side_effects=True, vmem_limit_bytes=VMEM_LIMIT
@@ -1935,25 +1954,20 @@
         2,
     )
     states = one_piece(all_states)
-    turned_inputs = jnp.where(section == 0, jnp.flip(all_inputs[0], axis=1), all_inputs[1])[None]
+    inputs = one_piece(all_inputs)
     if relayed:
-        moved_first, high_grad, proj_grad, conv_weight_grad, table_grad, turned_inputs = (
-            lax.optimization_barrier(
-                (moved_first, high_grad, proj_grad, conv_weight_grad, table_grad, turned_inputs)
-            )
+        moved_first, high_grad, proj_grad, conv_weight_grad, table_grad = lax.optimization_barrier(
+            (moved_first, high_grad, proj_grad, conv_weight_grad, table_grad)
         )
         all_gates = merge_late(0, all_gates, moved_first)
-        done = weight_grads([one_piece(all_inputs), states], flat(all_gates), 4, only=0)
+        done = weight_grads([inputs, states], flat(all_gates), 4, only=0)
         done, moved_second, all_gates = lax.optimization_barrier((done, moved_second, all_gates))
         all_gates = merge_late(1, all_gates, moved_second)
         input_grad, state_grad, bias_grad = weight_grads(
-            [one_piece(turned_inputs), states], flat(all_gates), 4, only=1, done=done
+            [inputs, states], flat(all_gates), 4, only=1, done=done
         )
     else:
-        both = jnp.concatenate([all_inputs[:1], turned_inputs])
-        input_grad, state_grad, bias_grad = weight_grads(
-            [one_piece(both), states], flat(all_gates), 4
-        )
+        input_grad, state_grad, bias_grad = weight_grads([inputs, states], flat(all_gates), 4)
     return (
         table_grad,
         conv_weight_grad,

time: 494 us -> 489 us (0.990)
  transfers between devices with their start and end apart: 7 -> 7, of which waited for: 0 -> 2; matrix products, arithmetic and copies ran while one was open for 3% -> 2% of each run, Pallas kernels for 77% -> 77%
where the time goes in v6:
time: 489 us; the launch traced here: 486 us
  Pallas kernels  437 us (89%)
  local copies, waits for them, and re-layouts  15.6 us (3%)
  between operations  14.1 us (3%)
  other arithmetic  9.58 us (2%)
    pallas_call x1, Pallas kernels, recurrence(): pl.pallas_call(recurrence_kernel, out_shape=(jax.ShapeDtypeStruct((2, gro...  228 us
    pallas_call x1, Pallas kernels, cnn_backward(): pl.pallas_call(cnn_backward_kernel, out_shape=(jax.ShapeDtypeStruct(gates...  74.3 us
    pallas_call x4, Pallas kernels, weight_grads(): pl.pallas_call(kernel, out_shape=(*[jax.ShapeDtypeStruct((batch, pieces *...  68.4 us
    pallas_call x1, Pallas kernels, cnn_forward(): pl.pallas_call(cnn_forward_kernel, out_shape=(jax.ShapeDtypeStruct((2, to...  60.3 us
  transfers between devices with their start and end apart: 7, of which 2 were waited for; matrix products, arithmetic and copies ran while one was open for 2% of the time, Pallas kernels for 77%

profile of v6, /device:TPU:0, one launch (start us, length us, event | category | flops | bytes accessed | tf_op | source)
XLA Modules:
  0.0 485.9 jit_solution(13778476311082091643)
XLA Ops:
  7.2 0.0 copy-start
  7.2 0.0 all-gather.5.cloned.1.call-start
  7.3 0.6 fusion.14.log_positions
  7.9 0.2 copy-done
  8.1 0.8 reshape.260.ids_ref
  8.9 1.0 copy.43
  9.9 1.6 select_bitcast_fusion
  11.5 0.8 copy.46.masked_ref
  12.3 8.2 %copy.52 = bf16[2,2048,2,512]{3,1,2,0:T(8,128)(2,1)} copy(bf16[2,2048,2,512]{3,2,1,0:T(2,128)(2,1)} %param.21) | data formatting | bytes 16777216 | tf_op args[6]
  20.5 0.0 copy-done.5
  20.5 0.1 copy.42
  20.7 0.6 broadcast_in_dim.59.b_proj
  21.2 0.6 pad.16.table_ref
  21.9 60.3 %cnn_forward.1 = (f32[2,160,512]{2,1,0:T(8,128)}, bf16[10,896,128]{2,1,0:T(8,128)(2,1)}, f32[160,1,512]{2,1,0:T(1,128)}, f32[160,512]{1,0:T(8,128)}, f32[2,160,5...) custom-call(s32[10,1,896]{2,1,0:T(1,128)} %reshape.260.ids_ref, ...), custom_call_target="tpu_custom_call" | custom-call | tf_op jit(solution)/shard_map/cnn_forward/pallas_call | solution.py:400
  82.2 0.0 all-gather.5.cloned.1.call-update
  82.2 0.0 all-gather.9.cloned.1.call-start
  82.3 1.0 copy.53
  83.3 0.8 broadcast_in_dim.60.live_ref
  84.1 227.8 %recurrence.1 = (bf16[2,4,20,16,512]{4,3,2,1,0:T(8,128)(2,1)}, bf16[2,4,21,16,512]{4,3,2,1,0:T(8,128)(2,1)}, bf16[2,4,20,16,1024]{4,3,2,1,0:T(8,128)(2,1)}, bf16...) custom-call(f32[2,160,512]{2,1,0:T(8,128)} %get-tuple-element.61.bas, ...), custom_call_target="tpu_custom_call", output_to_operand_aliasing={{6}: (7, {})} | custom-call | tf_op jit(solution)/shard_map/recurrence/pallas_call | solution.py:1599
  311.9 74.3 %cnn_backward.1 = (bf16[2,4,20,16,4096]{4,3,2,1,0:T(8,128)(2,1)}, bf16[2,4,20,16,512]{4,3,2,1,0:T(8,128)(2,1)}, bf16[2,4,20,16,512]{4,3,2,1,0:T(8,128)(2,1)}, bf...) custom-call(bf16[2,160,128]{2,1,0:T(8,128)(2,1)} %get-tuple-element., ...), custom_call_target="tpu_custom_call", output_to_operand_aliasing={{0}: (12, {}), {1}: (13, {}), {2}: (14, {}), {3}: (15, {})} | custom-call | tf_op jit(solution)/shard_map/cnn_backward/pallas_call | solution.py:898
  386.2 0.0 all-gather.9.cloned.1.call-update
  386.2 0.2 all-gather.7.cloned.1.call-start
  386.5 1.1 collective-permute-start
  387.5 1.1 collective-permute-start.1
  388.7 1.3 collective-permute-start.2
  390.0 0.6 collective-permute-start.3
  390.6 19.4 %weight_grads.4 = (f32[2,2048,2,512]{3,2,1,0:T(2,128)}, f32[2,2,512]{2,1,0:T(2,128)}) custom-call(bf16[2,8,4,160,512]{4,3,2,1,0:T(8,128)(2,1)} %bitcast.59, bf16[2,1280,1024]{2,1,0:T(8,128)(2,1)} %bitcast.74, bf16[2,1280,1024]{2,1,0:T(8,128)(2,1)} %bitcast.75), custom_call_target="tpu_custom_call" | custom-call | flops 10737418240 | bytes 32505856 | tf_op jit(solution)/shard_map/weight_grads/pallas_call | solution.py:1724
  410.0 0.0 all-gather.5.cloned.1.call-done
  410.1 3.5 convolution_convert_fusion
  413.5 0.0 all-gather.7.cloned.1.call-update
  413.6 0.8 convert_reduce_fusion
  414.4 8.5 %weight_grads.5 = (f32[2,1024,512]{2,1,0:T(8,128)}, f32[2,1,512]{2,1,0:T(1,128)}) custom-call(bf16[2,4,1,320,1024]{4,3,2,1,0:T(8,128)(2,1)} %bitcast.62, bf16[2,1280,512]{2,1,0:T(8,128)(2,1)} %bitcast.63), custom_call_target="tpu_custom_call" | custom-call | flops 2684354560 | bytes 12058624 | tf_op jit(solution)/shard_map/weight_grads/pallas_call | solution.py:1724
  422.9 1.5 convert_reduce_fusion.1
  424.5 0.6 slice_bitcast_fusion.1
  425.1 0.6 slice.25
  425.7 0.7 broadcast_select_fusion
  426.4 0.0 collective-permute-done.first_ref
  426.4 0.0 collective-permute-done.1.second_ref
  426.4 2.9 merge_late.2.gates_in
  429.4 20.1 %weight_grads.6 = (f32[2,512,4,1024]{3,2,1,0:T(4,128)}, f32[2,512,4,1024]{3,2,1,0:T(4,128)}, f32[2,4,1024]{2,1,0:T(4,128)}) custom-call(bf16[2,4,1,320,512]{4,3,2,1,0:T(8,128)(2,1)} %bitcast.55, bf16[2,4,1,336,512]{4,3,2,1,0:T(8,128)(2,1)} %bitcast.53, bf16[2,1280,4096]{2,1,0:T(8,128)(2,1)} %bitcast.43, bf16[2,1280,4096]{2,1,0:T(8,128)(2,1)} %bitcast.44, ...), custom_call_target="tpu_custom_call" | custom-call | flops 10737418240 | bytes 42991616 | tf_op jit(solution)/shard_map/weight_grads/pallas_call | solution.py:1724
  449.4 1.2 collective-permute-done.2.first_ref
  450.6 0.8 collective-permute-done.3.second_ref
  451.4 0.2 copy-done.2
  451.7 2.8 merge_late.3
  454.5 0.0 copy-start.1
  454.5 20.4 %weight_grads.7 = (f32[2,512,4,1024]{3,2,1,0:T(4,128)}, f32[2,512,4,1024]{3,2,1,0:T(4,128)}, f32[2,4,1024]{2,1,0:T(4,128)}) custom-call(bf16[2,4,1,320,512]{4,3,2,1,0:T(8,128)(2,1)} %bitcast.56, bf16[2,4,1,336,512]{4,3,2,1,0:T(8,128)(2,1)} %bitcast.54, bf16[2,1280,4096]{2,1,0:T(8,128)(2,1)} %bitcast.47, ...), custom_call_target="tpu_custom_call", output_to_operand_aliasing={{0}: (6, {}), {1}: (7, {}), {2}: (8, {})} | custom-call | flops 10737418240 | bytes 42991616 | tf_op jit(solution)/shard_map/weight_grads/pallas_call | solution.py:1724
  474.9 0.0 all-gather.7.cloned.1.call-done
  474.9 4.2 convert_element_type.181
  (22 shorter events, 0.1 us)
Async XLA Ops:
  7.2 0.9 copy-start
  7.2 402.9 %all-gather.5.cloned.1.call-start = ((), (), s32[]{:S(2)}) async-start(), calls=%async_computation | async-start | bytes 1474560 | tf_op jit(solution)/shard_map/all_gather | solution.py:1888
  12.3 8.2 %copy-start.5 = (bf16[262,16]{0,1:T(8,128)(2,1)S(1)}, bf16[262,16]{0,1:T(8,128)(2,1)}, u32[]{:S(2)}) copy-start(bf16[262,16]{0,1:T(8,128)(2,1)} %param.18) | copy-start | bytes 25156
  12.3 8.4 %copy-start.6 = (bf16[512]{0:T(512)(128)(2,1)S(1)}, bf16[512]{0:T(512)(128)(2,1)}, u32[]{:S(2)}) copy-start(bf16[512]{0:T(512)(128)(2,1)} %param.24) | copy-start | bytes 3076
  21.9 60.4 %copy-start.4 = (bf16[16,20,2,512]{3,2,1,0:T(2,128)(2,1)S(1)}, bf16[16,20,2,512]{3,2,1,0:T(2,128)(2,1)}, u32[]{:S(2)}) copy-start(bf16[16,20,2,512]{3,2,1,0:T(2,128)(2,1)} %param.17) | copy-start | bytes 1966084
  21.9 61.4 %copy-start.7 = (s32[16]{0:T(128)S(1)}, s32[16]{0:T(128)}, u32[]{:S(2)}) copy-start(s32[16]{0:T(128)} %param.16) | copy-start | bytes 196
  82.2 340.7 %all-gather.9.cloned.1.call-start = ((), (), s32[]{:S(2)}) async-start(), calls=%async_computation.2 | async-start | bytes 1327104 | tf_op jit(solution)/shard_map/all_gather | solution.py:1930
  386.2 88.7 %all-gather.7.cloned.1.call-start = ((), (), s32[]{:S(2)}) async-start(), calls=%async_computation.1 | async-start | bytes 2621440 | tf_op jit(solution)/shard_map/all_gather | solution.py:1946
  386.5 40.0 %collective-permute-start = (bf16[10,16,4096]{2,1,0:T(8,128)(2,1)}, bf16[10,16,4096]{2,1,0:T(8,128)(2,1)}, u32[]{:S(2)}, u32[]{:S(2)}) collective-permute-start(bf16[10,16,4096]{2,1,0:T(8,128)(2,1)} %get-tuple-element.77), channel_id=1, source_target_pairs={{0,2},{1,3},{2,0},{3,1},{4,6},{5,7},{6,4},{7,5},{8,10},{9,11},{10,... | collective-permute-start | bytes 3932168 | tf_op jit(solution)/shard_map/ppermute | solution.py:1801
  387.5 38.9 %collective-permute-start.1 = (bf16[10,16,4096]{2,1,0:T(8,128)(2,1)}, bf16[10,16,4096]{2,1,0:T(8,128)(2,1)}, u32[]{:S(2)}, u32[]{:S(2)}) collective-permute-start(bf16[10,16,4096]{2,1,0:T(8,128)(2,1)} %get-tuple-element.78), channel_id=1, source_target_pairs={{0,1},{1,0},{2,3},{3,2},{4,5},{5,4},{6,7},{7,6},{8,9},{9,8},{10,11... | collective-permute-start | bytes 3932168 | tf_op jit(solution)/shard_map/ppermute | solution.py:1801
  388.7 62.0 %collective-permute-start.2 = (bf16[10,16,4096]{2,1,0:T(8,128)(2,1)}, bf16[10,16,4096]{2,1,0:T(8,128)(2,1)S(1)}, u32[]{:S(2)}, u32[]{:S(2)}) collective-permute-start(bf16[10,16,4096]{2,1,0:T(8,128)(2,1)} %get-tuple-element.99), channel_id=1, source_target_pairs={{0,2},{1,3},{2,0},{3,1},{4,6},{5,7},{6,4},{7,5},{8,10},{9,11},{10,... | collective-permute-start | bytes 3932168 | tf_op jit(solution)/shard_map/ppermute | solution.py:1801
  390.0 61.5 %collective-permute-start.3 = (bf16[10,16,4096]{2,1,0:T(8,128)(2,1)}, bf16[10,16,4096]{2,1,0:T(8,128)(2,1)}, u32[]{:S(2)}, u32[]{:S(2)}) collective-permute-start(bf16[10,16,4096]{2,1,0:T(8,128)(2,1)} %get-tuple-element.100), channel_id=1, source_target_pairs={{0,1},{1,0},{2,3},{3,2},{4,5},{5,4},{6,7},{7,6},{8,9},{9,8},{10,11... | collective-permute-start | bytes 3932168 | tf_op jit(solution)/shard_map/ppermute | solution.py:1801
  410.0 3.5 copy-start.3
  450.6 1.1 copy-start.2
  454.5 24.6 %copy-start.1 = (s32[16,20,50]{2,0,1:T(8,128)S(1)}, s32[16,20,50]{2,0,1:T(8,128)}, u32[]{:S(2)}) copy-start(s32[16,20,50]{2,0,1:T(8,128)} %param.15) | copy-start | bytes 192004
Sparse Core Ops, SparseCore 0:
  82.3 31.9 all-gather.4
  386.4 28.1 all-gather.8
  416.2 45.9 all-gather.6

commit v7 on v6

--- a/solution.py
+++ b/solution.py
@@ -1665,7 +1665,7 @@
     )(base_seq, live_seq, top_seq, *weights, features_all)
 
 
-def weight_grads(lefts, right, parts, only=None, done=()):
+def weight_grads(lefts, right, parts, only=None, done=(), widen=()):
     _, outer, pieces, inner, size = lefts[0].shape
     batch = right.shape[0]
     tokens = right.shape[1]
@@ -1688,8 +1688,12 @@
     def kernel(*refs):
         left_refs = refs[: len(lefts)]
         right_refs = refs[len(lefts) : len(lefts) + parts]
-        out_refs = refs[len(lefts) + parts + len(done) : -3]
-        bias_out, turned, ones = refs[-3:]
+        outs = len(lefts) + parts + len(done) + len(widen)
+        out_refs = refs[outs : outs + len(lefts)]
+        bias_out = refs[outs + len(lefts)]
+        turned, ones = refs[-2:]
+        if widen:
+            refs[outs + len(lefts) + 1][...] = refs[outs - 1][...].astype(F32)
 
         @pl.when(pl.program_id(2) == 0)
         def _():
@@ -1731,6 +1735,7 @@
                 for _ in lefts
             ],
             jax.ShapeDtypeStruct((batch, parts, columns), F32),
+            *[jax.ShapeDtypeStruct(item.shape, F32) for item in widen],
         ),
         grid=(chosen, pieces, blocks),
         in_specs=[
@@ -1751,6 +1756,10 @@
                 for g in range(parts)
             ],
             *[ANY_SPEC] * len(done),
+            *[
+                pl.BlockSpec((item.shape[0] // blocks, item.shape[1]), lambda b, p, n: (n, 0))
+                for item in widen
+            ],
         ],
         input_output_aliases={len(lefts) + parts + i: i for i in range(len(done))},
         out_specs=(
@@ -1761,6 +1770,10 @@
                 for _ in lefts
             ],
             pl.BlockSpec((1, parts, block), lambda b, p, n: (entry(b), 0, n)),
+            *[
+                pl.BlockSpec((item.shape[0] // blocks, item.shape[1]), lambda b, p, n: (n, 0))
+                for item in widen
+            ],
         ),
         scratch_shapes=[
             pltpu.VMEM((total, tokens), BF16),
@@ -1773,7 +1786,7 @@
             transcendentals=0,
         ),
         name="weight_grads",
-    )(*lefts, *[right] * parts, *done)
+    )(*lefts, *[right] * parts, *done, *widen)
 
 
 def merge_kernel(d, first_ref, second_ref, gates_in, gates_all, staged, sems):
@@ -1927,13 +1940,6 @@
     if relayed:
         moved_first = send_late(late[:2])
         moved_second = send_late(late[2:])
-    small = lax.all_gather(small, ("section", "dp"), axis=0)
-    small = jnp.sum(small.astype(F32), axis=0)
-    conv_weight_grad = jnp.where(
-        tap_keep[:, None, :], small[: TAPS * emb].reshape(conv_weight.shape), 0.0
-    )
-    table_grad = small[128:].reshape(-1, emb, local)
-    table_grad = jnp.transpose(table_grad, (0, 2, 1)).reshape(-1, emb)[: char_table.shape[0]]
     all_base = base_full.reshape(-1, proj_width)
 
     def flat(values):
@@ -1943,9 +1949,9 @@
         batch, groups, _, _, width = values.shape
         return values.reshape(batch, groups, 1, -1, width)
 
-    proj_weight_grad = lax.all_gather(
-        dot(last_features, all_base, 0, 0).astype(BF16), "mp", axis=0, tiled=True
-    ).astype(F32)
+    own_proj = dot(last_features, all_base, 0, 0).astype(BF16)
+    all_mixed, own_proj = lax.optimization_barrier((all_mixed, own_proj))
+    proj_weight_low = lax.all_gather(own_proj, "mp", axis=0, tiled=True)
     proj_grad = weight_grads([one_piece(all_hidden)], flat(all_projected), 1)[0]
     batch, _, groups, count, _, _ = high_features.shape
     high_grad, high_bias_grad = weight_grads(
@@ -1953,21 +1959,31 @@
         all_mixed.reshape(batch, -1, 2 * local),
         2,
     )
+    small, high_grad, proj_grad = lax.optimization_barrier((small, high_grad, proj_grad))
+    small = lax.all_gather(small, ("section", "dp"), axis=0)
     states = one_piece(all_states)
     inputs = one_piece(all_inputs)
     if relayed:
-        moved_first, high_grad, proj_grad, conv_weight_grad, table_grad = lax.optimization_barrier(
-            (moved_first, high_grad, proj_grad, conv_weight_grad, table_grad)
+        moved_first, high_grad, proj_grad = lax.optimization_barrier(
+            (moved_first, high_grad, proj_grad)
         )
         all_gates = merge_late(0, all_gates, moved_first)
         done = weight_grads([inputs, states], flat(all_gates), 4, only=0)
         done, moved_second, all_gates = lax.optimization_barrier((done, moved_second, all_gates))
         all_gates = merge_late(1, all_gates, moved_second)
-        input_grad, state_grad, bias_grad = weight_grads(
-            [inputs, states], flat(all_gates), 4, only=1, done=done
+        input_grad, state_grad, bias_grad, proj_weight_grad = weight_grads(
+            [inputs, states], flat(all_gates), 4, only=1, done=done, widen=(proj_weight_low,)
         )
     else:
         input_grad, state_grad, bias_grad = weight_grads([inputs, states], flat(all_gates), 4)
+        proj_weight_grad = proj_weight_low.astype(F32)
+    small, bias_grad = lax.optimization_barrier((small, bias_grad))
+    small = jnp.sum(small.astype(F32), axis=0)
+    conv_weight_grad = jnp.where(
+        tap_keep[:, None, :], small[: TAPS * emb].reshape(conv_weight.shape), 0.0
+    )
+    table_grad = small[128:].reshape(-1, emb, local)
+    table_grad = jnp.transpose(table_grad, (0, 2, 1)).reshape(-1, emb)[: char_table.shape[0]]
     return (
         table_grad,
         conv_weight_grad,

time: 489 us -> 491 us (level)
  transfers between devices with their start and end apart: 7 -> 7, of which waited for: 2 -> 2; matrix products, arithmetic and copies ran while one was open for 2% -> 1% of each run, Pallas kernels for 77% -> 77%
where the time goes in v7:
time: 491 us; the launch traced here: 487 us
  Pallas kernels  438 us (89%)
  local copies, waits for them, and re-layouts  16.8 us (3%)
  between operations  14.1 us (3%)
  other arithmetic  6.62 us (1%)
    pallas_call x1, Pallas kernels, recurrence(): pl.pallas_call(recurrence_kernel, out_shape=(jax.ShapeDtypeStruct((2, gro...  228 us
    pallas_call x1, Pallas kernels, cnn_backward(): pl.pallas_call(cnn_backward_kernel, out_shape=(jax.ShapeDtypeStruct(gates...  74.3 us
    pallas_call x4, Pallas kernels, weight_grads(): pl.pallas_call(kernel, out_shape=(*[jax.ShapeDtypeStruct((batch, pieces *...  69.4 us
    pallas_call x1, Pallas kernels, cnn_forward(): pl.pallas_call(cnn_forward_kernel, out_shape=(jax.ShapeDtypeStruct((2, to...  60.3 us
  transfers between devices with their start and end apart: 7, of which 2 were waited for; matrix products, arithmetic and copies ran while one was open for 1% of the time, Pallas kernels for 77%

profile of v7, /device:TPU:0, one launch (start us, length us, event | category | flops | bytes accessed | tf_op | source)
XLA Modules:
  0.0 487.4 jit_solution(1252501768598010907)
XLA Ops:
  7.2 0.0 copy-start
  7.2 0.0 all-gather.5.cloned.1.call-start
  7.3 0.6 fusion.14.log_positions
  7.9 1.3 broadcast_in_dim.59.b_proj
  9.2 0.0 copy-done
  9.2 0.8 reshape.259.ids_ref
  10.0 0.7 tile.4
  10.7 0.1 copy.42
  10.8 1.0 copy.43
  11.8 1.6 select_bitcast_fusion
  13.5 0.8 copy.46.masked_ref
  14.2 8.2 %copy.52 = bf16[2,2048,2,512]{3,1,2,0:T(8,128)(2,1)} copy(bf16[2,2048,2,512]{3,2,1,0:T(2,128)(2,1)} %param.21) | data formatting | bytes 16777216 | tf_op args[6]
  22.4 0.6 pad.16.table_ref
  23.1 60.3 %cnn_forward.1 = (f32[2,160,512]{2,1,0:T(8,128)}, bf16[10,896,128]{2,1,0:T(8,128)(2,1)}, f32[160,1,512]{2,1,0:T(1,128)}, f32[160,512]{1,0:T(8,128)}, f32[2,160,5...) custom-call(s32[10,1,896]{2,1,0:T(1,128)} %reshape.259.ids_ref, ...), custom_call_target="tpu_custom_call" | custom-call | tf_op jit(solution)/shard_map/cnn_forward/pallas_call | solution.py:400
  83.3 0.0 all-gather.5.cloned.1.call-update
  83.4 0.0 all-gather.7.cloned.1.call-start
  83.4 1.0 copy.53
  84.5 0.8 broadcast_in_dim.60.live_ref
  85.3 227.8 %recurrence.1 = (bf16[2,4,20,16,512]{4,3,2,1,0:T(8,128)(2,1)}, bf16[2,4,21,16,512]{4,3,2,1,0:T(8,128)(2,1)}, bf16[2,4,20,16,1024]{4,3,2,1,0:T(8,128)(2,1)}, bf16...) custom-call(f32[2,160,512]{2,1,0:T(8,128)} %get-tuple-element.67.bas, ...), custom_call_target="tpu_custom_call", output_to_operand_aliasing={{6}: (7, {})} | custom-call | tf_op jit(solution)/shard_map/recurrence/pallas_call | solution.py:1599
  313.1 74.3 %cnn_backward.1 = (bf16[2,4,20,16,4096]{4,3,2,1,0:T(8,128)(2,1)}, bf16[2,4,20,16,512]{4,3,2,1,0:T(8,128)(2,1)}, bf16[2,4,20,16,512]{4,3,2,1,0:T(8,128)(2,1)}, bf...) custom-call(bf16[2,160,128]{2,1,0:T(8,128)(2,1)} %get-tuple-element., ...), custom_call_target="tpu_custom_call", output_to_operand_aliasing={{0}: (12, {}), {1}: (13, {}), {2}: (14, {}), {3}: (15, {})} | custom-call | tf_op jit(solution)/shard_map/cnn_backward/pallas_call | solution.py:898
  387.4 0.0 all-gather.5.cloned.1.call-done
  387.4 3.4 convolution_convert_fusion
  390.8 0.0 all-gather.7.cloned.1.call-update
  390.8 0.2 all-gather.9.cloned.1.call-start
  391.0 1.0 collective-permute-start
  392.1 1.1 collective-permute-start.1
  393.2 1.4 collective-permute-start.2
  394.6 0.6 collective-permute-start.3
  395.2 8.7 %weight_grads.5 = (f32[2,1024,512]{2,1,0:T(8,128)}, f32[2,1,512]{2,1,0:T(1,128)}) custom-call(bf16[2,4,1,320,1024]{4,3,2,1,0:T(8,128)(2,1)} %bitcast.61, bf16[2,1280,512]{2,1,0:T(8,128)(2,1)} %bitcast.62), custom_call_target="tpu_custom_call" | custom-call | flops 2684354560 | bytes 12058624 | tf_op jit(solution)/shard_map/weight_grads/pallas_call | solution.py:1728
  403.9 19.4 %weight_grads.4 = (f32[2,2048,2,512]{3,2,1,0:T(2,128)}, f32[2,2,512]{2,1,0:T(2,128)}) custom-call(bf16[2,8,4,160,512]{4,3,2,1,0:T(8,128)(2,1)} %bitcast.58, bf16[2,1280,1024]{2,1,0:T(8,128)(2,1)} %bitcast.73, bf16[2,1280,1024]{2,1,0:T(8,128)(2,1)} %bitcast.74), custom_call_target="tpu_custom_call" | custom-call | flops 10737418240 | bytes 32505856 | tf_op jit(solution)/shard_map/weight_grads/pallas_call | solution.py:1728
  423.3 0.0 all-gather.9.cloned.1.call-update
  423.3 2.1 convert_reduce_fusion
  425.4 0.0 collective-permute-done.first_ref
  425.5 0.0 collective-permute-done.1.second_ref
  425.5 2.9 merge_late.2.gates_in
  428.4 20.1 %weight_grads.6 = (f32[2,512,4,1024]{3,2,1,0:T(4,128)}, f32[2,512,4,1024]{3,2,1,0:T(4,128)}, f32[2,4,1024]{2,1,0:T(4,128)}) custom-call(bf16[2,4,1,320,512]{4,3,2,1,0:T(8,128)(2,1)} %bitcast.54, bf16[2,4,1,336,512]{4,3,2,1,0:T(8,128)(2,1)} %bitcast.52, bf16[2,1280,4096]{2,1,0:T(8,128)(2,1)} %bitcast.42, bf16[2,1280,4096]{2,1,0:T(8,128)(2,1)} %bitcast.43, ...), custom_call_target="tpu_custom_call" | custom-call | flops 10737418240 | bytes 42991616 | tf_op jit(solution)/shard_map/weight_grads/pallas_call | solution.py:1728
  448.4 3.6 collective-permute-done.2.first_ref
  452.0 0.8 collective-permute-done.3.second_ref
  452.8 0.3 copy-done.2
  453.1 2.8 merge_late.3
  455.9 0.0 all-gather.7.cloned.1.call-done.refs_9_
  455.9 0.0 copy-start.1
  455.9 21.3 %weight_grads.7 = (f32[2,512,4,1024]{3,2,1,0:T(4,128)}, f32[2,512,4,1024]{3,2,1,0:T(4,128)}, f32[2,4,1024]{2,1,0:T(4,128)}, f32[2048,512]{1,0:T(8,128)}) custom-call(bf16[2,4,1,320,512]{4,3,2,1,0:T(8,128)(2,1)} %bitcast.55, bf16[2,4,1,336,512]{4,3,2,1,0:T(8,128)(2,1)} %bitcast.53, ...), custom_call_target="tpu_custom_call", output_to_operand_aliasing={{0}: (6, {}), {1}: (7, {}), {2}: (8, {})} | custom-call | flops 10737418240 | bytes 42991616 | tf_op jit(solution)/shard_map/weight_grads/pallas_call | solution.py:1728
  477.2 0.0 all-gather.9.cloned.1.call-done
  477.2 1.5 convert_reduce_fusion.1
  478.7 0.6 slice.25
  479.3 0.6 slice_bitcast_fusion.1
  479.9 0.7 broadcast_select_fusion
  (15 shorter events, 0.1 us)
Async XLA Ops:
  7.2 2.0 copy-start
  7.2 380.2 %all-gather.5.cloned.1.call-start = ((), (), s32[]{:S(2)}) async-start(), calls=%async_computation | async-start | bytes 1474560 | tf_op jit(solution)/shard_map/all_gather | solution.py:1901
  23.1 60.4 %copy-start.3 = (bf16[16,20,2,512]{3,2,1,0:T(2,128)(2,1)S(1)}, bf16[16,20,2,512]{3,2,1,0:T(2,128)(2,1)}, u32[]{:S(2)}) copy-start(bf16[16,20,2,512]{3,2,1,0:T(2,128)(2,1)} %param.17) | copy-start | bytes 1966084
  23.1 61.4 %copy-start.4 = (s32[16]{0:T(128)S(1)}, s32[16]{0:T(128)}, u32[]{:S(2)}) copy-start(s32[16]{0:T(128)} %param.16) | copy-start | bytes 196
  83.4 372.6 %all-gather.7.cloned.1.call-start = ((), (), s32[]{:S(2)}) async-start(), calls=%async_computation.1 | async-start | bytes 2621440 | tf_op jit(solution)/shard_map/all_gather | solution.py:1954
  390.8 86.4 %all-gather.9.cloned.1.call-start = ((), (), s32[]{:S(2)}) async-start(), calls=%async_computation.2 | async-start | bytes 1327104 | tf_op jit(solution)/shard_map/all_gather | solution.py:1963
  391.0 34.4 %collective-permute-start = (bf16[10,16,4096]{2,1,0:T(8,128)(2,1)}, bf16[10,16,4096]{2,1,0:T(8,128)(2,1)}, u32[]{:S(2)}, u32[]{:S(2)}) collective-permute-start(bf16[10,16,4096]{2,1,0:T(8,128)(2,1)} %get-tuple-element.95), channel_id=1, source_target_pairs={{0,2},{1,3},{2,0},{3,1},{4,6},{5,7},{6,4},{7,5},{8,10},{9,11},{10,... | collective-permute-start | bytes 3932168 | tf_op jit(solution)/shard_map/ppermute | solution.py:1814
  392.1 33.4 %collective-permute-start.1 = (bf16[10,16,4096]{2,1,0:T(8,128)(2,1)}, bf16[10,16,4096]{2,1,0:T(8,128)(2,1)}, u32[]{:S(2)}, u32[]{:S(2)}) collective-permute-start(bf16[10,16,4096]{2,1,0:T(8,128)(2,1)} %get-tuple-element.96), channel_id=1, source_target_pairs={{0,1},{1,0},{2,3},{3,2},{4,5},{5,4},{6,7},{7,6},{8,9},{9,8},{10,11... | collective-permute-start | bytes 3932168 | tf_op jit(solution)/shard_map/ppermute | solution.py:1814
  393.2 58.9 %collective-permute-start.2 = (bf16[10,16,4096]{2,1,0:T(8,128)(2,1)}, bf16[10,16,4096]{2,1,0:T(8,128)(2,1)S(1)}, u32[]{:S(2)}, u32[]{:S(2)}) collective-permute-start(bf16[10,16,4096]{2,1,0:T(8,128)(2,1)} %get-tuple-element.105), channel_id=1, source_target_pairs={{0,2},{1,3},{2,0},{3,1},{4,6},{5,7},{6,4},{7,5},{8,10},{9,11},{10,... | collective-permute-start | bytes 3932168 | tf_op jit(solution)/shard_map/ppermute | solution.py:1814
  394.6 58.3 %collective-permute-start.3 = (bf16[10,16,4096]{2,1,0:T(8,128)(2,1)}, bf16[10,16,4096]{2,1,0:T(8,128)(2,1)}, u32[]{:S(2)}, u32[]{:S(2)}) collective-permute-start(bf16[10,16,4096]{2,1,0:T(8,128)(2,1)} %get-tuple-element.106), channel_id=1, source_target_pairs={{0,1},{1,0},{2,3},{3,2},{4,5},{5,4},{6,7},{7,6},{8,9},{9,8},{10,11... | collective-permute-start | bytes 3932168 | tf_op jit(solution)/shard_map/ppermute | solution.py:1814
  452.0 1.1 copy-start.2
  455.9 24.7 %copy-start.1 = (s32[16,20,50]{2,0,1:T(8,128)S(1)}, s32[16,20,50]{2,0,1:T(8,128)}, u32[]{:S(2)}) copy-start(s32[16,20,50]{2,0,1:T(8,128)} %param.15) | copy-start | bytes 192004
Sparse Core Ops, SparseCore 0:
  83.5 31.9 all-gather.4
  390.9 45.0 all-gather.6
  438.0 24.8 all-gather.8

commit v8 on v6

--- a/solution.py
+++ b/solution.py
@@ -14,7 +14,7 @@
 TAPS = 7
 VMEM_LIMIT = 62 * 1024 * 1024
 SLOTS = 4
-DEFER = 3
+DEFER = 2
 CHUNK = 16
 TURN = 128
 PER_TOKEN = 50

time: 489 us -> 492 us (level)
    pallas_call x1, Pallas kernels: 228 us -> 233 us  [recurrence(): pl.pallas_call(recurrence_kernel, out_shape=(jax.ShapeDtypeStruct((2, gro...]
  transfers between devices with their start and end apart: 7 -> 7, of which waited for: 2 -> 2; matrix products, arithmetic and copies ran while one was open for 2% -> 2% of each run, Pallas kernels for 77% -> 78%
where the time goes in v8:
time: 492 us; the launch traced here: 489 us
  Pallas kernels  440 us (89%)
  local copies, waits for them, and re-layouts  15.8 us (3%)
  between operations  14.1 us (3%)
  other arithmetic  9.6 us (2%)
    pallas_call x1, Pallas kernels, recurrence(): pl.pallas_call(recurrence_kernel, out_shape=(jax.ShapeDtypeStruct((2, gro...  233 us
    pallas_call x1, Pallas kernels, cnn_backward(): pl.pallas_call(cnn_backward_kernel, out_shape=(jax.ShapeDtypeStruct(gates...  72 us
    pallas_call x4, Pallas kernels, weight_grads(): pl.pallas_call(kernel, out_shape=(*[jax.ShapeDtypeStruct((batch, pieces *...  68.5 us
    pallas_call x1, Pallas kernels, cnn_forward(): pl.pallas_call(cnn_forward_kernel, out_shape=(jax.ShapeDtypeStruct((2, to...  60.3 us
    unnamed x18, local copies, waits for them, and re-layouts  9.91 us
  transfers between devices with their start and end apart: 7, of which 2 were waited for; matrix products, arithmetic and copies ran while one was open for 2% of the time, Pallas kernels for 78%

profile of v8, /device:TPU:0, one launch (start us, length us, event | category | flops | bytes accessed | tf_op | source)
XLA Modules:
  0.0 489.2 jit_solution(16972620502356392495)
XLA Ops:
  7.2 0.0 copy-start
  7.2 0.0 all-gather.5.cloned.1.call-start
  7.3 0.6 fusion.14.log_positions
  7.9 0.2 copy-done
  8.1 0.8 reshape.260.ids_ref
  8.9 1.0 copy.43
  9.9 1.6 select_bitcast_fusion
  11.5 0.8 copy.46.masked_ref
  12.3 8.2 %copy.52 = bf16[2,2048,2,512]{3,1,2,0:T(8,128)(2,1)} copy(bf16[2,2048,2,512]{3,2,1,0:T(2,128)(2,1)} %param.21) | data formatting | bytes 16777216 | tf_op args[6]
  20.5 0.0 copy-done.5
  20.5 0.1 copy.42
  20.7 0.6 broadcast_in_dim.59.b_proj
  21.2 0.6 pad.16.table_ref
  21.9 60.3 %cnn_forward.1 = (f32[2,160,512]{2,1,0:T(8,128)}, bf16[10,896,128]{2,1,0:T(8,128)(2,1)}, f32[160,1,512]{2,1,0:T(1,128)}, f32[160,512]{1,0:T(8,128)}, f32[2,160,5...) custom-call(s32[10,1,896]{2,1,0:T(1,128)} %reshape.260.ids_ref, ...), custom_call_target="tpu_custom_call" | custom-call | tf_op jit(solution)/shard_map/cnn_forward/pallas_call | solution.py:400
  82.2 0.0 all-gather.5.cloned.1.call-update
  82.2 0.0 all-gather.9.cloned.1.call-start
  82.3 1.0 copy.53
  83.3 0.8 broadcast_in_dim.60.live_ref
  84.1 233.4 %recurrence.1 = (bf16[2,4,20,16,512]{4,3,2,1,0:T(8,128)(2,1)}, bf16[2,4,21,16,512]{4,3,2,1,0:T(8,128)(2,1)}, bf16[2,4,20,16,1024]{4,3,2,1,0:T(8,128)(2,1)}, bf16...) custom-call(f32[2,160,512]{2,1,0:T(8,128)} %get-tuple-element.61.bas, ...), custom_call_target="tpu_custom_call", output_to_operand_aliasing={{6}: (7, {})} | custom-call | tf_op jit(solution)/shard_map/recurrence/pallas_call | solution.py:1599
  317.5 72.0 %cnn_backward.1 = (bf16[2,4,20,16,4096]{4,3,2,1,0:T(8,128)(2,1)}, bf16[2,4,20,16,512]{4,3,2,1,0:T(8,128)(2,1)}, bf16[2,4,20,16,512]{4,3,2,1,0:T(8,128)(2,1)}, bf...) custom-call(bf16[2,160,128]{2,1,0:T(8,128)(2,1)} %get-tuple-element., ...), custom_call_target="tpu_custom_call", output_to_operand_aliasing={{0}: (12, {}), {1}: (13, {}), {2}: (14, {}), {3}: (15, {})} | custom-call | tf_op jit(solution)/shard_map/cnn_backward/pallas_call | solution.py:898
  389.6 0.0 all-gather.9.cloned.1.call-update
  389.6 0.2 all-gather.7.cloned.1.call-start
  389.8 0.9 collective-permute-start
  390.7 1.3 collective-permute-start.1
  392.0 0.6 collective-permute-start.2
  392.7 1.3 collective-permute-start.3
  394.0 19.5 %weight_grads.4 = (f32[2,2048,2,512]{3,2,1,0:T(2,128)}, f32[2,2,512]{2,1,0:T(2,128)}) custom-call(bf16[2,8,4,160,512]{4,3,2,1,0:T(8,128)(2,1)} %bitcast.59, bf16[2,1280,1024]{2,1,0:T(8,128)(2,1)} %bitcast.74, bf16[2,1280,1024]{2,1,0:T(8,128)(2,1)} %bitcast.75), custom_call_target="tpu_custom_call" | custom-call | flops 10737418240 | bytes 32505856 | tf_op jit(solution)/shard_map/weight_grads/pallas_call | solution.py:1724
  413.4 0.0 all-gather.5.cloned.1.call-done
  413.5 3.5 convolution_convert_fusion
  416.9 0.0 all-gather.7.cloned.1.call-update
  417.0 0.8 convert_reduce_fusion
  417.8 8.5 %weight_grads.5 = (f32[2,1024,512]{2,1,0:T(8,128)}, f32[2,1,512]{2,1,0:T(1,128)}) custom-call(bf16[2,4,1,320,1024]{4,3,2,1,0:T(8,128)(2,1)} %bitcast.62, bf16[2,1280,512]{2,1,0:T(8,128)(2,1)} %bitcast.63), custom_call_target="tpu_custom_call" | custom-call | flops 2684354560 | bytes 12058624 | tf_op jit(solution)/shard_map/weight_grads/pallas_call | solution.py:1724
  426.3 1.6 convert_reduce_fusion.1
  427.9 0.6 slice_bitcast_fusion.1
  428.5 0.6 slice.25
  429.1 0.7 broadcast_select_fusion
  429.8 0.0 collective-permute-done.first_ref
  429.8 0.0 collective-permute-done.1.second_ref
  429.8 2.9 merge_late.2.gates_in
  432.8 20.1 %weight_grads.6 = (f32[2,512,4,1024]{3,2,1,0:T(4,128)}, f32[2,512,4,1024]{3,2,1,0:T(4,128)}, f32[2,4,1024]{2,1,0:T(4,128)}) custom-call(bf16[2,4,1,320,512]{4,3,2,1,0:T(8,128)(2,1)} %bitcast.55, bf16[2,4,1,336,512]{4,3,2,1,0:T(8,128)(2,1)} %bitcast.53, bf16[2,1280,4096]{2,1,0:T(8,128)(2,1)} %bitcast.43, bf16[2,1280,4096]{2,1,0:T(8,128)(2,1)} %bitcast.44, ...), custom_call_target="tpu_custom_call" | custom-call | flops 10737418240 | bytes 42991616 | tf_op jit(solution)/shard_map/weight_grads/pallas_call | solution.py:1724
  452.8 1.1 collective-permute-done.2.first_ref
  454.0 0.6 collective-permute-done.3.second_ref
  454.6 0.4 copy-done.2
  455.0 2.8 merge_late.3
  457.8 0.0 copy-start.1
  457.9 20.4 %weight_grads.7 = (f32[2,512,4,1024]{3,2,1,0:T(4,128)}, f32[2,512,4,1024]{3,2,1,0:T(4,128)}, f32[2,4,1024]{2,1,0:T(4,128)}) custom-call(bf16[2,4,1,320,512]{4,3,2,1,0:T(8,128)(2,1)} %bitcast.56, bf16[2,4,1,336,512]{4,3,2,1,0:T(8,128)(2,1)} %bitcast.54, bf16[2,1280,4096]{2,1,0:T(8,128)(2,1)} %bitcast.47, ...), custom_call_target="tpu_custom_call", output_to_operand_aliasing={{0}: (6, {}), {1}: (7, {}), {2}: (8, {})} | custom-call | flops 10737418240 | bytes 42991616 | tf_op jit(solution)/shard_map/weight_grads/pallas_call | solution.py:1724
  478.3 0.0 all-gather.7.cloned.1.call-done
  478.3 4.2 convert_element_type.181
  (22 shorter events, 0.1 us)
Async XLA Ops:
  7.2 0.9 copy-start
  7.2 406.3 %all-gather.5.cloned.1.call-start = ((), (), s32[]{:S(2)}) async-start(), calls=%async_computation | async-start | bytes 1474560 | tf_op jit(solution)/shard_map/all_gather | solution.py:1888
  12.3 8.2 %copy-start.5 = (bf16[262,16]{0,1:T(8,128)(2,1)S(1)}, bf16[262,16]{0,1:T(8,128)(2,1)}, u32[]{:S(2)}) copy-start(bf16[262,16]{0,1:T(8,128)(2,1)} %param.18) | copy-start | bytes 25156
  12.3 8.4 %copy-start.6 = (bf16[512]{0:T(512)(128)(2,1)S(1)}, bf16[512]{0:T(512)(128)(2,1)}, u32[]{:S(2)}) copy-start(bf16[512]{0:T(512)(128)(2,1)} %param.24) | copy-start | bytes 3076
  21.9 60.4 %copy-start.4 = (bf16[16,20,2,512]{3,2,1,0:T(2,128)(2,1)S(1)}, bf16[16,20,2,512]{3,2,1,0:T(2,128)(2,1)}, u32[]{:S(2)}) copy-start(bf16[16,20,2,512]{3,2,1,0:T(2,128)(2,1)} %param.17) | copy-start | bytes 1966084
  21.9 61.4 %copy-start.7 = (s32[16]{0:T(128)S(1)}, s32[16]{0:T(128)}, u32[]{:S(2)}) copy-start(s32[16]{0:T(128)} %param.16) | copy-start | bytes 196
  82.2 344.1 %all-gather.9.cloned.1.call-start = ((), (), s32[]{:S(2)}) async-start(), calls=%async_computation.2 | async-start | bytes 1327104 | tf_op jit(solution)/shard_map/all_gather | solution.py:1930
  389.6 88.7 %all-gather.7.cloned.1.call-start = ((), (), s32[]{:S(2)}) async-start(), calls=%async_computation.1 | async-start | bytes 2621440 | tf_op jit(solution)/shard_map/all_gather | solution.py:1946
  389.8 40.0 %collective-permute-start = (bf16[10,16,4096]{2,1,0:T(8,128)(2,1)}, bf16[10,16,4096]{2,1,0:T(8,128)(2,1)}, u32[]{:S(2)}, u32[]{:S(2)}) collective-permute-start(bf16[10,16,4096]{2,1,0:T(8,128)(2,1)} %get-tuple-element.77), channel_id=1, source_target_pairs={{0,2},{1,3},{2,0},{3,1},{4,6},{5,7},{6,4},{7,5},{8,10},{9,11},{10,... | collective-permute-start | bytes 3932168 | tf_op jit(solution)/shard_map/ppermute | solution.py:1801
  390.7 39.1 %collective-permute-start.1 = (bf16[10,16,4096]{2,1,0:T(8,128)(2,1)}, bf16[10,16,4096]{2,1,0:T(8,128)(2,1)}, u32[]{:S(2)}, u32[]{:S(2)}) collective-permute-start(bf16[10,16,4096]{2,1,0:T(8,128)(2,1)} %get-tuple-element.78), channel_id=1, source_target_pairs={{0,1},{1,0},{2,3},{3,2},{4,5},{5,4},{6,7},{7,6},{8,9},{9,8},{10,11... | collective-permute-start | bytes 3932168 | tf_op jit(solution)/shard_map/ppermute | solution.py:1801
  392.0 62.0 %collective-permute-start.2 = (bf16[10,16,4096]{2,1,0:T(8,128)(2,1)}, bf16[10,16,4096]{2,1,0:T(8,128)(2,1)S(1)}, u32[]{:S(2)}, u32[]{:S(2)}) collective-permute-start(bf16[10,16,4096]{2,1,0:T(8,128)(2,1)} %get-tuple-element.99), channel_id=1, source_target_pairs={{0,2},{1,3},{2,0},{3,1},{4,6},{5,7},{6,4},{7,5},{8,10},{9,11},{10,... | collective-permute-start | bytes 3932168 | tf_op jit(solution)/shard_map/ppermute | solution.py:1801
  392.7 61.9 %collective-permute-start.3 = (bf16[10,16,4096]{2,1,0:T(8,128)(2,1)}, bf16[10,16,4096]{2,1,0:T(8,128)(2,1)}, u32[]{:S(2)}, u32[]{:S(2)}) collective-permute-start(bf16[10,16,4096]{2,1,0:T(8,128)(2,1)} %get-tuple-element.100), channel_id=1, source_target_pairs={{0,1},{1,0},{2,3},{3,2},{4,5},{5,4},{6,7},{7,6},{8,9},{9,8},{10,11... | collective-permute-start | bytes 3932168 | tf_op jit(solution)/shard_map/ppermute | solution.py:1801
  413.4 3.5 copy-start.3
  454.0 1.1 copy-start.2
  457.8 24.6 %copy-start.1 = (s32[16,20,50]{2,0,1:T(8,128)S(1)}, s32[16,20,50]{2,0,1:T(8,128)}, u32[]{:S(2)}) copy-start(s32[16,20,50]{2,0,1:T(8,128)} %param.15) | copy-start | bytes 192004
Sparse Core Ops, SparseCore 0:
  82.3 31.9 all-gather.4
  389.7 26.8 all-gather.8
  418.2 45.9 all-gather.6
